TPU v7x, 512 devices: a whole 4x4x16 slice. The times are simulated.
512 devices in a mesh: section: 4 (over x_hi, core), expert: 16 (over z), tensor: 8 (over y, x_lo).
Axes of the slice: x: 4 (x_hi: 2, x_lo: 2; x = x_hi * 2 + x_lo), y: 4, z: 16, core: 2. Of those that a mesh axis runs over, the one named last changes fastest.
Arguments:
- tokens: bfloat16 [8192, 5120], P(('section', 'expert'), 'tensor'), may hold values from -6 to 6
- norm_gain: float32 [5120], P('tensor'), may hold values from 0.1 to 1.9
- router: bfloat16 [5120, 16], P('tensor'), may hold values from -0.078125 to 0.078125
- expert_ids: int32 [8192, 1], P(('section', 'expert')), may hold values from 0 to 15; in each aligned block of 128 rows (0 to 127, 128 to 255, ...) at most 16 rows name the same one
- gate_proj: bfloat16 [16, 5120, 4096], P('expert', None, ('section', 'tensor')), may hold values from -0.078125 to 0.078125
- up_proj: bfloat16 [16, 5120, 4096], P('expert', None, ('section', 'tensor')), may hold values from -0.078125 to 0.078125
- down_proj: bfloat16 [16, 4096, 5120], P('expert', 'section', 'tensor'), may hold values from -0.09375 to 0.09375
Outputs:
- moe_out: bfloat16 [8192, 5120], P(('section', 'expert'), 'tensor')
Inputs may be any that keep to these rules, and one draw needn't show every extreme that they name: `expert_ids`: within each aligned block of 128 tokens (the tokens of one group of devices along section and expert) no expert is named by more than 16 tokens, a bound that some block reaches.
All inputs are finite; a program needn't handle non-finite values.
Results may differ from a plain program's by a relative error of at most 0.017.
Values may be sent and summed in bfloat16 or wider, within the bound.
No kernel may reach another device: no remote copies, remote signals or barrier semaphores. Data moves between devices by JAX's collectives and lax.ppermute only.
A program may use at most 64 MiB of HBM per device.

v0:
```python
import jax
import jax.numpy as jnp
from jax import lax
from jax.sharding import PartitionSpec as P

D = 5120


EPSILON = 1e-05


def from_everyone(array, axis):
    count = lax.axis_size(axis)
    return lax.all_to_all(
        jnp.broadcast_to(array[None], (count, *array.shape)), axis, 0, 0, tiled=True
    )


def of_everyone(array, axis):
    return from_everyone(array, axis).sum(axis=0)


def joined_along(parts, dim):
    parts = jnp.moveaxis(parts, 0, dim)
    shape = parts.shape
    return parts.reshape(*shape[:dim], shape[dim] * shape[dim + 1], *shape[dim + 2 :])


def collect(array, axis, dim):
    return joined_along(from_everyone(array, axis), dim)


def in_blocks(array, dim, count):
    shape = array.shape
    parts = array.reshape(*shape[:dim], count, shape[dim] // count, *shape[dim + 1 :])
    return jnp.moveaxis(parts, dim, 0)


def summed_on_arrival(array, axis, dim):
    parts = in_blocks(array, dim, lax.axis_size(axis))
    arrived = lax.all_to_all(parts, axis, split_axis=0, concat_axis=0, tiled=True)
    return arrived.sum(axis=0)


def slot_table(expert_ids, experts, capacity):
    chosen = expert_ids[:, 0]
    member = (chosen[:, None] == jnp.arange(experts, dtype=jnp.int32)[None, :]).astype(jnp.int32)
    earlier = jnp.cumsum(member, axis=0) - member
    placed = chosen * capacity + jnp.sum(earlier * member, axis=1)
    placing = placed[:, None] == jnp.arange(experts * capacity, dtype=jnp.int32)[None, :]
    return (member, placing)


def normalize(tokens, norm_gain, squares):
    values = tokens.astype(jnp.float32)
    return (values * lax.rsqrt(squares / D + EPSILON) * norm_gain).astype(jnp.bfloat16)


def on_device(tokens, norm_gain, router, expert_ids, gate_proj, up_proj, down_proj):
    row_count = tokens.shape[0]
    experts = router.shape[1]
    capacity = 2 * row_count // experts
    values = tokens.astype(jnp.float32)
    squares = of_everyone(jnp.sum(values * values, axis=1, keepdims=True), "tensor")
    normed = normalize(tokens, norm_gain, squares)
    logits = of_everyone(jnp.dot(normed, router, preferred_element_type=jnp.float32), "tensor")
    member, placing = slot_table(expert_ids, experts, capacity)
    score = jax.nn.sigmoid(jnp.sum(jnp.where(member > 0, logits, jnp.float32(0.0)), axis=1))
    routed = (normed.astype(jnp.float32) * score[:, None]).astype(jnp.bfloat16)
    placing = placing.astype(jnp.bfloat16)
    outgoing = jnp.einsum("tc,td->cd", placing, routed, preferred_element_type=jnp.float32).astype(
        jnp.bfloat16
    )
    arrived = lax.all_to_all(outgoing, "expert", split_axis=0, concat_axis=0, tiled=True)
    gate_cols = gate_proj[0]
    up_cols = up_proj[0]
    down_rows = down_proj[0]
    widened = collect(arrived, "tensor", 1)
    piece = lax.all_gather(widened, "section", axis=0, tiled=True)
    gate = jnp.dot(piece, gate_cols, preferred_element_type=jnp.float32)
    upper = jnp.dot(piece, up_cols, preferred_element_type=jnp.float32)
    hidden = (jax.nn.silu(gate) * upper).astype(jnp.bfloat16)
    full_hidden = collect(hidden, "tensor", 1)
    summed = summed_on_arrival(
        jnp.dot(full_hidden, down_rows, preferred_element_type=jnp.float32), "section", 0
    )
    returned = lax.all_to_all(
        summed.astype(jnp.bfloat16), "expert", split_axis=0, concat_axis=0, tiled=True
    )
    result = jnp.einsum("tc,cd->td", placing, returned, preferred_element_type=jnp.float32)
    return result.astype(jnp.bfloat16)


def solution(mesh):
    in_specs = (
        P(("section", "expert"), "tensor"),
        P("tensor"),
        P("tensor", None),
        P(("section", "expert"), None),
        P("expert", None, ("section", "tensor")),
        P("expert", None, ("section", "tensor")),
        P("expert", "section", "tensor"),
    )
    out_specs = P(("section", "expert"), "tensor")
    return jax.shard_map(
        on_device, mesh=mesh, in_specs=in_specs, out_specs=out_specs, check_vma=False
    )
```

profile of v0, /device:TPU:64, one launch (start us, length us, event | category | flops | bytes accessed | tf_op | source)
XLA Modules:
  0.0 304.4 jit_solution(2847538108800103751)
XLA Ops:
  6.5 0.0 copy-start
  6.5 1.1 fusion.12
  7.7 0.6 broadcast_in_dim.14
  8.3 5.4 %all-to-all-start = ((f32[8,128,1]{1,2,0:T(1,128)}), f32[8,128,1]{1,2,0:T(1,128)S(1)}, u32[]{:S(2)}, u32[]{:S(2)}) async-start(f32[8,128,1]{1,2,0:T(1,128)} %broadcast_in_dim.14), calls=%async_computation | async-start | bytes 8192 | tf_op jit(solution)/shard_map/all_to_all | solution.py:14
  13.7 0.7 fusion.18
  14.4 0.2 reduce_window_sum.11
  14.6 0.8 select_reduce_fusion.1
  15.4 4.3 %all-to-all-done = f32[8,128,1]{1,2,0:T(1,128)S(1)} async-done(((f32[8,128,1]{1,2,0:T(1,128)}), f32[8,128,1]{1,2,0:T(1,128)S(1)}, u32[]{:S(2)}, u32[]{:S(2)}) %all-to-all-start) | async-done | bytes 4128 | tf_op jit(solution)/shard_map/all_to_all | solution.py:14
  19.8 1.1 fusion.19
  20.9 0.7 broadcast_in_dim.15
  21.6 3.4 %all-to-all-start.1 = ((f32[8,128,16]{1,2,0:T(8,128)}), f32[8,128,16]{1,2,0:T(8,128)S(1)}, u32[]{:S(2)}, u32[]{:S(2)}) async-start(f32[8,128,16]{1,2,0:T(8,128)} %broadcast_in_dim.15), calls=%async_computation.1 | async-start | bytes 131072 | tf_op jit(solution)/shard_map/all_to_all | solution.py:14
  25.0 0.0 all-gather.2.cloned.1.call-start
  25.0 0.7 fusion.22
  25.7 5.6 %all-to-all-done.1 = f32[8,128,16]{1,2,0:T(8,128)S(1)} async-done(((f32[8,128,16]{1,2,0:T(8,128)}), f32[8,128,16]{1,2,0:T(8,128)S(1)}, u32[]{:S(2)}, u32[]{:S(2)}) %all-to-all-start.1) | async-done | bytes 65568 | tf_op jit(solution)/shard_map/all_to_all | solution.py:14
  31.3 0.1 copy.11
  31.4 0.8 select_reduce_fusion
  32.2 1.3 convolution_convert_fusion
  33.5 32.8 %all_to_all.43 = bf16[16,16,640]{2,1,0:T(8,128)(2,1)S(1)} all-to-all(bf16[16,16,640]{2,1,0:T(8,128)(2,1)S(1)} %bitcast.37), channel_id=1, replica_groups=mesh['section'=4,'expert'=16,'tensor'=8] {'expert'}, dimensions={0} | all-to-all | bytes 655360 | tf_op jit(solution)/shard_map/all_to_all | solution.py:74
  66.3 0.2 copy.12
  66.5 0.2 broadcast_in_dim.18
  66.7 27.6 %all_to_all.44 = bf16[8,256,640]{1,2,0:T(8,128)(2,1)} all-to-all(bf16[8,256,640]{1,2,0:T(8,128)(2,1)S(1)} %broadcast_in_dim.18), channel_id=1, replica_groups=mesh['section'=4,'expert'=16,'tensor'=8] {'tensor'}, dimensions={0} | all-to-all | bytes 5242880 | tf_op jit(solution)/shard_map/all_to_all | solution.py:14
  94.2 0.0 copy-start.2
  94.2 0.0 all-gather.2.cloned.1.call-update
  94.3 82.6 %all-gather.2.cloned.1.call-done = bf16[1024,5120]{0,1:T(8,128)(2,1)} async-done(((bf16[256,5120]{0,1:T(8,128)(2,1)}), bf16[1024,5120]{0,1:T(8,128)(2,1)}) %all-gather.2.cloned.1.call-update) | async-done | bytes 10485776 | tf_op jit(solution)/shard_map/all_gather | solution.py:79
  176.8 0.0 copy-done.2
  176.8 0.0 copy-start.1
  176.8 0.0 copy-start.3
  176.8 5.8 %fusion.4 = f32[1024,128]{1,0:T(8,128)S(1)} fusion(bf16[1024,5120]{0,1:T(8,128)(2,1)} %all-gather.2.cloned.1.call-done, bf16[1,5120,128]{2,1,0:T(8,128)(2,1)S(1)} %copy-done.2), kind=kOutput, calls=%fused_computation.4 | convolution fusion | flops 1342177280 | bytes 12320768 | tf_op jit(solution)/shard_map/dot_general | solution.py:80
  182.7 1.2 copy-done.1
  183.9 0.3 copy-done.3
  184.2 2.9 fusion.9
  187.1 0.3 broadcast_in_dim.19
  187.4 31.4 %all_to_all.45 = bf16[8,1024,128]{2,1,0:T(8,128)(2,1)S(1)} all-to-all(bf16[8,1024,128]{2,1,0:T(8,128)(2,1)S(1)} %broadcast_in_dim.19), channel_id=1, replica_groups=mesh['section'=4,'expert'=16,'tensor'=8] {'tensor'}, dimensions={0} | all-to-all | bytes 4194304 | tf_op jit(solution)/shard_map/all_to_all | solution.py:14
  218.8 1.4 copy.13
  220.2 2.3 dot_general.24
  222.5 0.0 copy-done
  222.5 3.4 %fusion = f32[4,256,640]{2,1,0:T(8,128)S(1)} fusion(bf16[4,256,1024]{2,1,0:T(8,128)(2,1)} %dot_general.24, bf16[1,1024,640]{2,1,0:T(8,128)(2,1)S(1)} %copy-done), kind=kOutput, calls=%fused_computation | convolution fusion | flops 1342177280 | bytes 6029312 | tf_op jit(solution)/shard_map/dot_general | solution.py:85
  225.9 36.1 %all_to_all.46 = f32[4,256,640]{2,1,0:T(8,128)} all-to-all(f32[4,256,640]{2,1,0:T(8,128)S(1)} %fusion), channel_id=1, replica_groups=mesh['section'=4,'expert'=16,'tensor'=8] {'section'}, dimensions={0} | all-to-all | bytes 5242880 | tf_op jit(solution)/shard_map/all_to_all | solution.py:41
  262.0 1.9 reduce_sum.62
  263.9 32.7 %all_to_all.47 = bf16[16,16,640]{2,1,0:T(8,128)(2,1)S(1)} all-to-all(bf16[16,16,640]{2,1,0:T(8,128)(2,1)S(1)} %bitcast.36), channel_id=1, replica_groups=mesh['section'=4,'expert'=16,'tensor'=8] {'expert'}, dimensions={0} | all-to-all | bytes 655360 | tf_op jit(solution)/shard_map/all_to_all | solution.py:87
  296.6 0.9 convolution_convert_fusion.1
  (4 shorter events, 0.1 us)
Async XLA Ops:
  6.5 216.0 %copy-start = (bf16[1,1024,640]{2,1,0:T(8,128)(2,1)S(1)}, bf16[1,1024,640]{2,1,0:T(8,128)(2,1)}, u32[]{:S(2)}) copy-start(bf16[1,1024,640]{2,1,0:T(8,128)(2,1)} %param.13) | copy-start | bytes 3932164
  8.3 11.5 %all-to-all-start = ((f32[8,128,1]{1,2,0:T(1,128)}), f32[8,128,1]{1,2,0:T(1,128)S(1)}, u32[]{:S(2)}, u32[]{:S(2)}) async-start(f32[8,128,1]{1,2,0:T(1,128)} %broadcast_in_dim.14), calls=%async_computation | async-start | bytes 8192 | tf_op jit(solution)/shard_map/all_to_all | solution.py:14
  21.6 9.6 %all-to-all-start.1 = ((f32[8,128,16]{1,2,0:T(8,128)}), f32[8,128,16]{1,2,0:T(8,128)S(1)}, u32[]{:S(2)}, u32[]{:S(2)}) async-start(f32[8,128,16]{1,2,0:T(8,128)} %broadcast_in_dim.15), calls=%async_computation.1 | async-start | bytes 131072 | tf_op jit(solution)/shard_map/all_to_all | solution.py:14
  25.0 151.8 %all-gather.2.cloned.1.call-start = ((), (), s32[]{:S(2)}) async-start(), calls=%async_computation.7 | async-start | bytes 13107200 | tf_op jit(solution)/shard_map/all_gather | solution.py:79
  94.2 82.6 %copy-start.2 = (bf16[1,5120,128]{2,1,0:T(8,128)(2,1)S(1)}, bf16[1,5120,128]{2,1,0:T(8,128)(2,1)}, u32[]{:S(2)}) copy-start(bf16[1,5120,128]{2,1,0:T(8,128)(2,1)} %param.11) | copy-start | bytes 3932164
  176.8 7.0 %copy-start.1 = (bf16[1024,5120]{0,1:T(8,128)(2,1)S(1)}, bf16[1024,5120]{0,1:T(8,128)(2,1)}, u32[]{:S(2)}) copy-start(bf16[1024,5120]{0,1:T(8,128)(2,1)} %all-gather.2.cloned.1.call-done) | copy-start | bytes 31457284
  176.8 7.3 %copy-start.3 = (bf16[1,5120,128]{2,1,0:T(8,128)(2,1)S(1)}, bf16[1,5120,128]{2,1,0:T(8,128)(2,1)}, u32[]{:S(2)}) copy-start(bf16[1,5120,128]{2,1,0:T(8,128)(2,1)} %param.12) | copy-start | bytes 3932164
Sparse Core Ops, SparseCore 0:
  94.4 82.4 all-gather.1
where the time goes:
time: 305 us; the launch traced here: 304 us
  blocking collectives  161 us (53%)
  waiting for transfers between devices  92.5 us (30%)
  matrix products  15.5 us (5%)
  between operations  13.5 us (4%)
  starting transfers between devices  8.79 us (3%)
  local copies, waits for them, and re-layouts  7.22 us (2%)
  other arithmetic  6.3 us (2%)
    all_gather x1, waiting for transfers between devices, on_device(): piece = lax.all_gather(widened, 'section', axis=0, tiled=True)  82.6 us
    all_to_all x2, blocking collectives, from_everyone(): lax.all_to_all(jnp.broadcast_to(array[None], (count, *array.shape)), axis...  59 us
    all_to_all x1, blocking collectives, summed_on_arrival(): lax.all_to_all(parts, axis, split_axis=0, concat_axis=0, tiled=True)  36.1 us
    all_to_all x1, blocking collectives, on_device(): lax.all_to_all(outgoing, 'expert', split_axis=0, concat_axis=0, tiled=True)  32.8 us
    all_to_all x1, blocking collectives, on_device(): lax.all_to_all(summed.astype(jnp.bfloat16), 'expert', split_axis=0, conca...  32.7 us
    all_to_all x2, waiting for transfers between devices, from_everyone(): lax.all_to_all(jnp.broadcast_to(array[None], (count, *array.shape)), axis...  9.89 us
    all_to_all x2, starting transfers between devices, from_everyone(): lax.all_to_all(jnp.broadcast_to(array[None], (count, *array.shape)), axis...  8.75 us
  transfers between devices with their start and end apart: 3, of which 3 were waited for; matrix products, arithmetic and copies ran while one was open for 1% of the time, Pallas kernels for 0%

commit v1 on v0

v1 whole, which is shorter than its diff:
```python
import functools

import jax
import jax.numpy as jnp
import numpy as np
from jax import lax
from jax.experimental import pallas as pl
from jax.experimental.pallas import tpu as pltpu
from jax.sharding import Mesh, PartitionSpec as P

D = 5120
EPSILON = 1e-05
EXPERTS = 16
CAP = 16
SLOTS = EXPERTS * CAP
TOK = 128
FEAT = 640
TENSOR = 8
EXTRA = 8
VMEM = 48 * 1024 * 1024
TENSOR_AXES = ("y", "xl")


def column_of(row):
    count = row.shape[1]
    i = lax.broadcasted_iota(jnp.int32, (count, count), 0)
    j = lax.broadcasted_iota(jnp.int32, (count, count), 1)
    return jnp.sum(jnp.where(i == j, row, 0), axis=1, keepdims=True), i, j


def dispatch_kernel(ids_ref, tokens_ref, out_ref):
    row = ids_ref[...]
    col, i, j = column_of(row)
    earlier = jnp.sum(jnp.where((col == row) & (i < j), 1, 0), axis=0, keepdims=True)
    placed = row * CAP + earlier
    slot = lax.broadcasted_iota(jnp.int32, (SLOTS, TOK), 0)
    placing = (slot == placed).astype(jnp.float32).astype(jnp.bfloat16)
    out_ref[...] = jnp.dot(
        placing, tokens_ref[...], preferred_element_type=jnp.float32
    ).astype(jnp.bfloat16)


def combine_kernel(ids_ref, back_ref, out_ref):
    row = ids_ref[...]
    col, i, j = column_of(row)
    earlier = jnp.sum(jnp.where((col == row) & (j < i), 1, 0), axis=1, keepdims=True)
    placed = col * CAP + earlier
    slot = lax.broadcasted_iota(jnp.int32, (TOK, SLOTS), 1)
    placing = (slot == placed).astype(jnp.float32).astype(jnp.bfloat16)
    out_ref[...] = jnp.dot(
        placing, back_ref[...], preferred_element_type=jnp.float32
    ).astype(jnp.bfloat16)


def gained(x_ref):
    rows = x_ref[0, :SLOTS, :].astype(jnp.float32)
    more = x_ref[0, SLOTS:, :].astype(jnp.float32)
    gain = more[0:1] + more[1:2] + more[2:3]
    return rows, rows * gain, more[3:4]


def activated(acc, scale, out_ref):
    for k in range(2):
        gate = acc[:, 256 * k : 256 * k + 128] * scale
        upper = acc[:, 256 * k + 128 : 256 * k + 256] * scale
        out_ref[:, 128 * k : 128 * k + 128] = (jax.nn.silu(gate) * upper).astype(jnp.bfloat16)


def joined(refs, axis):
    return jnp.concatenate([r[...] for r in refs], axis=axis)


def first_kernel(x_ref, g0, u0, g1, u1, out_ref, scale_ref, acc, squares, logit):
    step = pl.program_id(0)

    @pl.when(step == 0)
    def _():
        acc[...] = jnp.zeros_like(acc)
        squares[...] = jnp.zeros_like(squares)
        logit[...] = jnp.zeros_like(logit)

    rows, values, router = gained(x_ref)
    squares[...] += jnp.sum(rows * rows, axis=1, keepdims=True)
    logit[...] += jnp.sum(values * router, axis=1, keepdims=True)
    acc[...] += jnp.dot(
        values.astype(jnp.bfloat16), joined((g0, u0, g1, u1), 1), preferred_element_type=jnp.float32
    )

    @pl.when(step == TENSOR - 1)
    def _():
        rstd = lax.rsqrt(squares[...] / D + EPSILON)
        scale = rstd * jax.nn.sigmoid(logit[...] * rstd)
        scale_ref[...] = scale
        activated(acc[...], scale, out_ref)


def second_kernel(x_ref, scale_ref, g0, u0, g1, u1, out_ref, acc):
    step = pl.program_id(0)

    @pl.when(step == 0)
    def _():
        acc[...] = jnp.zeros_like(acc)

    _, values, _ = gained(x_ref)
    acc[...] += jnp.dot(
        values.astype(jnp.bfloat16), joined((g0, u0, g1, u1), 1), preferred_element_type=jnp.float32
    )

    @pl.when(step == TENSOR - 1)
    def _():
        activated(acc[...], scale_ref[...], out_ref)


X_SPEC = pl.BlockSpec((1, SLOTS + EXTRA, FEAT), lambda t: (t, 0, 0))
W_SPEC = pl.BlockSpec((FEAT, 128), lambda t: (t, 0))
H_SPEC = pl.BlockSpec((SLOTS, 256), lambda t: (0, 0))
S_SPEC = pl.BlockSpec((SLOTS, 1), lambda t: (0, 0))
HIDDEN = jax.ShapeDtypeStruct((SLOTS, 256), jnp.bfloat16)
GATE_COST = pl.CostEstimate(
    flops=2 * SLOTS * D * 512, bytes_accessed=2 * (D * 512 + D * SLOTS), transcendentals=SLOTS * 256
)
DOWN_COST = pl.CostEstimate(
    flops=2 * SLOTS * 2048 * FEAT, bytes_accessed=2 * 2048 * (FEAT + SLOTS), transcendentals=0
)
PARAMS = pltpu.CompilerParams(vmem_limit_bytes=VMEM, dimension_semantics=("arbitrary",))


def first_half(x, g0, u0, g1, u1):
    return pl.pallas_call(
        first_kernel,
        grid=(TENSOR,),
        in_specs=[X_SPEC] + [W_SPEC] * 4,
        out_specs=[H_SPEC, S_SPEC],
        out_shape=[HIDDEN, jax.ShapeDtypeStruct((SLOTS, 1), jnp.float32)],
        scratch_shapes=[
            pltpu.VMEM((SLOTS, 512), jnp.float32),
            pltpu.VMEM((SLOTS, 1), jnp.float32),
            pltpu.VMEM((SLOTS, 1), jnp.float32),
        ],
        compiler_params=PARAMS,
        cost_estimate=GATE_COST,
    )(x, g0, u0, g1, u1)


def second_half(x, scale, g0, u0, g1, u1):
    return pl.pallas_call(
        second_kernel,
        grid=(TENSOR,),
        in_specs=[X_SPEC, S_SPEC] + [W_SPEC] * 4,
        out_specs=H_SPEC,
        out_shape=HIDDEN,
        scratch_shapes=[pltpu.VMEM((SLOTS, 512), jnp.float32)],
        compiler_params=PARAMS,
        cost_estimate=GATE_COST,
    )(x, scale, g0, u0, g1, u1)


def down_kernel(last, h_ref, d0, d1, *rest):
    step = pl.program_id(0)
    before, (out_ref, acc) = rest[:-2], rest[-2:]

    @pl.when(step == 0)
    def _():
        acc[...] = before[0][...] if before else jnp.zeros_like(acc)

    acc[...] += jnp.dot(h_ref[0], joined((d0, d1), 0), preferred_element_type=jnp.float32)

    @pl.when(step == TENSOR - 1)
    def _():
        out_ref[...] = acc[...].astype(out_ref.dtype)


def down_half(hidden, d0, d1, before, dtype, order):
    total = pl.BlockSpec((SLOTS, FEAT), lambda t: (0, 0))
    d_spec = pl.BlockSpec((128, FEAT), lambda t: (t, 0))
    h_spec = pl.BlockSpec((1, SLOTS, 256), lambda t: (order(t), 0, 0))
    return pl.pallas_call(
        functools.partial(down_kernel, before is not None),
        grid=(TENSOR,),
        in_specs=[h_spec, d_spec, d_spec] + ([total] if before is not None else []),
        out_specs=total,
        out_shape=jax.ShapeDtypeStruct((SLOTS, FEAT), dtype),
        scratch_shapes=[pltpu.VMEM((SLOTS, FEAT), jnp.float32)],
        compiler_params=PARAMS,
        cost_estimate=DOWN_COST,
    )(hidden, d0, d1, *(() if before is None else (before,)))


def gathered(array):
    copies = jnp.broadcast_to(array[None], (TENSOR, *array.shape))
    return lax.all_to_all(copies, TENSOR_AXES, 0, 0, tiled=True)


def over_experts(array):
    parts = array.reshape(EXPERTS, CAP, FEAT)
    return lax.all_to_all(parts, "z", 0, 0, tiled=True).reshape(SLOTS, FEAT)


def other_core(array):
    return lax.ppermute(array, "co", [(0, 1), (1, 0)])


def across_border(array):
    return lax.ppermute(array, ("xh", "xl"), [(i, 3 - i) for i in range(4)])


def across_halves(array):
    return lax.ppermute(array, "xh", [(0, 1), (1, 0)])


def side_rows(norm_gain, router):
    high = norm_gain.astype(jnp.bfloat16)
    rest = norm_gain - high.astype(jnp.float32)
    middle = rest.astype(jnp.bfloat16)
    low = (rest - middle.astype(jnp.float32)).astype(jnp.bfloat16)
    mine = lax.axis_index("z") == jnp.arange(EXPERTS, dtype=jnp.int32)
    column = jnp.sum(jnp.where(mine[None, :], router.astype(jnp.float32), 0.0), axis=1)
    zero = jnp.zeros_like(high)
    return jnp.stack([high, middle, low, column.astype(jnp.bfloat16)] + [zero] * (EXTRA - 4))


def on_device(tokens, norm_gain, router, expert_ids, gate_proj, up_proj, down_proj):
    ids = expert_ids.reshape(1, TOK)
    gate, upper, down = gate_proj[0], up_proj[0], down_proj[0]

    outgoing = pl.pallas_call(
        dispatch_kernel, out_shape=jax.ShapeDtypeStruct((SLOTS, FEAT), jnp.bfloat16)
    )(ids, tokens)
    arrived = over_experts(outgoing)

    gate_far, upper_far = across_border(gate), across_border(upper)
    gate_near, upper_near = other_core(gate), other_core(upper)
    gate_last, upper_last = other_core(gate_far), other_core(upper_far)
    down_far, down_near = across_halves(down), other_core(down)
    down_last = other_core(down_far)

    rows = gathered(jnp.concatenate([arrived, side_rows(norm_gain, router)], axis=0))
    hidden, scale = first_half(rows, gate, upper, gate_near, upper_near)
    full = gathered(hidden)
    hidden_far = second_half(rows, scale, gate_far, upper_far, gate_last, upper_last)
    full_far = gathered(hidden_far)
    part = down_half(full, down, down_near, None, jnp.float32, lambda t: t)
    summed = down_half(
        full_far, down_far, down_last, part, jnp.bfloat16, lambda t: t + 1 - 2 * (t % 2)
    )
    returned = over_experts(summed)
    return pl.pallas_call(
        combine_kernel, out_shape=jax.ShapeDtypeStruct((TOK, FEAT), jnp.bfloat16)
    )(ids, returned)


def solution(mesh):
    fine = Mesh(
        np.asarray(mesh.devices).reshape(2, 2, 16, 4, 2), ("xh", "co", "z", "y", "xl")
    )
    section, tensor = ("xh", "co"), ("y", "xl")
    in_specs = (
        P((*section, "z"), tensor),
        P(tensor),
        P(tensor, None),
        P((*section, "z"), None),
        P("z", None, (*section, *tensor)),
        P("z", None, (*section, *tensor)),
        P("z", section, tensor),
    )
    return jax.shard_map(
        on_device,
        mesh=fine,
        in_specs=in_specs,
        out_specs=P((*section, "z"), tensor),
        check_vma=False,
    )
```

time: 305 us -> 227 us (0.74)
  the two profiles are of different devices: /device:TPU:64 before, /device:TPU:14 now
where the time goes in v1:
time: 227 us; the launch traced here: 225 us
  waiting for transfers between devices  98.2 us (43%)
  starting transfers between devices  54 us (24%)
  blocking collectives  32.8 us (14%)
  Pallas kernels  28.2 us (12%)
  local copies, waits for them, and re-layouts  10.4 us (5%)
    ppermute x2, waiting for transfers between devices, across_border(): return lax.ppermute(array, ('xh', 'xl'), [(i, 3 - i) for i in range(4)])  68.1 us
    all_to_all x1, blocking collectives, over_experts(): return lax.all_to_all(parts, 'z', 0, 0, tiled=True).reshape(SLOTS, FEAT)  32.8 us
    all_to_all x1, waiting for transfers between devices, over_experts(): return lax.all_to_all(parts, 'z', 0, 0, tiled=True).reshape(SLOTS, FEAT)  19.1 us
    all_to_all x3, starting transfers between devices, gathered(): return lax.all_to_all(copies, TENSOR_AXES, 0, 0, tiled=True)  17.2 us
    all_to_all x1, starting transfers between devices, over_experts(): return lax.all_to_all(parts, 'z', 0, 0, tiled=True).reshape(SLOTS, FEAT)  15.2 us
    ppermute x6, starting transfers between devices, other_core(): return lax.ppermute(array, 'co', [(0, 1), (1, 0)])  12.5 us
    pallas_call x2, Pallas kernels, down_half(): pl.pallas_call(functools.partial(down_kernel, before is not None), grid=(...  11.1 us
    all_to_all x3, waiting for transfers between devices, gathered(): return lax.all_to_all(copies, TENSOR_AXES, 0, 0, tiled=True)  11 us
  transfers between devices with their start and end apart: 13, of which 5 were waited for; matrix products, arithmetic and copies ran while one was open for 2% of the time, Pallas kernels for 8%

profile of v1, /device:TPU:14, one launch (start us, length us, event | category | flops | bytes accessed | tf_op | source)
XLA Modules:
  0.0 225.4 jit_solution(12616928140945963562)
XLA Ops:
  0.0 2.0 shard_map.73
  2.0 15.2 %all-to-all-start = ((bf16[16,16,640]{2,1,0:T(8,128)(2,1)}), bf16[16,16,640]{2,1,0:T(8,128)(2,1)S(1)}, u32[]{:S(2)}, u32[]{:S(2)}) async-start(bf16[16,16,640]{2,1,0:T(8,128)(2,1)} %bitcast.16), calls=%async_computation | async-start | bytes 655360 | tf_op jit(solution)/shard_map/all_to_all | solution.py:196
  17.2 0.8 subtract_convert_fusion
  18.0 0.8 select_reduce_fusion
  18.9 19.1 %all-to-all-done = bf16[16,16,640]{2,1,0:T(8,128)(2,1)S(1)} async-done(((bf16[16,16,640]{2,1,0:T(8,128)(2,1)}), bf16[16,16,640]{2,1,0:T(8,128)(2,1)S(1)}, u32[]{:S(2)}, u32[]{:S(2)}) %all-to-all-start) | async-done | bytes 327712 | tf_op jit(solution)/shard_map/all_to_all | solution.py:196
  38.0 0.3 concatenate.7
  38.3 1.8 broadcast_in_dim.20
  40.1 0.0 copy-start
  40.1 5.9 %all-to-all-start.1 = ((bf16[8,264,640]{2,1,0:T(8,128)(2,1)}), bf16[8,264,640]{2,1,0:T(8,128)(2,1)}, u32[]{:S(2)}, u32[]{:S(2)}) async-start(bf16[8,264,640]{2,1,0:T(8,128)(2,1)} %broadcast_in_dim.20), calls=%async_computation.1 | async-start | bytes 5406720 | tf_op jit(solution)/shard_map/all_to_all | solution.py:191
  46.1 0.0 copy-done
  46.1 2.4 %collective-permute-start.2 = (bf16[5120,128]{1,0:T(8,128)(2,1)S(1)}, bf16[5120,128]{1,0:T(8,128)(2,1)S(1)}, u32[]{:S(2)}, u32[]{:S(2)}) collective-permute-start(bf16[5120,128]{1,0:T(8,128)(2,1)S(1)} %bitcast.9), channel_id=1, source_target_pairs={{0,257},{1,256},{256,1},{257,0},{2,259},{3,258},{258,3},{259,2},{4... | collective-permute-start | bytes 3932168 | tf_op jit(solution)/shard_map/ppermute | solution.py:204
  48.5 4.6 %collective-permute-start.3 = (bf16[5120,128]{1,0:T(8,128)(2,1)}, bf16[5120,128]{1,0:T(8,128)(2,1)}, u32[]{:S(2)}, u32[]{:S(2)}) collective-permute-start(bf16[5120,128]{1,0:T(8,128)(2,1)} %bitcast.12), channel_id=1, source_target_pairs={{0,257},{1,256},{256,1},{257,0},{2,259},{3,258},{258,3},{259,2},{4... | collective-permute-start | bytes 3932168 | tf_op jit(solution)/shard_map/ppermute | solution.py:204
  53.1 1.9 collective-permute-start
  55.1 2.4 %collective-permute-start.1 = (bf16[5120,128]{1,0:T(8,128)(2,1)}, bf16[5120,128]{1,0:T(8,128)(2,1)S(1)}, u32[]{:S(2)}, u32[]{:S(2)}) collective-permute-start(bf16[5120,128]{1,0:T(8,128)(2,1)} %bitcast.13), channel_id=1, source_target_pairs={{0,128},{128,0},{1,129},{129,1},{2,130},{130,2},{3,131},{131,3},{4... | collective-permute-start | bytes 3932168 | tf_op jit(solution)/shard_map/ppermute | solution.py:200
  57.5 2.1 collective-permute-start.6
  59.6 49.4 %collective-permute-done.2.g0 = bf16[5120,128]{1,0:T(8,128)(2,1)S(1)} collective-permute-done((bf16[5120,128]{1,0:T(8,128)(2,1)S(1)}, bf16[5120,128]{1,0:T(8,128)(2,1)S(1)}, u32[]{:S(2)}, u32[]{:S(2)}) %collective-permute-start.2) | collective-permute-done | bytes 1310752 | tf_op jit(solution)/shard_map/ppermute | solution.py:204
  109.0 1.9 collective-permute-start.4
  110.9 18.7 %collective-permute-done.3.u0 = bf16[5120,128]{1,0:T(8,128)(2,1)} collective-permute-done((bf16[5120,128]{1,0:T(8,128)(2,1)}, bf16[5120,128]{1,0:T(8,128)(2,1)}, u32[]{:S(2)}, u32[]{:S(2)}) %collective-permute-start.3) | collective-permute-done | bytes 1310752 | tf_op jit(solution)/shard_map/ppermute | solution.py:204
  129.6 1.9 collective-permute-start.5
  131.5 0.0 collective-permute-done.g1
  131.5 0.0 copy-start.2
  131.5 1.0 copy-done.2
  132.6 0.0 collective-permute-done.1.u1
  132.6 0.0 copy-start.4
  132.6 1.1 copy-done.4
  133.7 0.0 all-to-all-done.1.x_ref
  133.7 0.0 copy-start.1
  133.7 1.3 copy-done.1
  135.0 0.0 copy-start.3
  135.0 1.3 copy-done.3
  136.3 0.0 copy-start.5
  136.3 1.3 copy-done.5
  137.6 6.1 %shard_map.74 = (bf16[256,256]{1,0:T(8,128)(2,1)S(1)}, f32[256,1]{1,0:T(8,128)S(1)}) custom-call(bf16[8,264,640]{2,1,0:T(8,128)(2,1)} %all-to-all-done.1.x_ref, bf16[5120,128]{1,0:T(8,128)(2,1)S(1)} %bitcast.11, bf16[5120,128]{1,0:T(8,128)(2,1)S(1)} %bitcast.14, bf16[5120,128]{1,0:T(8,128)(2,1)S(1)} %copy-done.3, bf16[5120,128]{1,0:T(8,128)(2,1)S(1)} %copy-done.5), custom_call_target="tpu_custom_call" | custom-call | flops 1342177280 | bytes 7864320 | tf_op jit(solution)/shard_map/pallas_call | solution.py:129
  143.8 1.1 broadcast_in_dim.35
  144.8 5.7 %all-to-all-start.3 = ((bf16[8,256,256]{2,1,0:T(8,128)(2,1)}), bf16[8,256,256]{2,1,0:T(8,128)(2,1)S(1)}, u32[]{:S(2)}, u32[]{:S(2)}) async-start(bf16[8,256,256]{2,1,0:T(8,128)(2,1)} %broadcast_in_dim.35), calls=%async_computation.3 | async-start | bytes 2097152 | tf_op jit(solution)/shard_map/all_to_all | solution.py:191
  150.5 1.9 collective-permute-start.8
  152.5 0.0 collective-permute-done.6.d0
  152.5 2.4 %collective-permute-start.7 = (bf16[1024,640]{1,0:T(8,128)(2,1)}, bf16[1024,640]{1,0:T(8,128)(2,1)}, u32[]{:S(2)}, u32[]{:S(2)}) collective-permute-start(bf16[1024,640]{1,0:T(8,128)(2,1)} %collective-permute-done.6.d0), channel_id=1, source_target_pairs={{0,128},{128,0},{1,129},{129,1},{2,130},{130,2},{3,131},{131,3},{4... | collective-permute-start | bytes 3932168 | tf_op jit(solution)/shard_map/ppermute | solution.py:200
  154.9 0.0 collective-permute-done.4.g1
  154.9 0.0 collective-permute-done.5.u1
  154.9 6.9 %shard_map.75 = bf16[256,256]{1,0:T(8,128)(2,1)S(1)} custom-call(bf16[8,264,640]{2,1,0:T(8,128)(2,1)} %all-to-all-done.1.x_ref, f32[256,1]{1,0:T(8,128)S(1)} %get-tuple-element.7.scale_ref, bf16[5120,128]{1,0:T(8,128)(2,1)S(1)} %collective-permute-done.2.g0, bf16[5120,128]{1,0:T(8,128)(2,1)} %collective-permute-done.3.u0, ...), custom_call_target="tpu_custom_call" | custom-call | flops 1342177280 | bytes 7864320 | tf_op jit(solution)/shard_map/pallas_call | solution.py:146
  161.8 3.0 %all-to-all-done.3.h_ref = bf16[8,256,256]{2,1,0:T(8,128)(2,1)S(1)} async-done(((bf16[8,256,256]{2,1,0:T(8,128)(2,1)}), bf16[8,256,256]{2,1,0:T(8,128)(2,1)S(1)}, u32[]{:S(2)}, u32[]{:S(2)}) %all-to-all-start.3) | async-done | bytes 1048608 | tf_op jit(solution)/shard_map/all_to_all | solution.py:191
  164.9 1.1 broadcast_in_dim.34
  165.9 5.6 %all-to-all-start.2 = ((bf16[8,256,256]{2,1,0:T(8,128)(2,1)}), bf16[8,256,256]{2,1,0:T(8,128)(2,1)S(1)}, u32[]{:S(2)}, u32[]{:S(2)}) async-start(bf16[8,256,256]{2,1,0:T(8,128)(2,1)} %broadcast_in_dim.34), calls=%async_computation.2 | async-start | bytes 2097152 | tf_op jit(solution)/shard_map/all_to_all | solution.py:191
  171.5 0.0 collective-permute-done.8.d1
  171.5 5.6 %shard_map.76.rest_0_ = f32[256,640]{1,0:T(8,128)S(1)} custom-call(bf16[8,256,256]{2,1,0:T(8,128)(2,1)S(1)} %all-to-all-done.3.h_ref, bf16[1024,640]{1,0:T(8,128)(2,1)} %bitcast.5.d0, bf16[1024,640]{1,0:T(8,128)(2,1)} %collective-permute-done.8.d1), custom_call_target="tpu_custom_call" | custom-call | flops 671088640 | bytes 3670016 | tf_op jit(solution)/shard_map/pallas_call | solution.py:177
  177.1 0.0 collective-permute-done.7.d1
  177.1 7.9 %all-to-all-done.2.h_ref = bf16[8,256,256]{2,1,0:T(8,128)(2,1)S(1)} async-done(((bf16[8,256,256]{2,1,0:T(8,128)(2,1)}), bf16[8,256,256]{2,1,0:T(8,128)(2,1)S(1)}, u32[]{:S(2)}, u32[]{:S(2)}) %all-to-all-start.2) | async-done | bytes 1048608 | tf_op jit(solution)/shard_map/all_to_all | solution.py:191
  185.0 5.6 %shard_map.77 = bf16[256,640]{1,0:T(8,128)(2,1)S(1)} custom-call(bf16[8,256,256]{2,1,0:T(8,128)(2,1)S(1)} %all-to-all-done.2.h_ref, bf16[1024,640]{1,0:T(8,128)(2,1)} %collective-permute-done.6.d0, bf16[1024,640]{1,0:T(8,128)(2,1)} %collective-permute-done.7.d1, f32[256,640]{1,0:T(8,128)S(1)} %shard_map.76.rest_0_), custom_call_target="tpu_custom_call" | custom-call | flops 671088640 | bytes 3670016 | tf_op jit(solution)/shard_map/pallas_call | solution.py:177
  190.6 32.8 %all_to_all.25 = bf16[16,16,640]{2,1,0:T(8,128)(2,1)} all-to-all(bf16[16,16,640]{2,1,0:T(8,128)(2,1)S(1)} %bitcast.8), channel_id=1, replica_groups=mesh['xh'=2,'co'=2,'z'=16,'y'=4,'xl'=2] {'z'}, dimensions={0} | all-to-all | bytes 655360 | tf_op jit(solution)/shard_map/all_to_all | solution.py:196
  223.4 2.0 shard_map.78
  (6 shorter events, 0.0 us)
Async XLA Ops:
  2.0 36.0 %all-to-all-start = ((bf16[16,16,640]{2,1,0:T(8,128)(2,1)}), bf16[16,16,640]{2,1,0:T(8,128)(2,1)S(1)}, u32[]{:S(2)}, u32[]{:S(2)}) async-start(bf16[16,16,640]{2,1,0:T(8,128)(2,1)} %bitcast.16), calls=%async_computation | async-start | bytes 655360 | tf_op jit(solution)/shard_map/all_to_all | solution.py:196
  40.1 6.0 %copy-start = (bf16[1,5120,128]{2,1,0:T(8,128)(2,1)S(1)}, bf16[1,5120,128]{2,1,0:T(8,128)(2,1)}, u32[]{:S(2)}) copy-start(bf16[1,5120,128]{2,1,0:T(8,128)(2,1)} %param.11) | copy-start | bytes 3932164
  40.1 93.6 %all-to-all-start.1 = ((bf16[8,264,640]{2,1,0:T(8,128)(2,1)}), bf16[8,264,640]{2,1,0:T(8,128)(2,1)}, u32[]{:S(2)}, u32[]{:S(2)}) async-start(bf16[8,264,640]{2,1,0:T(8,128)(2,1)} %broadcast_in_dim.20), calls=%async_computation.1 | async-start | bytes 5406720 | tf_op jit(solution)/shard_map/all_to_all | solution.py:191
  46.1 62.9 %collective-permute-start.2 = (bf16[5120,128]{1,0:T(8,128)(2,1)S(1)}, bf16[5120,128]{1,0:T(8,128)(2,1)S(1)}, u32[]{:S(2)}, u32[]{:S(2)}) collective-permute-start(bf16[5120,128]{1,0:T(8,128)(2,1)S(1)} %bitcast.9), channel_id=1, source_target_pairs={{0,257},{1,256},{256,1},{257,0},{2,259},{3,258},{258,3},{259,2},{4... | collective-permute-start | bytes 3932168 | tf_op jit(solution)/shard_map/ppermute | solution.py:204
  48.5 81.1 %collective-permute-start.3 = (bf16[5120,128]{1,0:T(8,128)(2,1)}, bf16[5120,128]{1,0:T(8,128)(2,1)}, u32[]{:S(2)}, u32[]{:S(2)}) collective-permute-start(bf16[5120,128]{1,0:T(8,128)(2,1)} %bitcast.12), channel_id=1, source_target_pairs={{0,257},{1,256},{256,1},{257,0},{2,259},{3,258},{258,3},{259,2},{4... | collective-permute-start | bytes 3932168 | tf_op jit(solution)/shard_map/ppermute | solution.py:204
  53.1 78.4 %collective-permute-start = (bf16[5120,128]{1,0:T(8,128)(2,1)S(1)}, bf16[5120,128]{1,0:T(8,128)(2,1)S(1)}, u32[]{:S(2)}, u32[]{:S(2)}) collective-permute-start(bf16[5120,128]{1,0:T(8,128)(2,1)S(1)} %bitcast.10), channel_id=1, source_target_pairs={{0,128},{128,0},{1,129},{129,1},{2,130},{130,2},{3,131},{131,3},{4... | collective-permute-start | bytes 3932168 | tf_op jit(solution)/shard_map/ppermute | solution.py:200
  55.1 77.5 %collective-permute-start.1 = (bf16[5120,128]{1,0:T(8,128)(2,1)}, bf16[5120,128]{1,0:T(8,128)(2,1)S(1)}, u32[]{:S(2)}, u32[]{:S(2)}) collective-permute-start(bf16[5120,128]{1,0:T(8,128)(2,1)} %bitcast.13), channel_id=1, source_target_pairs={{0,128},{128,0},{1,129},{129,1},{2,130},{130,2},{3,131},{131,3},{4... | collective-permute-start | bytes 3932168 | tf_op jit(solution)/shard_map/ppermute | solution.py:200
  57.5 95.0 %collective-permute-start.6 = (bf16[1024,640]{1,0:T(8,128)(2,1)}, bf16[1024,640]{1,0:T(8,128)(2,1)}, u32[]{:S(2)}, u32[]{:S(2)}) collective-permute-start(bf16[1024,640]{1,0:T(8,128)(2,1)} %bitcast.5.d0), channel_id=1, source_target_pairs={{0,256},{256,0},{1,257},{257,1},{2,258},{258,2},{3,259},{259,3},{4... | collective-permute-start | bytes 3932168 | tf_op jit(solution)/shard_map/ppermute | solution.py:208
  109.0 45.9 %collective-permute-start.4 = (bf16[5120,128]{1,0:T(8,128)(2,1)S(1)}, bf16[5120,128]{1,0:T(8,128)(2,1)}, u32[]{:S(2)}, u32[]{:S(2)}) collective-permute-start(bf16[5120,128]{1,0:T(8,128)(2,1)S(1)} %collective-permute-done.2.g0), channel_id=1, source_target_pairs={{0,128},{128,0},{1,129},{129,1},{2,130},{130,2},{3,131},{131,3},{4... | collective-permute-start | bytes 3932168 | tf_op jit(solution)/shard_map/ppermute | solution.py:200
  129.6 25.3 %collective-permute-start.5 = (bf16[5120,128]{1,0:T(8,128)(2,1)}, bf16[5120,128]{1,0:T(8,128)(2,1)}, u32[]{:S(2)}, u32[]{:S(2)}) collective-permute-start(bf16[5120,128]{1,0:T(8,128)(2,1)} %collective-permute-done.3.u0), channel_id=1, source_target_pairs={{0,128},{128,0},{1,129},{129,1},{2,130},{130,2},{3,131},{131,3},{4... | collective-permute-start | bytes 3932168 | tf_op jit(solution)/shard_map/ppermute | solution.py:200
  131.5 1.1 copy-start.2
  132.6 1.1 copy-start.4
  133.7 1.3 copy-start.1
  135.0 1.3 copy-start.3
  136.3 1.3 copy-start.5
  144.8 20.0 %all-to-all-start.3 = ((bf16[8,256,256]{2,1,0:T(8,128)(2,1)}), bf16[8,256,256]{2,1,0:T(8,128)(2,1)S(1)}, u32[]{:S(2)}, u32[]{:S(2)}) async-start(bf16[8,256,256]{2,1,0:T(8,128)(2,1)} %broadcast_in_dim.35), calls=%async_computation.3 | async-start | bytes 2097152 | tf_op jit(solution)/shard_map/all_to_all | solution.py:191
  150.5 21.0 %collective-permute-start.8 = (bf16[1024,640]{1,0:T(8,128)(2,1)}, bf16[1024,640]{1,0:T(8,128)(2,1)}, u32[]{:S(2)}, u32[]{:S(2)}) collective-permute-start(bf16[1024,640]{1,0:T(8,128)(2,1)} %bitcast.5.d0), channel_id=1, source_target_pairs={{0,128},{128,0},{1,129},{129,1},{2,130},{130,2},{3,131},{131,3},{4... | collective-permute-start | bytes 3932168 | tf_op jit(solution)/shard_map/ppermute | solution.py:200
  152.5 24.6 %collective-permute-start.7 = (bf16[1024,640]{1,0:T(8,128)(2,1)}, bf16[1024,640]{1,0:T(8,128)(2,1)}, u32[]{:S(2)}, u32[]{:S(2)}) collective-permute-start(bf16[1024,640]{1,0:T(8,128)(2,1)} %collective-permute-done.6.d0), channel_id=1, source_target_pairs={{0,128},{128,0},{1,129},{129,1},{2,130},{130,2},{3,131},{131,3},{4... | collective-permute-start | bytes 3932168 | tf_op jit(solution)/shard_map/ppermute | solution.py:200
  165.9 19.1 %all-to-all-start.2 = ((bf16[8,256,256]{2,1,0:T(8,128)(2,1)}), bf16[8,256,256]{2,1,0:T(8,128)(2,1)S(1)}, u32[]{:S(2)}, u32[]{:S(2)}) async-start(bf16[8,256,256]{2,1,0:T(8,128)(2,1)} %broadcast_in_dim.34), calls=%async_computation.2 | async-start | bytes 2097152 | tf_op jit(solution)/shard_map/all_to_all | solution.py:191

commit v2 on v1

v2 whole, which is shorter than its diff:
```python
import functools

import jax
import jax.numpy as jnp
import numpy as np
from jax import lax
from jax.experimental import pallas as pl
from jax.experimental.pallas import tpu as pltpu
from jax.sharding import Mesh, PartitionSpec as P

D = 5120
EPSILON = 1e-05
EXPERTS = 16
CAP = 16
SLOTS = EXPERTS * CAP
TOK = 128
FEAT = 640
TENSOR = 8
EXTRA = 8
VMEM = 20 * 1024 * 1024
PIECES = 4
PER = TENSOR // PIECES
DOWN_PIECES = 2
FLIPPED = (1, 0, 3, 2, 5, 4, 7, 6)
TENSOR_AXES = ("y", "xl")


def column_of(row):
    count = row.shape[1]
    i = lax.broadcasted_iota(jnp.int32, (count, count), 0)
    j = lax.broadcasted_iota(jnp.int32, (count, count), 1)
    return jnp.sum(jnp.where(i == j, row, 0), axis=1, keepdims=True), i, j


def dispatch_kernel(ids_ref, tokens_ref, out_ref):
    row = ids_ref[...]
    col, i, j = column_of(row)
    earlier = jnp.sum(jnp.where((col == row) & (i < j), 1, 0), axis=0, keepdims=True)
    placed = row * CAP + earlier
    slot = lax.broadcasted_iota(jnp.int32, (SLOTS, TOK), 0)
    placing = (slot == placed).astype(jnp.float32).astype(jnp.bfloat16)
    out_ref[...] = jnp.dot(
        placing, tokens_ref[...], preferred_element_type=jnp.float32
    ).astype(jnp.bfloat16)


def combine_kernel(ids_ref, back_ref, out_ref):
    row = ids_ref[...]
    col, i, j = column_of(row)
    earlier = jnp.sum(jnp.where((col == row) & (j < i), 1, 0), axis=1, keepdims=True)
    placed = col * CAP + earlier
    slot = lax.broadcasted_iota(jnp.int32, (TOK, SLOTS), 1)
    placing = (slot == placed).astype(jnp.float32).astype(jnp.bfloat16)
    out_ref[...] = jnp.dot(
        placing, back_ref[...], preferred_element_type=jnp.float32
    ).astype(jnp.bfloat16)


def gained(x_ref, k):
    rows = x_ref[k, :SLOTS, :].astype(jnp.float32)
    more = x_ref[k, SLOTS:, :].astype(jnp.float32)
    return rows, rows * (more[0:1] + more[1:2] + more[2:3]), more[3:4]


def fetched(sources, held, sems, pieces):
    depth = held.shape[1] // pieces
    copies = []
    for piece in range(pieces):
        part = pl.ds(piece * depth, depth)
        for k, source in enumerate(sources):
            copies.append(
                pltpu.make_async_copy(source.at[part], held.at[k, part], sems.at[piece, k])
            )
    for copy in copies:
        copy.start()
    return lambda piece: [c.wait() for c in copies[len(sources) * piece :][: len(sources)]]


def activated(acc, scale, out_ref):
    for k in range(2):
        gate = acc[:, 256 * k : 256 * k + 128] * scale
        upper = acc[:, 256 * k + 128 : 256 * k + 256] * scale
        out_ref[:, 128 * k : 128 * k + 128] = (jax.nn.silu(gate) * upper).astype(jnp.bfloat16)


def weighed(held, piece):
    depth = PER * FEAT
    return jnp.concatenate(
        [held[k, piece * depth : (piece + 1) * depth, :] for k in range(4)], axis=1
    )


def first_kernel(x_ref, g0, u0, g1, u1, out_ref, scale_ref, held, acc, sems):
    wait = fetched((g0, u0, g1, u1), held, sems, PIECES)
    squares, logit = 0.0, 0.0
    for piece in range(PIECES):
        parts = []
        for k in range(PER):
            rows, values, router = gained(x_ref, piece * PER + k)
            squares += jnp.sum(rows * rows, axis=1, keepdims=True)
            logit += jnp.sum(values * router, axis=1, keepdims=True)
            parts.append(values.astype(jnp.bfloat16))
        wait(piece)
        term = jnp.dot(
            jnp.concatenate(parts, axis=1), weighed(held, piece), preferred_element_type=jnp.float32
        )
        acc[...] = term if piece == 0 else acc[...] + term
    rstd = lax.rsqrt(squares / D + EPSILON)
    scale = rstd * jax.nn.sigmoid(logit * rstd)
    scale_ref[...] = scale
    activated(acc, scale, out_ref)


def second_kernel(x_ref, scale_ref, g0, u0, g1, u1, out_ref, held, acc, sems):
    wait = fetched((g0, u0, g1, u1), held, sems, PIECES)
    for piece in range(PIECES):
        parts = [gained(x_ref, piece * PER + k)[1].astype(jnp.bfloat16) for k in range(PER)]
        wait(piece)
        term = jnp.dot(
            jnp.concatenate(parts, axis=1), weighed(held, piece), preferred_element_type=jnp.float32
        )
        acc[...] = term if piece == 0 else acc[...] + term
    activated(acc, scale_ref[...], out_ref)


IN_VMEM = pl.BlockSpec(memory_space=pltpu.VMEM)
IN_HBM = pl.BlockSpec(memory_space=pl.ANY)


def left_in_hbm(arrays):
    return [pltpu.with_memory_space_constraint(a, pltpu.HBM) for a in arrays]


HIDDEN = jax.ShapeDtypeStruct((SLOTS, 256), jnp.bfloat16)
GATE_COST = pl.CostEstimate(
    flops=2 * SLOTS * D * 512, bytes_accessed=2 * (D * 512 + D * SLOTS), transcendentals=SLOTS * 256
)
DOWN_COST = pl.CostEstimate(
    flops=2 * SLOTS * 2048 * FEAT, bytes_accessed=2 * 2048 * (FEAT + SLOTS), transcendentals=0
)
PARAMS = pltpu.CompilerParams(vmem_limit_bytes=VMEM)
GATE_SCRATCH = [
    pltpu.VMEM((4, D, 128), jnp.bfloat16),
    pltpu.VMEM((SLOTS, 512), jnp.float32),
    pltpu.SemaphoreType.DMA((PIECES, 4)),
]


def first_half(x, *weights):
    return pl.pallas_call(
        first_kernel,
        in_specs=[IN_VMEM] + [IN_HBM] * 4,
        out_specs=[IN_VMEM, IN_VMEM],
        out_shape=[HIDDEN, jax.ShapeDtypeStruct((SLOTS, 1), jnp.float32)],
        scratch_shapes=GATE_SCRATCH,
        compiler_params=PARAMS,
        cost_estimate=GATE_COST,
    )(x, *left_in_hbm(weights))


def second_half(x, scale, *weights):
    return pl.pallas_call(
        second_kernel,
        in_specs=[IN_VMEM, IN_VMEM] + [IN_HBM] * 4,
        out_specs=IN_VMEM,
        out_shape=HIDDEN,
        scratch_shapes=GATE_SCRATCH,
        compiler_params=PARAMS,
        cost_estimate=GATE_COST,
    )(x, scale, *left_in_hbm(weights))


def down_kernel(order, h_ref, d0, d1, *rest):
    *before, out_ref, held, acc, sems = rest
    wait = fetched((d0, d1), held, sems, DOWN_PIECES)
    each = TENSOR // DOWN_PIECES
    for piece in range(DOWN_PIECES):
        places = range(piece * each, (piece + 1) * each)
        hidden = jnp.concatenate([h_ref[order[k]] for k in places], axis=1)
        wait(piece)
        slices = [held[w, 128 * k : 128 * k + 128, :] for k in places for w in range(2)]
        term = jnp.dot(
            hidden, jnp.concatenate(slices, axis=0), preferred_element_type=jnp.float32
        )
        if piece == 0:
            acc[...] = before[0][...] + term if before else term
        elif piece < DOWN_PIECES - 1:
            acc[...] += term
        else:
            out_ref[...] = (acc[...] + term).astype(out_ref.dtype)


def down_half(hidden, d0, d1, before, dtype, order):
    return pl.pallas_call(
        functools.partial(down_kernel, order),
        in_specs=[IN_VMEM, IN_HBM, IN_HBM] + ([IN_VMEM] if before is not None else []),
        out_specs=IN_VMEM,
        out_shape=jax.ShapeDtypeStruct((SLOTS, FEAT), dtype),
        scratch_shapes=[
            pltpu.VMEM((2, 1024, FEAT), jnp.bfloat16),
            pltpu.VMEM((SLOTS, FEAT), jnp.float32),
            pltpu.SemaphoreType.DMA((DOWN_PIECES, 2)),
        ],
        compiler_params=PARAMS,
        cost_estimate=DOWN_COST,
    )(hidden, *left_in_hbm((d0, d1)), *(() if before is None else (before,)))


def gathered(array):
    copies = jnp.broadcast_to(array[None], (TENSOR, *array.shape))
    return lax.all_to_all(copies, TENSOR_AXES, 0, 0, tiled=True)


def over_experts(array):
    parts = array.reshape(EXPERTS, CAP, FEAT)
    return lax.all_to_all(parts, "z", 0, 0, tiled=True).reshape(SLOTS, FEAT)


def other_core(array):
    return lax.ppermute(array, "co", [(0, 1), (1, 0)])


def across_border(array):
    return lax.ppermute(array, ("xh", "xl"), [(i, 3 - i) for i in range(4)])


def across_halves(array):
    return lax.ppermute(array, "xh", [(0, 1), (1, 0)])


def side_rows(norm_gain, router):
    high = norm_gain.astype(jnp.bfloat16)
    rest = norm_gain - high.astype(jnp.float32)
    middle = rest.astype(jnp.bfloat16)
    low = (rest - middle.astype(jnp.float32)).astype(jnp.bfloat16)
    mine = lax.axis_index("z") == jnp.arange(EXPERTS, dtype=jnp.int32)
    column = jnp.sum(jnp.where(mine[None, :], router.astype(jnp.float32), 0.0), axis=1)
    zero = jnp.zeros_like(high)
    return jnp.stack([high, middle, low, column.astype(jnp.bfloat16)] + [zero] * (EXTRA - 4))


def on_device(tokens, norm_gain, router, expert_ids, gate_proj, up_proj, down_proj):
    ids = expert_ids.reshape(1, TOK)
    gate, upper, down = gate_proj[0], up_proj[0], down_proj[0]

    outgoing = pl.pallas_call(
        dispatch_kernel, out_shape=jax.ShapeDtypeStruct((SLOTS, FEAT), jnp.bfloat16)
    )(ids, tokens)
    arrived = over_experts(outgoing)

    gate_far, upper_far = across_border(gate), across_border(upper)
    gate_near, upper_near = other_core(gate), other_core(upper)
    arrived, gate_far = lax.optimization_barrier((arrived, gate_far))
    gate_last, upper_last = other_core(gate_far), other_core(upper_far)
    down_near = other_core(down)
    down_sent, upper_far = lax.optimization_barrier((down, upper_far))
    down_far = across_halves(down_sent)
    down_last = other_core(down_far)

    rows = gathered(jnp.concatenate([arrived, side_rows(norm_gain, router)], axis=0))
    hidden, scale = first_half(rows, gate, upper, gate_near, upper_near)
    full = gathered(hidden)
    hidden_far = second_half(rows, scale, gate_far, upper_far, gate_last, upper_last)
    full_far = gathered(hidden_far)
    part = down_half(full, down, down_near, None, jnp.float32, tuple(range(TENSOR)))
    summed = down_half(full_far, down_far, down_last, part, jnp.bfloat16, FLIPPED)
    returned = over_experts(summed)
    return pl.pallas_call(
        combine_kernel, out_shape=jax.ShapeDtypeStruct((TOK, FEAT), jnp.bfloat16)
    )(ids, returned)


def solution(mesh):
    fine = Mesh(
        np.asarray(mesh.devices).reshape(2, 2, 16, 4, 2), ("xh", "co", "z", "y", "xl")
    )
    section, tensor = ("xh", "co"), ("y", "xl")
    in_specs = (
        P((*section, "z"), tensor),
        P(tensor),
        P(tensor, None),
        P((*section, "z"), None),
        P("z", None, (*section, *tensor)),
        P("z", None, (*section, *tensor)),
        P("z", section, tensor),
    )
    return jax.shard_map(
        on_device,
        mesh=fine,
        in_specs=in_specs,
        out_specs=P((*section, "z"), tensor),
        check_vma=False,
    )
```

time: 227 us -> 178 us (0.78)
  waiting for transfers between devices: 98.2 us -> 67.2 us
  Pallas kernels: 28.2 us -> 17.2 us
  local copies, waits for them, and re-layouts: 10.4 us -> 6.3 us
    ppermute x2, waiting for transfers between devices: 68.1 us -> 32.8 us  [across_border(): return lax.ppermute(array, ('xh', 'xl'), [(i, 3 - i) for i in range(4)])]
    pallas_call x4, Pallas kernels: 24.2 us -> 13.2 us  [the longest x2 6.28 us: down_half(): pl.pallas_call(functools.partial(down_kernel, order), in_specs=[IN_VMEM,...]
    all_to_all x3, waiting for transfers between devices: 11 us -> 15.2 us  [gathered(): return lax.all_to_all(copies, TENSOR_AXES, 0, 0, tiled=True)]
    unnamed x12 -> x4, local copies, waits for them, and re-layouts: 6.13 us -> 2.11 us
  transfers between devices with their start and end apart: 13 -> 13, of which waited for: 5 -> 5; matrix products, arithmetic and copies ran while one was open for 2% -> 2% of each run, Pallas kernels for 8% -> 7%
where the time goes in v2:
time: 178 us
  waiting for transfers between devices  67.2 us (38%)
  starting transfers between devices  54.5 us (31%)
  blocking collectives  30.6 us (17%)
  Pallas kernels  17.2 us (10%)
  local copies, waits for them, and re-layouts  6.3 us (4%)
    ppermute x2, waiting for transfers between devices, across_border(): return lax.ppermute(array, ('xh', 'xl'), [(i, 3 - i) for i in range(4)])  32.8 us
    all_to_all x1, blocking collectives, over_experts(): return lax.all_to_all(parts, 'z', 0, 0, tiled=True).reshape(SLOTS, FEAT)  30.6 us
    all_to_all x1, waiting for transfers between devices, over_experts(): return lax.all_to_all(parts, 'z', 0, 0, tiled=True).reshape(SLOTS, FEAT)  18.8 us
    all_to_all x3, starting transfers between devices, gathered(): return lax.all_to_all(copies, TENSOR_AXES, 0, 0, tiled=True)  17.1 us
    all_to_all x3, waiting for transfers between devices, gathered(): return lax.all_to_all(copies, TENSOR_AXES, 0, 0, tiled=True)  15.2 us
    all_to_all x1, starting transfers between devices, over_experts(): return lax.all_to_all(parts, 'z', 0, 0, tiled=True).reshape(SLOTS, FEAT)  15.2 us
    ppermute x6, starting transfers between devices, other_core(): return lax.ppermute(array, 'co', [(0, 1), (1, 0)])  12.7 us
    pallas_call x2, Pallas kernels, down_half(): pl.pallas_call(functools.partial(down_kernel, order), in_specs=[IN_VMEM,...  6.28 us
  transfers between devices with their start and end apart: 13, of which 5 were waited for; matrix products, arithmetic and copies ran while one was open for 2% of the time, Pallas kernels for 7%

profile of v2, /device:TPU:14, one launch (start us, length us, event | category | flops | bytes accessed | tf_op | source)
XLA Modules:
  0.0 177.6 jit_solution(15551110188556252151)
XLA Ops:
  0.0 2.4 %collective-permute-start = (bf16[5120,128]{1,0:T(8,128)(2,1)}, bf16[5120,128]{1,0:T(8,128)(2,1)S(1)}, u32[]{:S(2)}, u32[]{:S(2)}) collective-permute-start(bf16[5120,128]{1,0:T(8,128)(2,1)} %bitcast.15), channel_id=1, source_target_pairs={{0,257},{1,256},{256,1},{257,0},{2,259},{3,258},{258,3},{259,2},{4... | collective-permute-start | bytes 3932168 | tf_op jit(solution)/shard_map/ppermute | solution.py:224
  2.4 2.0 %shard_map.73 = bf16[256,640]{1,0:T(8,128)(2,1)} custom-call(s32[1,128]{1,0:T(1,128)} %bitcast.21, bf16[128,640]{1,0:T(8,128)(2,1)} %tokens_ref.1), custom_call_target="tpu_custom_call" | custom-call | tf_op jit(solution)/shard_map/pallas_call | solution.py:246
  4.4 15.2 %all-to-all-start = ((bf16[16,16,640]{2,1,0:T(8,128)(2,1)}), bf16[16,16,640]{2,1,0:T(8,128)(2,1)S(1)}, u32[]{:S(2)}, u32[]{:S(2)}) async-start(bf16[16,16,640]{2,1,0:T(8,128)(2,1)} %bitcast.13), calls=%async_computation | async-start | bytes 655360 | tf_op jit(solution)/shard_map/all_to_all | solution.py:216
  19.6 0.8 subtract_convert_fusion
  20.4 0.8 select_reduce_fusion
  21.2 18.8 %all-to-all-done = bf16[16,16,640]{2,1,0:T(8,128)(2,1)S(1)} async-done(((bf16[16,16,640]{2,1,0:T(8,128)(2,1)}), bf16[16,16,640]{2,1,0:T(8,128)(2,1)S(1)}, u32[]{:S(2)}, u32[]{:S(2)}) %all-to-all-start) | async-done | bytes 327712 | tf_op jit(solution)/shard_map/all_to_all | solution.py:216
  40.0 0.0 collective-permute-done.g0
  40.0 0.0 copy-start
  40.0 1.1 copy-done
  41.1 0.3 concatenate.7
  41.4 1.7 broadcast_in_dim.20
  43.1 5.8 %all-to-all-start.1 = ((bf16[8,264,640]{2,1,0:T(8,128)(2,1)}), bf16[8,264,640]{2,1,0:T(8,128)(2,1)S(1)}, u32[]{:S(2)}, u32[]{:S(2)}) async-start(bf16[8,264,640]{2,1,0:T(8,128)(2,1)} %broadcast_in_dim.20), calls=%async_computation.1 | async-start | bytes 5406720 | tf_op jit(solution)/shard_map/all_to_all | solution.py:211
  49.0 3.8 %collective-permute-start.3 = (bf16[5120,128]{1,0:T(8,128)(2,1)}, bf16[5120,128]{1,0:T(8,128)(2,1)}, u32[]{:S(2)}, u32[]{:S(2)}) collective-permute-start(bf16[5120,128]{1,0:T(8,128)(2,1)} %bitcast.18), channel_id=1, source_target_pairs={{0,257},{1,256},{256,1},{257,0},{2,259},{3,258},{258,3},{259,2},{4... | collective-permute-start | bytes 3932168 | tf_op jit(solution)/shard_map/ppermute | solution.py:224
  52.7 1.9 %collective-permute-start.1 = (bf16[5120,128]{1,0:T(8,128)(2,1)}, bf16[5120,128]{1,0:T(8,128)(2,1)S(1)}, u32[]{:S(2)}, u32[]{:S(2)}) collective-permute-start(bf16[5120,128]{1,0:T(8,128)(2,1)} %bitcast.16), channel_id=1, source_target_pairs={{0,128},{128,0},{1,129},{129,1},{2,130},{130,2},{3,131},{131,3},{4... | collective-permute-start | bytes 3932168 | tf_op jit(solution)/shard_map/ppermute | solution.py:220
  54.7 2.4 %collective-permute-start.2 = (bf16[5120,128]{1,0:T(8,128)(2,1)}, bf16[5120,128]{1,0:T(8,128)(2,1)}, u32[]{:S(2)}, u32[]{:S(2)}) collective-permute-start(bf16[5120,128]{1,0:T(8,128)(2,1)} %bitcast.19), channel_id=1, source_target_pairs={{0,128},{128,0},{1,129},{129,1},{2,130},{130,2},{3,131},{131,3},{4... | collective-permute-start | bytes 3932168 | tf_op jit(solution)/shard_map/ppermute | solution.py:220
  57.1 32.8 %collective-permute-done.3.u0 = bf16[5120,128]{1,0:T(8,128)(2,1)} collective-permute-done((bf16[5120,128]{1,0:T(8,128)(2,1)}, bf16[5120,128]{1,0:T(8,128)(2,1)}, u32[]{:S(2)}, u32[]{:S(2)}) %collective-permute-start.3) | collective-permute-done | bytes 1310752 | tf_op jit(solution)/shard_map/ppermute | solution.py:224
  89.9 3.4 %collective-permute-start.6 = (bf16[1024,640]{1,0:T(8,128)(2,1)}, bf16[1024,640]{1,0:T(8,128)(2,1)}, u32[]{:S(2)}, u32[]{:S(2)}) collective-permute-start(bf16[1024,640]{1,0:T(8,128)(2,1)} %bitcast.9), channel_id=1, source_target_pairs={{0,256},{256,0},{1,257},{257,1},{2,258},{258,2},{3,259},{259,3},{4... | collective-permute-start | bytes 3932168 | tf_op jit(solution)/shard_map/ppermute | solution.py:228
  93.4 1.9 %collective-permute-start.4 = (bf16[5120,128]{1,0:T(8,128)(2,1)}, bf16[5120,128]{1,0:T(8,128)(2,1)}, u32[]{:S(2)}, u32[]{:S(2)}) collective-permute-start(bf16[5120,128]{1,0:T(8,128)(2,1)} %copy-done), channel_id=1, source_target_pairs={{0,128},{128,0},{1,129},{129,1},{2,130},{130,2},{3,131},{131,3},{4... | collective-permute-start | bytes 3932168 | tf_op jit(solution)/shard_map/ppermute | solution.py:220
  95.3 2.4 %collective-permute-start.5 = (bf16[5120,128]{1,0:T(8,128)(2,1)}, bf16[5120,128]{1,0:T(8,128)(2,1)}, u32[]{:S(2)}, u32[]{:S(2)}) collective-permute-start(bf16[5120,128]{1,0:T(8,128)(2,1)} %collective-permute-done.3.u0), channel_id=1, source_target_pairs={{0,128},{128,0},{1,129},{129,1},{2,130},{130,2},{3,131},{131,3},{4... | collective-permute-start | bytes 3932168 | tf_op jit(solution)/shard_map/ppermute | solution.py:220
  97.7 0.0 collective-permute-done.1.g1
  97.7 0.0 copy-start.1
  97.7 1.0 copy-done.1
  98.8 0.0 collective-permute-done.2.u1
  98.8 0.0 all-to-all-done.1.x_ref
  98.8 3.4 %shard_map.74 = (bf16[256,256]{1,0:T(8,128)(2,1)S(1)}, f32[256,1]{1,0:T(8,128)S(1)}) custom-call(bf16[8,264,640]{2,1,0:T(8,128)(2,1)S(1)} %all-to-all-done.1.x_ref, bf16[5120,128]{1,0:T(8,128)(2,1)} %bitcast.17, bf16[5120,128]{1,0:T(8,128)(2,1)} %bitcast.20, bf16[5120,128]{1,0:T(8,128)(2,1)} %copy-done.1, bf16[5120,128]{1,0:T(8,128)(2,1)} %collective-permute-done.2.u1), custom_call_target="tpu_custom_call" | custom-call | flops 1342177280 | bytes 7864320 | tf_op jit(solution)/shard_map/pallas_call | solution.py:150
  102.2 1.1 broadcast_in_dim.35
  103.3 5.7 %all-to-all-start.3 = ((bf16[8,256,256]{2,1,0:T(8,128)(2,1)}), bf16[8,256,256]{2,1,0:T(8,128)(2,1)}, u32[]{:S(2)}, u32[]{:S(2)}) async-start(bf16[8,256,256]{2,1,0:T(8,128)(2,1)} %broadcast_in_dim.35), calls=%async_computation.3 | async-start | bytes 2097152 | tf_op jit(solution)/shard_map/all_to_all | solution.py:211
  109.0 1.9 %collective-permute-start.8 = (bf16[1024,640]{1,0:T(8,128)(2,1)}, bf16[1024,640]{1,0:T(8,128)(2,1)}, u32[]{:S(2)}, u32[]{:S(2)}) collective-permute-start(bf16[1024,640]{1,0:T(8,128)(2,1)} %bitcast.10), channel_id=1, source_target_pairs={{0,128},{128,0},{1,129},{129,1},{2,130},{130,2},{3,131},{131,3},{4... | collective-permute-start | bytes 3932168 | tf_op jit(solution)/shard_map/ppermute | solution.py:220
  110.9 0.3 collective-permute-done.6.d0
  111.2 2.1 %collective-permute-start.7 = (bf16[1024,640]{1,0:T(8,128)(2,1)}, bf16[1024,640]{1,0:T(8,128)(2,1)}, u32[]{:S(2)}, u32[]{:S(2)}) collective-permute-start(bf16[1024,640]{1,0:T(8,128)(2,1)} %collective-permute-done.6.d0), channel_id=1, source_target_pairs={{0,128},{128,0},{1,129},{129,1},{2,130},{130,2},{3,131},{131,3},{4... | collective-permute-start | bytes 3932168 | tf_op jit(solution)/shard_map/ppermute | solution.py:220
  113.3 0.0 collective-permute-done.4.g1
  113.3 0.0 collective-permute-done.5.u1
  113.3 3.5 %shard_map.75 = bf16[256,256]{1,0:T(8,128)(2,1)S(1)} custom-call(bf16[8,264,640]{2,1,0:T(8,128)(2,1)S(1)} %all-to-all-done.1.x_ref, f32[256,1]{1,0:T(8,128)S(1)} %get-tuple-element.12.scale_ref, bf16[5120,128]{1,0:T(8,128)(2,1)} %copy-done, bf16[5120,128]{1,0:T(8,128)(2,1)} %collective-permute-done.3.u0, bf16[5120,128]{1,0:T(8,128)(2,1)} %collective-permute-done.4.g1, ...), custom_call_target="tpu_custom_call" | custom-call | flops 1342177280 | bytes 7864320 | tf_op jit(solution)/shard_map/pallas_call | solution.py:162
  116.8 6.1 %all-to-all-done.3.h_ref = bf16[8,256,256]{2,1,0:T(8,128)(2,1)} async-done(((bf16[8,256,256]{2,1,0:T(8,128)(2,1)}), bf16[8,256,256]{2,1,0:T(8,128)(2,1)}, u32[]{:S(2)}, u32[]{:S(2)}) %all-to-all-start.3) | async-done | bytes 1048608 | tf_op jit(solution)/shard_map/all_to_all | solution.py:211
  122.9 1.0 broadcast_in_dim.34
  123.9 5.6 %all-to-all-start.2 = ((bf16[8,256,256]{2,1,0:T(8,128)(2,1)}), bf16[8,256,256]{2,1,0:T(8,128)(2,1)S(1)}, u32[]{:S(2)}, u32[]{:S(2)}) async-start(bf16[8,256,256]{2,1,0:T(8,128)(2,1)} %broadcast_in_dim.34), calls=%async_computation.2 | async-start | bytes 2097152 | tf_op jit(solution)/shard_map/all_to_all | solution.py:211
  129.5 0.0 collective-permute-done.8.d1
  129.5 3.7 %shard_map.76.rest_0_ = f32[256,640]{1,0:T(8,128)S(1)} custom-call(bf16[8,256,256]{2,1,0:T(8,128)(2,1)} %all-to-all-done.3.h_ref, bf16[1024,640]{1,0:T(8,128)(2,1)} %bitcast.11, bf16[1024,640]{1,0:T(8,128)(2,1)} %collective-permute-done.8.d1), custom_call_target="tpu_custom_call" | custom-call | flops 671088640 | bytes 3670016 | tf_op jit(solution)/shard_map/pallas_call | solution.py:194
  133.3 0.0 collective-permute-done.7.d1
  133.3 9.2 %all-to-all-done.2.h_ref = bf16[8,256,256]{2,1,0:T(8,128)(2,1)S(1)} async-done(((bf16[8,256,256]{2,1,0:T(8,128)(2,1)}), bf16[8,256,256]{2,1,0:T(8,128)(2,1)S(1)}, u32[]{:S(2)}, u32[]{:S(2)}) %all-to-all-start.2) | async-done | bytes 1048608 | tf_op jit(solution)/shard_map/all_to_all | solution.py:211
  142.5 2.5 %shard_map.77 = bf16[256,640]{1,0:T(8,128)(2,1)S(1)} custom-call(bf16[8,256,256]{2,1,0:T(8,128)(2,1)S(1)} %all-to-all-done.2.h_ref, bf16[1024,640]{1,0:T(8,128)(2,1)} %collective-permute-done.6.d0, bf16[1024,640]{1,0:T(8,128)(2,1)} %collective-permute-done.7.d1, f32[256,640]{1,0:T(8,128)S(1)} %shard_map.76.rest_0_), custom_call_target="tpu_custom_call" | custom-call | flops 671088640 | bytes 3670016 | tf_op jit(solution)/shard_map/pallas_call | solution.py:194
  145.0 30.6 %all_to_all.25 = bf16[16,16,640]{2,1,0:T(8,128)(2,1)} all-to-all(bf16[16,16,640]{2,1,0:T(8,128)(2,1)S(1)} %bitcast.8), channel_id=1, replica_groups=mesh['xh'=2,'co'=2,'z'=16,'y'=4,'xl'=2] {'z'}, dimensions={0} | all-to-all | bytes 655360 | tf_op jit(solution)/shard_map/all_to_all | solution.py:216
  175.6 2.0 %shard_map.78 = bf16[128,640]{1,0:T(8,128)(2,1)} custom-call(s32[1,128]{1,0:T(1,128)} %bitcast.22, bf16[256,640]{1,0:T(8,128)(2,1)} %bitcast.14), custom_call_target="tpu_custom_call" | custom-call | tf_op jit(solution)/shard_map/pallas_call | solution.py:268
  (6 shorter events, 0.0 us)
Async XLA Ops:
  0.0 40.0 %collective-permute-start = (bf16[5120,128]{1,0:T(8,128)(2,1)}, bf16[5120,128]{1,0:T(8,128)(2,1)S(1)}, u32[]{:S(2)}, u32[]{:S(2)}) collective-permute-start(bf16[5120,128]{1,0:T(8,128)(2,1)} %bitcast.15), channel_id=1, source_target_pairs={{0,257},{1,256},{256,1},{257,0},{2,259},{3,258},{258,3},{259,2},{4... | collective-permute-start | bytes 3932168 | tf_op jit(solution)/shard_map/ppermute | solution.py:224
  4.4 35.6 %all-to-all-start = ((bf16[16,16,640]{2,1,0:T(8,128)(2,1)}), bf16[16,16,640]{2,1,0:T(8,128)(2,1)S(1)}, u32[]{:S(2)}, u32[]{:S(2)}) async-start(bf16[16,16,640]{2,1,0:T(8,128)(2,1)} %bitcast.13), calls=%async_computation | async-start | bytes 655360 | tf_op jit(solution)/shard_map/all_to_all | solution.py:216
  40.0 1.1 copy-start
  43.1 55.6 %all-to-all-start.1 = ((bf16[8,264,640]{2,1,0:T(8,128)(2,1)}), bf16[8,264,640]{2,1,0:T(8,128)(2,1)S(1)}, u32[]{:S(2)}, u32[]{:S(2)}) async-start(bf16[8,264,640]{2,1,0:T(8,128)(2,1)} %broadcast_in_dim.20), calls=%async_computation.1 | async-start | bytes 5406720 | tf_op jit(solution)/shard_map/all_to_all | solution.py:211
  49.0 41.0 %collective-permute-start.3 = (bf16[5120,128]{1,0:T(8,128)(2,1)}, bf16[5120,128]{1,0:T(8,128)(2,1)}, u32[]{:S(2)}, u32[]{:S(2)}) collective-permute-start(bf16[5120,128]{1,0:T(8,128)(2,1)} %bitcast.18), channel_id=1, source_target_pairs={{0,257},{1,256},{256,1},{257,0},{2,259},{3,258},{258,3},{259,2},{4... | collective-permute-start | bytes 3932168 | tf_op jit(solution)/shard_map/ppermute | solution.py:224
  52.7 45.0 %collective-permute-start.1 = (bf16[5120,128]{1,0:T(8,128)(2,1)}, bf16[5120,128]{1,0:T(8,128)(2,1)S(1)}, u32[]{:S(2)}, u32[]{:S(2)}) collective-permute-start(bf16[5120,128]{1,0:T(8,128)(2,1)} %bitcast.16), channel_id=1, source_target_pairs={{0,128},{128,0},{1,129},{129,1},{2,130},{130,2},{3,131},{131,3},{4... | collective-permute-start | bytes 3932168 | tf_op jit(solution)/shard_map/ppermute | solution.py:220
  54.7 44.1 %collective-permute-start.2 = (bf16[5120,128]{1,0:T(8,128)(2,1)}, bf16[5120,128]{1,0:T(8,128)(2,1)}, u32[]{:S(2)}, u32[]{:S(2)}) collective-permute-start(bf16[5120,128]{1,0:T(8,128)(2,1)} %bitcast.19), channel_id=1, source_target_pairs={{0,128},{128,0},{1,129},{129,1},{2,130},{130,2},{3,131},{131,3},{4... | collective-permute-start | bytes 3932168 | tf_op jit(solution)/shard_map/ppermute | solution.py:220
  89.9 21.3 %collective-permute-start.6 = (bf16[1024,640]{1,0:T(8,128)(2,1)}, bf16[1024,640]{1,0:T(8,128)(2,1)}, u32[]{:S(2)}, u32[]{:S(2)}) collective-permute-start(bf16[1024,640]{1,0:T(8,128)(2,1)} %bitcast.9), channel_id=1, source_target_pairs={{0,256},{256,0},{1,257},{257,1},{2,258},{258,2},{3,259},{259,3},{4... | collective-permute-start | bytes 3932168 | tf_op jit(solution)/shard_map/ppermute | solution.py:228
  93.4 19.9 %collective-permute-start.4 = (bf16[5120,128]{1,0:T(8,128)(2,1)}, bf16[5120,128]{1,0:T(8,128)(2,1)}, u32[]{:S(2)}, u32[]{:S(2)}) collective-permute-start(bf16[5120,128]{1,0:T(8,128)(2,1)} %copy-done), channel_id=1, source_target_pairs={{0,128},{128,0},{1,129},{129,1},{2,130},{130,2},{3,131},{131,3},{4... | collective-permute-start | bytes 3932168 | tf_op jit(solution)/shard_map/ppermute | solution.py:220
  95.3 18.0 %collective-permute-start.5 = (bf16[5120,128]{1,0:T(8,128)(2,1)}, bf16[5120,128]{1,0:T(8,128)(2,1)}, u32[]{:S(2)}, u32[]{:S(2)}) collective-permute-start(bf16[5120,128]{1,0:T(8,128)(2,1)} %collective-permute-done.3.u0), channel_id=1, source_target_pairs={{0,128},{128,0},{1,129},{129,1},{2,130},{130,2},{3,131},{131,3},{4... | collective-permute-start | bytes 3932168 | tf_op jit(solution)/shard_map/ppermute | solution.py:220
  97.7 1.1 copy-start.1
  103.3 19.6 %all-to-all-start.3 = ((bf16[8,256,256]{2,1,0:T(8,128)(2,1)}), bf16[8,256,256]{2,1,0:T(8,128)(2,1)}, u32[]{:S(2)}, u32[]{:S(2)}) async-start(bf16[8,256,256]{2,1,0:T(8,128)(2,1)} %broadcast_in_dim.35), calls=%async_computation.3 | async-start | bytes 2097152 | tf_op jit(solution)/shard_map/all_to_all | solution.py:211
  109.0 20.5 %collective-permute-start.8 = (bf16[1024,640]{1,0:T(8,128)(2,1)}, bf16[1024,640]{1,0:T(8,128)(2,1)}, u32[]{:S(2)}, u32[]{:S(2)}) collective-permute-start(bf16[1024,640]{1,0:T(8,128)(2,1)} %bitcast.10), channel_id=1, source_target_pairs={{0,128},{128,0},{1,129},{129,1},{2,130},{130,2},{3,131},{131,3},{4... | collective-permute-start | bytes 3932168 | tf_op jit(solution)/shard_map/ppermute | solution.py:220
  111.2 22.0 %collective-permute-start.7 = (bf16[1024,640]{1,0:T(8,128)(2,1)}, bf16[1024,640]{1,0:T(8,128)(2,1)}, u32[]{:S(2)}, u32[]{:S(2)}) collective-permute-start(bf16[1024,640]{1,0:T(8,128)(2,1)} %collective-permute-done.6.d0), channel_id=1, source_target_pairs={{0,128},{128,0},{1,129},{129,1},{2,130},{130,2},{3,131},{131,3},{4... | collective-permute-start | bytes 3932168 | tf_op jit(solution)/shard_map/ppermute | solution.py:220
  123.9 18.5 %all-to-all-start.2 = ((bf16[8,256,256]{2,1,0:T(8,128)(2,1)}), bf16[8,256,256]{2,1,0:T(8,128)(2,1)S(1)}, u32[]{:S(2)}, u32[]{:S(2)}) async-start(bf16[8,256,256]{2,1,0:T(8,128)(2,1)} %broadcast_in_dim.34), calls=%async_computation.2 | async-start | bytes 2097152 | tf_op jit(solution)/shard_map/all_to_all | solution.py:211

commit v3 on v2

v3 whole, which is shorter than its diff:
```python
import jax
import jax.numpy as jnp
import numpy as np
from jax import lax
from jax.experimental import pallas as pl
from jax.experimental.pallas import tpu as pltpu
from jax.sharding import Mesh, PartitionSpec as P

D = 5120
EPSILON = 1e-05
EXPERTS = 16
CAP = 16
SLOTS = EXPERTS * CAP
TOK = 128
FEAT = 640
TENSOR = 8
EXTRA = 8
VMEM = 28 * 1024 * 1024
PIECES = 4
PER = TENSOR // PIECES
DOWN_PIECES = 4
TOP = D // PIECES
TENSOR_AXES = ("y", "xl")


def column_of(row):
    count = row.shape[1]
    i = lax.broadcasted_iota(jnp.int32, (count, count), 0)
    j = lax.broadcasted_iota(jnp.int32, (count, count), 1)
    return jnp.sum(jnp.where(i == j, row, 0), axis=1, keepdims=True), i, j


def dispatch_kernel(ids_ref, tokens_ref, out_ref):
    row = ids_ref[...]
    col, i, j = column_of(row)
    earlier = jnp.sum(jnp.where((col == row) & (i < j), 1, 0), axis=0, keepdims=True)
    placed = row * CAP + earlier
    slot = lax.broadcasted_iota(jnp.int32, (SLOTS, TOK), 0)
    placing = (slot == placed).astype(jnp.float32).astype(jnp.bfloat16)
    out_ref[...] = jnp.dot(
        placing, tokens_ref[...], preferred_element_type=jnp.float32
    ).astype(jnp.bfloat16)


def combine_kernel(ids_ref, back_ref, out_ref):
    row = ids_ref[...]
    col, i, j = column_of(row)
    earlier = jnp.sum(jnp.where((col == row) & (j < i), 1, 0), axis=1, keepdims=True)
    placed = col * CAP + earlier
    slot = lax.broadcasted_iota(jnp.int32, (TOK, SLOTS), 1)
    placing = (slot == placed).astype(jnp.float32).astype(jnp.bfloat16)
    out_ref[...] = jnp.dot(
        placing, back_ref[...], preferred_element_type=jnp.float32
    ).astype(jnp.bfloat16)


def gained(x_ref, k):
    rows = x_ref[k, :SLOTS, :].astype(jnp.float32)
    more = x_ref[k, SLOTS:, :].astype(jnp.float32)
    return rows, rows * (more[0:1] + more[1:2] + more[2:3]), more[3:4]


def fetched(sources, held, sems, pieces):
    depth = held.shape[1] // pieces
    copies = []
    for piece in range(pieces):
        for k, parts in enumerate(sources):
            start, index = piece * depth, 0
            while start >= parts[index].shape[0]:
                start, index = start - parts[index].shape[0], index + 1
            copies.append(
                pltpu.make_async_copy(
                    parts[index].at[pl.ds(start, depth)],
                    held.at[k, pl.ds(piece * depth, depth)],
                    sems.at[piece, k],
                )
            )
    for copy in copies:
        copy.start()
    return lambda piece: [c.wait() for c in copies[len(sources) * piece :][: len(sources)]]


def weighed(held, piece):
    depth = PER * FEAT
    return jnp.concatenate(
        [held[k, piece * depth : (piece + 1) * depth, :] for k in range(8)], axis=1
    )


def hidden_kernel(x_ref, g0, u0, g1, u1, g2, u2, v2, g3, u3, v3, out_ref, held, acc, sems):
    weights = ((g0,), (u0,), (g1,), (u1,), (g2,), (u2, v2), (g3,), (u3, v3))
    wait = fetched(weights, held, sems, PIECES)
    squares, logit = 0.0, 0.0
    for piece in range(PIECES):
        parts = []
        for k in range(PER):
            rows, values, router = gained(x_ref, piece * PER + k)
            squares += jnp.sum(rows * rows, axis=1, keepdims=True)
            logit += jnp.sum(values * router, axis=1, keepdims=True)
            parts.append(values.astype(jnp.bfloat16))
        wait(piece)
        term = jnp.dot(
            jnp.concatenate(parts, axis=1), weighed(held, piece), preferred_element_type=jnp.float32
        )
        acc[...] = term if piece == 0 else acc[...] + term
    rstd = lax.rsqrt(squares / D + EPSILON)
    scale = rstd * jax.nn.sigmoid(logit * rstd)
    for k in range(4):
        gate = acc[:, 256 * k : 256 * k + 128] * scale
        upper = acc[:, 256 * k + 128 : 256 * k + 256] * scale
        out_ref[:, 128 * k : 128 * k + 128] = (jax.nn.silu(gate) * upper).astype(jnp.bfloat16)


def down_kernel(h_ref, d0, d1, d2, d3, out_ref, held, acc, sems):
    wait = fetched(((d0,), (d1,), (d2,), (d3,)), held, sems, DOWN_PIECES)
    each = TENSOR // DOWN_PIECES
    for piece in range(DOWN_PIECES):
        places = range(piece * each, (piece + 1) * each)
        hidden = jnp.concatenate(
            [h for k in places for h in (h_ref[k, :, :256], h_ref[k ^ 1, :, 256:])], axis=1
        )
        wait(piece)
        slices = [held[w, 128 * k : 128 * k + 128, :] for k in places for w in range(4)]
        term = jnp.dot(
            hidden, jnp.concatenate(slices, axis=0), preferred_element_type=jnp.float32
        )
        if piece == 0:
            acc[...] = term
        elif piece < DOWN_PIECES - 1:
            acc[...] += term
        else:
            out_ref[...] = (acc[...] + term).astype(out_ref.dtype)


IN_VMEM = pl.BlockSpec(memory_space=pltpu.VMEM)
IN_HBM = pl.BlockSpec(memory_space=pl.ANY)
PARAMS = pltpu.CompilerParams(vmem_limit_bytes=VMEM)


def left_in_hbm(arrays):
    return [pltpu.with_memory_space_constraint(a, pltpu.HBM) for a in arrays]


def hidden_units(x, *weights):
    return pl.pallas_call(
        hidden_kernel,
        in_specs=[IN_VMEM] + [IN_HBM] * len(weights),
        out_specs=IN_VMEM,
        out_shape=jax.ShapeDtypeStruct((SLOTS, 512), jnp.bfloat16),
        scratch_shapes=[
            pltpu.VMEM((8, D, 128), jnp.bfloat16),
            pltpu.VMEM((SLOTS, 1024), jnp.float32),
            pltpu.SemaphoreType.DMA((PIECES, 8)),
        ],
        compiler_params=PARAMS,
        cost_estimate=pl.CostEstimate(
            flops=2 * SLOTS * D * 1024,
            bytes_accessed=2 * D * (1024 + SLOTS),
            transcendentals=SLOTS * 512,
        ),
    )(x, *left_in_hbm(weights))


def down_sums(hidden, *weights):
    return pl.pallas_call(
        down_kernel,
        in_specs=[IN_VMEM] + [IN_HBM] * 4,
        out_specs=IN_VMEM,
        out_shape=jax.ShapeDtypeStruct((SLOTS, FEAT), jnp.bfloat16),
        scratch_shapes=[
            pltpu.VMEM((4, 1024, FEAT), jnp.bfloat16),
            pltpu.VMEM((SLOTS, FEAT), jnp.float32),
            pltpu.SemaphoreType.DMA((DOWN_PIECES, 4)),
        ],
        compiler_params=PARAMS,
        cost_estimate=pl.CostEstimate(
            flops=2 * SLOTS * 4096 * FEAT,
            bytes_accessed=2 * 4096 * (FEAT + SLOTS),
            transcendentals=0,
        ),
    )(hidden, *left_in_hbm(weights))


def gathered(array):
    copies = jnp.broadcast_to(array[None], (TENSOR, *array.shape))
    return lax.all_to_all(copies, TENSOR_AXES, 0, 0, tiled=True)


def over_experts(array):
    parts = array.reshape(EXPERTS, CAP, FEAT)
    return lax.all_to_all(parts, "z", 0, 0, tiled=True).reshape(SLOTS, FEAT)


def other_core(array):
    return lax.ppermute(array, "co", [(0, 1), (1, 0)])


def across_border(array):
    return lax.ppermute(array, ("xh", "xl"), [(i, 3 - i) for i in range(4)])


def across_halves(array):
    return lax.ppermute(array, "xh", [(0, 1), (1, 0)])


def tied(*arrays):
    return lax.optimization_barrier(arrays)


def side_rows(norm_gain, router):
    high = norm_gain.astype(jnp.bfloat16)
    rest = norm_gain - high.astype(jnp.float32)
    middle = rest.astype(jnp.bfloat16)
    low = (rest - middle.astype(jnp.float32)).astype(jnp.bfloat16)
    mine = lax.axis_index("z") == jnp.arange(EXPERTS, dtype=jnp.int32)
    column = jnp.sum(jnp.where(mine[None, :], router.astype(jnp.float32), 0.0), axis=1)
    zero = jnp.zeros_like(high)
    return jnp.stack([high, middle, low, column.astype(jnp.bfloat16)] + [zero] * (EXTRA - 4))


def on_device(tokens, norm_gain, router, expert_ids, gate_proj, up_proj, down_proj):
    ids = expert_ids.reshape(1, TOK)
    gate, upper, down = gate_proj[0], up_proj[0], down_proj[0]

    outgoing = pl.pallas_call(
        dispatch_kernel, out_shape=jax.ShapeDtypeStruct((SLOTS, FEAT), jnp.bfloat16)
    )(ids, tokens)
    arrived = over_experts(outgoing)
    side = side_rows(norm_gain, router)

    gate_far = across_border(gate)
    top_sent, side = tied(upper[:TOP], side)
    top_far = across_border(top_sent)
    arrived, gate_far, top_far = tied(arrived, gate_far, top_far)
    rest_far = across_border(upper[TOP:])
    rest_far, down_sent = tied(rest_far, down)
    near = (other_core(gate), other_core(upper))
    last = (other_core(gate_far), other_core(top_far), other_core(rest_far))

    rows = gathered(jnp.concatenate([arrived, side], axis=0))
    hidden = hidden_units(rows, gate, upper, *near, gate_far, top_far, rest_far, *last)

    down_far = across_halves(down_sent)
    down_near, down_last = other_core(down), other_core(down_far)
    summed = down_sums(gathered(hidden), down, down_near, down_far, down_last)
    returned = over_experts(summed)
    return pl.pallas_call(
        combine_kernel, out_shape=jax.ShapeDtypeStruct((TOK, FEAT), jnp.bfloat16)
    )(ids, returned)


def solution(mesh):
    fine = Mesh(
        np.asarray(mesh.devices).reshape(2, 2, 16, 4, 2), ("xh", "co", "z", "y", "xl")
    )
    section, tensor = ("xh", "co"), ("y", "xl")
    in_specs = (
        P((*section, "z"), tensor),
        P(tensor),
        P(tensor, None),
        P((*section, "z"), None),
        P("z", None, (*section, *tensor)),
        P("z", None, (*section, *tensor)),
        P("z", section, tensor),
    )
    return jax.shard_map(
        on_device,
        mesh=fine,
        in_specs=in_specs,
        out_specs=P((*section, "z"), tensor),
        check_vma=False,
    )
```

time: 178 us -> 179 us (level)
  the two profiles are of different devices: /device:TPU:14 before, /device:TPU:64 now
where the time goes in v3:
time: 179 us; the launch traced here: 178 us
  waiting for transfers between devices  64.7 us (36%)
  starting transfers between devices  55 us (31%)
  blocking collectives  35.3 us (20%)
  Pallas kernels  13 us (7%)
  local copies, waits for them, and re-layouts  7.96 us (4%)
    all_to_all x1, blocking collectives, over_experts(): return lax.all_to_all(parts, 'z', 0, 0, tiled=True).reshape(SLOTS, FEAT)  35.3 us
    ppermute x3, waiting for transfers between devices, across_border(): return lax.ppermute(array, ('xh', 'xl'), [(i, 3 - i) for i in range(4)])  28.4 us
    all_to_all x2, waiting for transfers between devices, gathered(): return lax.all_to_all(copies, TENSOR_AXES, 0, 0, tiled=True)  19.1 us
    all_to_all x1, starting transfers between devices, over_experts(): return lax.all_to_all(parts, 'z', 0, 0, tiled=True).reshape(SLOTS, FEAT)  14.8 us
    ppermute x7, starting transfers between devices, other_core(): return lax.ppermute(array, 'co', [(0, 1), (1, 0)])  14.1 us
    ppermute x1, waiting for transfers between devices, across_halves(): return lax.ppermute(array, 'xh', [(0, 1), (1, 0)])  12.5 us
    ppermute x3, starting transfers between devices, across_border(): return lax.ppermute(array, ('xh', 'xl'), [(i, 3 - i) for i in range(4)])  12.2 us
    all_to_all x2, starting transfers between devices, gathered(): return lax.all_to_all(copies, TENSOR_AXES, 0, 0, tiled=True)  10.6 us
  transfers between devices with their start and end apart: 14, of which 7 were waited for; matrix products, arithmetic and copies ran while one was open for 3% of the time, Pallas kernels for 4%

profile of v3, /device:TPU:64, one launch (start us, length us, event | category | flops | bytes accessed | tf_op | source)
XLA Modules:
  0.0 177.8 jit_solution(7012488495146895806)
XLA Ops:
  0.0 4.7 %collective-permute-start = (bf16[5120,128]{1,0:T(8,128)(2,1)}, bf16[5120,128]{1,0:T(8,128)(2,1)S(1)}, u32[]{:S(2)}, u32[]{:S(2)}) collective-permute-start(bf16[5120,128]{1,0:T(8,128)(2,1)} %bitcast.15), channel_id=1, source_target_pairs={{0,257},{1,256},{256,1},{257,0},{2,259},{3,258},{258,3},{259,2},{4... | collective-permute-start | bytes 3932168 | tf_op jit(solution)/shard_map/ppermute | solution.py:199
  4.7 2.0 %shard_map.73 = bf16[256,640]{1,0:T(8,128)(2,1)} custom-call(s32[1,128]{1,0:T(1,128)} %bitcast.24, bf16[128,640]{1,0:T(8,128)(2,1)} %tokens_ref.1), custom_call_target="tpu_custom_call" | custom-call | tf_op jit(solution)/shard_map/pallas_call | solution.py:225
  6.7 14.8 %all-to-all-start = ((bf16[16,16,640]{2,1,0:T(8,128)(2,1)}), bf16[16,16,640]{2,1,0:T(8,128)(2,1)S(1)}, u32[]{:S(2)}, u32[]{:S(2)}) async-start(bf16[16,16,640]{2,1,0:T(8,128)(2,1)} %bitcast.19), calls=%async_computation | async-start | bytes 655360 | tf_op jit(solution)/shard_map/all_to_all | solution.py:191
  21.4 0.8 subtract_convert_fusion
  22.2 0.8 select_reduce_fusion
  23.1 1.0 slice_bitcast_fusion.1
  24.1 2.4 %collective-permute-start.1 = (bf16[1280,128]{1,0:T(8,128)(2,1)S(1)}, bf16[1280,128]{1,0:T(8,128)(2,1)S(1)}, u32[]{:S(2)}, u32[]{:S(2)}) collective-permute-start(bf16[1280,128]{1,0:T(8,128)(2,1)S(1)} %slice_bitcast_fusion.1), channel_id=1, source_target_pairs={{0,257},{1,256},{256,1},{257,0},{2,259},{3,258},{258,3},{259,2},{4... | collective-permute-start | bytes 983048 | tf_op jit(solution)/shard_map/ppermute | solution.py:199
  26.5 14.3 %collective-permute-done.1.u2 = bf16[1280,128]{1,0:T(8,128)(2,1)S(1)} collective-permute-done((bf16[1280,128]{1,0:T(8,128)(2,1)S(1)}, bf16[1280,128]{1,0:T(8,128)(2,1)S(1)}, u32[]{:S(2)}, u32[]{:S(2)}) %collective-permute-start.1) | collective-permute-done | bytes 327712 | tf_op jit(solution)/shard_map/ppermute | solution.py:199
  40.8 0.0 copy-start.8
  40.8 1.0 all-to-all-done
  41.9 0.0 collective-permute-done.g2
  41.9 0.0 copy-start.1
  41.9 1.9 %broadcast_in_dim.27 = bf16[8,264,640]{2,1,0:T(8,128)(2,1)} broadcast(bf16[264,640]{1,0:T(8,128)(2,1)S(1)} %pad_maximum_fusion), dimensions={1,2} | broadcast | bytes 3041280 | tf_op jit(solution)/shard_map/broadcast_in_dim | solution.py:185
  43.8 0.0 copy-done.1
  43.8 4.5 %all-to-all-start.1 = ((bf16[8,264,640]{2,1,0:T(8,128)(2,1)}), bf16[8,264,640]{2,1,0:T(8,128)(2,1)S(1)}, u32[]{:S(2)}, u32[]{:S(2)}) async-start(bf16[8,264,640]{2,1,0:T(8,128)(2,1)} %broadcast_in_dim.27), calls=%async_computation.1 | async-start | bytes 5406720 | tf_op jit(solution)/shard_map/all_to_all | solution.py:186
  48.3 0.0 copy-start
  48.3 1.4 slice_bitcast_fusion
  49.7 5.1 %collective-permute-start.4 = (bf16[3840,128]{1,0:T(8,128)(2,1)S(1)}, bf16[3840,128]{1,0:T(8,128)(2,1)S(1)}, u32[]{:S(2)}, u32[]{:S(2)}) collective-permute-start(bf16[3840,128]{1,0:T(8,128)(2,1)S(1)} %slice_bitcast_fusion), channel_id=1, source_target_pairs={{0,257},{1,256},{256,1},{257,0},{2,259},{3,258},{258,3},{259,2},{4... | collective-permute-start | bytes 2949128 | tf_op jit(solution)/shard_map/ppermute | solution.py:199
  54.8 1.9 %collective-permute-start.2 = (bf16[5120,128]{1,0:T(8,128)(2,1)}, bf16[5120,128]{1,0:T(8,128)(2,1)S(1)}, u32[]{:S(2)}, u32[]{:S(2)}) collective-permute-start(bf16[5120,128]{1,0:T(8,128)(2,1)} %bitcast.16), channel_id=1, source_target_pairs={{0,128},{128,0},{1,129},{129,1},{2,130},{130,2},{3,131},{131,3},{4... | collective-permute-start | bytes 3932168 | tf_op jit(solution)/shard_map/ppermute | solution.py:195
  56.7 0.0 copy-done
  56.7 2.4 %collective-permute-start.3 = (bf16[5120,128]{1,0:T(8,128)(2,1)S(1)}, bf16[5120,128]{1,0:T(8,128)(2,1)S(1)}, u32[]{:S(2)}, u32[]{:S(2)}) collective-permute-start(bf16[5120,128]{1,0:T(8,128)(2,1)S(1)} %bitcast.14), channel_id=1, source_target_pairs={{0,128},{128,0},{1,129},{129,1},{2,130},{130,2},{3,131},{131,3},{4... | collective-permute-start | bytes 3932168 | tf_op jit(solution)/shard_map/ppermute | solution.py:195
  59.1 1.9 %collective-permute-start.5 = (bf16[5120,128]{1,0:T(8,128)(2,1)}, bf16[5120,128]{1,0:T(8,128)(2,1)}, u32[]{:S(2)}, u32[]{:S(2)}) collective-permute-start(bf16[5120,128]{1,0:T(8,128)(2,1)} %copy-done.1), channel_id=1, source_target_pairs={{0,128},{128,0},{1,129},{129,1},{2,130},{130,2},{3,131},{131,3},{4... | collective-permute-start | bytes 3932168 | tf_op jit(solution)/shard_map/ppermute | solution.py:195
  61.1 14.0 %collective-permute-done.4.v2 = bf16[3840,128]{1,0:T(8,128)(2,1)S(1)} collective-permute-done((bf16[3840,128]{1,0:T(8,128)(2,1)S(1)}, bf16[3840,128]{1,0:T(8,128)(2,1)S(1)}, u32[]{:S(2)}, u32[]{:S(2)}) %collective-permute-start.4) | collective-permute-done | bytes 983072 | tf_op jit(solution)/shard_map/ppermute | solution.py:199
  75.1 0.0 copy-start.6
  75.1 1.9 %collective-permute-start.7 = (bf16[3840,128]{1,0:T(8,128)(2,1)S(1)}, bf16[3840,128]{1,0:T(8,128)(2,1)S(1)}, u32[]{:S(2)}, u32[]{:S(2)}) collective-permute-start(bf16[3840,128]{1,0:T(8,128)(2,1)S(1)} %collective-permute-done.4.v2), channel_id=1, source_target_pairs={{0,128},{128,0},{1,129},{129,1},{2,130},{130,2},{3,131},{131,3},{4... | collective-permute-start | bytes 2949128 | tf_op jit(solution)/shard_map/ppermute | solution.py:195
  77.0 3.4 %collective-permute-start.9 = (bf16[1024,640]{1,0:T(8,128)(2,1)}, bf16[1024,640]{1,0:T(8,128)(2,1)}, u32[]{:S(2)}, u32[]{:S(2)}) collective-permute-start(bf16[1024,640]{1,0:T(8,128)(2,1)} %bitcast.21), channel_id=1, source_target_pairs={{0,256},{256,0},{1,257},{257,1},{2,258},{258,2},{3,259},{259,3},{4... | collective-permute-start | bytes 3932168 | tf_op jit(solution)/shard_map/ppermute | solution.py:203
  80.4 0.0 collective-permute-done.2.g1
  80.4 0.0 copy-done.8
  80.4 0.0 copy-start.2
  80.4 2.1 %collective-permute-start.6 = (bf16[1280,128]{1,0:T(8,128)(2,1)S(1)}, bf16[1280,128]{1,0:T(8,128)(2,1)S(1)}, u32[]{:S(2)}, u32[]{:S(2)}) collective-permute-start(bf16[1280,128]{1,0:T(8,128)(2,1)S(1)} %collective-permute-done.1.u2), channel_id=1, source_target_pairs={{0,128},{128,0},{1,129},{129,1},{2,130},{130,2},{3,131},{131,3},{4... | collective-permute-start | bytes 983048 | tf_op jit(solution)/shard_map/ppermute | solution.py:195
  82.6 0.0 collective-permute-done.3.u1
  82.6 0.0 copy-start.3
  82.6 1.4 collective-permute-done.6.u3
  84.0 0.0 copy-start.9
  84.0 0.0 collective-permute-done.7.v3
  84.0 0.0 copy-done.6
  84.0 0.0 copy-done.2
  84.0 0.0 copy-done.3
  84.0 0.0 copy-start.7
  84.0 1.0 copy-done.7
  85.0 0.0 collective-permute-done.5.g3
  85.0 0.0 all-to-all-done.1.x_ref
  85.0 0.0 copy-done.9
  85.0 5.1 %shard_map.74 = bf16[256,512]{1,0:T(8,128)(2,1)S(1)} custom-call(bf16[8,264,640]{2,1,0:T(8,128)(2,1)S(1)} %all-to-all-done.1.x_ref, bf16[5120,128]{1,0:T(8,128)(2,1)} %bitcast.17, bf16[5120,128]{1,0:T(8,128)(2,1)} %bitcast.13, bf16[5120,128]{1,0:T(8,128)(2,1)} %copy-done.2, bf16[5120,128]{1,0:T(8,128)(2,1)} %copy-done.3, bf16[5120,128]{1,0:T(8,128)(2,1)} %copy-done.1, ...), custom_call_target="tpu_custom_call" | custom-call | flops 2684354560 | bytes 13107200 | tf_op jit(solution)/shard_map/pallas_call | solution.py:145
  90.2 1.5 broadcast_in_dim.28
  91.7 0.0 copy-start.4
  91.7 6.2 %all-to-all-start.2 = ((bf16[8,256,512]{2,1,0:T(8,128)(2,1)}), bf16[8,256,512]{2,1,0:T(8,128)(2,1)S(1)}, u32[]{:S(2)}, u32[]{:S(2)}) async-start(bf16[8,256,512]{2,1,0:T(8,128)(2,1)} %broadcast_in_dim.28), calls=%async_computation.2 | async-start | bytes 4194304 | tf_op jit(solution)/shard_map/all_to_all | solution.py:186
  97.8 0.0 copy-done.4
  97.8 1.9 %collective-permute-start.8 = (bf16[1024,640]{1,0:T(8,128)(2,1)S(1)}, bf16[1024,640]{1,0:T(8,128)(2,1)S(1)}, u32[]{:S(2)}, u32[]{:S(2)}) collective-permute-start(bf16[1024,640]{1,0:T(8,128)(2,1)S(1)} %bitcast.23), channel_id=1, source_target_pairs={{0,128},{128,0},{1,129},{129,1},{2,130},{130,2},{3,131},{131,3},{4... | collective-permute-start | bytes 3932168 | tf_op jit(solution)/shard_map/ppermute | solution.py:195
  99.8 12.5 %collective-permute-done.9.d2 = bf16[1024,640]{1,0:T(8,128)(2,1)} collective-permute-done((bf16[1024,640]{1,0:T(8,128)(2,1)}, bf16[1024,640]{1,0:T(8,128)(2,1)}, u32[]{:S(2)}, u32[]{:S(2)}) %collective-permute-start.9) | collective-permute-done | bytes 1310752 | tf_op jit(solution)/shard_map/ppermute | solution.py:203
  112.3 1.9 %collective-permute-start.10 = (bf16[1024,640]{1,0:T(8,128)(2,1)}, bf16[1024,640]{1,0:T(8,128)(2,1)}, u32[]{:S(2)}, u32[]{:S(2)}) collective-permute-start(bf16[1024,640]{1,0:T(8,128)(2,1)} %collective-permute-done.9.d2), channel_id=1, source_target_pairs={{0,128},{128,0},{1,129},{129,1},{2,130},{130,2},{3,131},{131,3},{4... | collective-permute-start | bytes 3932168 | tf_op jit(solution)/shard_map/ppermute | solution.py:195
  114.2 0.0 collective-permute-done.8.d1
  114.2 0.0 copy-start.5
  114.3 1.1 copy-done.5
  115.3 2.2 %collective-permute-done.10.d3 = bf16[1024,640]{1,0:T(8,128)(2,1)} collective-permute-done((bf16[1024,640]{1,0:T(8,128)(2,1)}, bf16[1024,640]{1,0:T(8,128)(2,1)}, u32[]{:S(2)}, u32[]{:S(2)}) %collective-permute-start.10) | collective-permute-done | bytes 1310752 | tf_op jit(solution)/shard_map/ppermute | solution.py:195
  117.6 19.1 %all-to-all-done.2.h_ref = bf16[8,256,512]{2,1,0:T(8,128)(2,1)S(1)} async-done(((bf16[8,256,512]{2,1,0:T(8,128)(2,1)}), bf16[8,256,512]{2,1,0:T(8,128)(2,1)S(1)}, u32[]{:S(2)}, u32[]{:S(2)}) %all-to-all-start.2) | async-done | bytes 2097184 | tf_op jit(solution)/shard_map/all_to_all | solution.py:186
  136.7 3.8 %shard_map.75 = bf16[256,640]{1,0:T(8,128)(2,1)S(1)} custom-call(bf16[8,256,512]{2,1,0:T(8,128)(2,1)S(1)} %all-to-all-done.2.h_ref, bf16[1024,640]{1,0:T(8,128)(2,1)} %bitcast.22, bf16[1024,640]{1,0:T(8,128)(2,1)} %copy-done.5, bf16[1024,640]{1,0:T(8,128)(2,1)} %collective-permute-done.9.d2, bf16[1024,640]{1,0:T(8,128)(2,1)} %collective-permute-done.10.d3), custom_call_target="tpu_custom_call" | custom-call | flops 1342177280 | bytes 7340032 | tf_op jit(solution)/shard_map/pallas_call | solution.py:165
  140.5 35.3 %all_to_all.20 = bf16[16,16,640]{2,1,0:T(8,128)(2,1)} all-to-all(bf16[16,16,640]{2,1,0:T(8,128)(2,1)S(1)} %bitcast.12), channel_id=1, replica_groups=mesh['xh'=2,'co'=2,'z'=16,'y'=4,'xl'=2] {'z'}, dimensions={0} | all-to-all | bytes 655360 | tf_op jit(solution)/shard_map/all_to_all | solution.py:191
  175.8 2.0 %shard_map.76 = bf16[128,640]{1,0:T(8,128)(2,1)} custom-call(s32[1,128]{1,0:T(1,128)} %bitcast.25, bf16[256,640]{1,0:T(8,128)(2,1)} %bitcast.20), custom_call_target="tpu_custom_call" | custom-call | tf_op jit(solution)/shard_map/pallas_call | solution.py:247
  (8 shorter events, 0.1 us)
Async XLA Ops:
  0.0 41.9 %collective-permute-start = (bf16[5120,128]{1,0:T(8,128)(2,1)}, bf16[5120,128]{1,0:T(8,128)(2,1)S(1)}, u32[]{:S(2)}, u32[]{:S(2)}) collective-permute-start(bf16[5120,128]{1,0:T(8,128)(2,1)} %bitcast.15), channel_id=1, source_target_pairs={{0,257},{1,256},{256,1},{257,0},{2,259},{3,258},{258,3},{259,2},{4... | collective-permute-start | bytes 3932168 | tf_op jit(solution)/shard_map/ppermute | solution.py:199
  6.7 35.2 %all-to-all-start = ((bf16[16,16,640]{2,1,0:T(8,128)(2,1)}), bf16[16,16,640]{2,1,0:T(8,128)(2,1)S(1)}, u32[]{:S(2)}, u32[]{:S(2)}) async-start(bf16[16,16,640]{2,1,0:T(8,128)(2,1)} %bitcast.19), calls=%async_computation | async-start | bytes 655360 | tf_op jit(solution)/shard_map/all_to_all | solution.py:191
  24.1 16.7 %collective-permute-start.1 = (bf16[1280,128]{1,0:T(8,128)(2,1)S(1)}, bf16[1280,128]{1,0:T(8,128)(2,1)S(1)}, u32[]{:S(2)}, u32[]{:S(2)}) collective-permute-start(bf16[1280,128]{1,0:T(8,128)(2,1)S(1)} %slice_bitcast_fusion.1), channel_id=1, source_target_pairs={{0,257},{1,256},{256,1},{257,0},{2,259},{3,258},{258,3},{259,2},{4... | collective-permute-start | bytes 983048 | tf_op jit(solution)/shard_map/ppermute | solution.py:199
  40.8 39.6 %copy-start.8 = (bf16[1280,128]{1,0:T(8,128)(2,1)}, bf16[1280,128]{1,0:T(8,128)(2,1)S(1)}, u32[]{:S(2)}) copy-start(bf16[1280,128]{1,0:T(8,128)(2,1)S(1)} %collective-permute-done.1.u2) | copy-start | bytes 983044
  41.9 1.9 %copy-start.1 = (bf16[5120,128]{1,0:T(8,128)(2,1)}, bf16[5120,128]{1,0:T(8,128)(2,1)S(1)}, u32[]{:S(2)}) copy-start(bf16[5120,128]{1,0:T(8,128)(2,1)S(1)} %collective-permute-done.g2) | copy-start | bytes 3932164
  43.8 41.2 %all-to-all-start.1 = ((bf16[8,264,640]{2,1,0:T(8,128)(2,1)}), bf16[8,264,640]{2,1,0:T(8,128)(2,1)S(1)}, u32[]{:S(2)}, u32[]{:S(2)}) async-start(bf16[8,264,640]{2,1,0:T(8,128)(2,1)} %broadcast_in_dim.27), calls=%async_computation.1 | async-start | bytes 5406720 | tf_op jit(solution)/shard_map/all_to_all | solution.py:186
  48.3 8.4 %copy-start = (bf16[1,5120,128]{2,1,0:T(8,128)(2,1)S(1)}, bf16[1,5120,128]{2,1,0:T(8,128)(2,1)}, u32[]{:S(2)}) copy-start(bf16[1,5120,128]{2,1,0:T(8,128)(2,1)} %param.12) | copy-start | bytes 3932164
  49.7 25.4 %collective-permute-start.4 = (bf16[3840,128]{1,0:T(8,128)(2,1)S(1)}, bf16[3840,128]{1,0:T(8,128)(2,1)S(1)}, u32[]{:S(2)}, u32[]{:S(2)}) collective-permute-start(bf16[3840,128]{1,0:T(8,128)(2,1)S(1)} %slice_bitcast_fusion), channel_id=1, source_target_pairs={{0,257},{1,256},{256,1},{257,0},{2,259},{3,258},{258,3},{259,2},{4... | collective-permute-start | bytes 2949128 | tf_op jit(solution)/shard_map/ppermute | solution.py:199
  54.8 25.6 %collective-permute-start.2 = (bf16[5120,128]{1,0:T(8,128)(2,1)}, bf16[5120,128]{1,0:T(8,128)(2,1)S(1)}, u32[]{:S(2)}, u32[]{:S(2)}) collective-permute-start(bf16[5120,128]{1,0:T(8,128)(2,1)} %bitcast.16), channel_id=1, source_target_pairs={{0,128},{128,0},{1,129},{129,1},{2,130},{130,2},{3,131},{131,3},{4... | collective-permute-start | bytes 3932168 | tf_op jit(solution)/shard_map/ppermute | solution.py:195
  56.7 25.8 %collective-permute-start.3 = (bf16[5120,128]{1,0:T(8,128)(2,1)S(1)}, bf16[5120,128]{1,0:T(8,128)(2,1)S(1)}, u32[]{:S(2)}, u32[]{:S(2)}) collective-permute-start(bf16[5120,128]{1,0:T(8,128)(2,1)S(1)} %bitcast.14), channel_id=1, source_target_pairs={{0,128},{128,0},{1,129},{129,1},{2,130},{130,2},{3,131},{131,3},{4... | collective-permute-start | bytes 3932168 | tf_op jit(solution)/shard_map/ppermute | solution.py:195
  59.1 25.8 %collective-permute-start.5 = (bf16[5120,128]{1,0:T(8,128)(2,1)}, bf16[5120,128]{1,0:T(8,128)(2,1)}, u32[]{:S(2)}, u32[]{:S(2)}) collective-permute-start(bf16[5120,128]{1,0:T(8,128)(2,1)} %copy-done.1), channel_id=1, source_target_pairs={{0,128},{128,0},{1,129},{129,1},{2,130},{130,2},{3,131},{131,3},{4... | collective-permute-start | bytes 3932168 | tf_op jit(solution)/shard_map/ppermute | solution.py:195
  75.1 8.9 %copy-start.6 = (bf16[3840,128]{1,0:T(8,128)(2,1)}, bf16[3840,128]{1,0:T(8,128)(2,1)S(1)}, u32[]{:S(2)}) copy-start(bf16[3840,128]{1,0:T(8,128)(2,1)S(1)} %collective-permute-done.4.v2) | copy-start | bytes 2949124
  75.1 8.9 %collective-permute-start.7 = (bf16[3840,128]{1,0:T(8,128)(2,1)S(1)}, bf16[3840,128]{1,0:T(8,128)(2,1)S(1)}, u32[]{:S(2)}, u32[]{:S(2)}) collective-permute-start(bf16[3840,128]{1,0:T(8,128)(2,1)S(1)} %collective-permute-done.4.v2), channel_id=1, source_target_pairs={{0,128},{128,0},{1,129},{129,1},{2,130},{130,2},{3,131},{131,3},{4... | collective-permute-start | bytes 2949128 | tf_op jit(solution)/shard_map/ppermute | solution.py:195
  77.0 35.3 %collective-permute-start.9 = (bf16[1024,640]{1,0:T(8,128)(2,1)}, bf16[1024,640]{1,0:T(8,128)(2,1)}, u32[]{:S(2)}, u32[]{:S(2)}) collective-permute-start(bf16[1024,640]{1,0:T(8,128)(2,1)} %bitcast.21), channel_id=1, source_target_pairs={{0,256},{256,0},{1,257},{257,1},{2,258},{258,2},{3,259},{259,3},{4... | collective-permute-start | bytes 3932168 | tf_op jit(solution)/shard_map/ppermute | solution.py:203
  80.4 3.5 %copy-start.2 = (bf16[5120,128]{1,0:T(8,128)(2,1)}, bf16[5120,128]{1,0:T(8,128)(2,1)S(1)}, u32[]{:S(2)}) copy-start(bf16[5120,128]{1,0:T(8,128)(2,1)S(1)} %collective-permute-done.2.g1) | copy-start | bytes 3932164
  80.4 3.5 %collective-permute-start.6 = (bf16[1280,128]{1,0:T(8,128)(2,1)S(1)}, bf16[1280,128]{1,0:T(8,128)(2,1)S(1)}, u32[]{:S(2)}, u32[]{:S(2)}) collective-permute-start(bf16[1280,128]{1,0:T(8,128)(2,1)S(1)} %collective-permute-done.1.u2), channel_id=1, source_target_pairs={{0,128},{128,0},{1,129},{129,1},{2,130},{130,2},{3,131},{131,3},{4... | collective-permute-start | bytes 983048 | tf_op jit(solution)/shard_map/ppermute | solution.py:195
  82.6 1.4 copy-start.3
  84.0 1.1 copy-start.9
  84.0 1.0 copy-start.7
  91.7 6.2 %copy-start.4 = (bf16[1,1024,640]{2,1,0:T(8,128)(2,1)S(1)}, bf16[1,1024,640]{2,1,0:T(8,128)(2,1)}, u32[]{:S(2)}) copy-start(bf16[1,1024,640]{2,1,0:T(8,128)(2,1)} %param.13) | copy-start | bytes 3932164
  91.7 45.0 %all-to-all-start.2 = ((bf16[8,256,512]{2,1,0:T(8,128)(2,1)}), bf16[8,256,512]{2,1,0:T(8,128)(2,1)S(1)}, u32[]{:S(2)}, u32[]{:S(2)}) async-start(bf16[8,256,512]{2,1,0:T(8,128)(2,1)} %broadcast_in_dim.28), calls=%async_computation.2 | async-start | bytes 4194304 | tf_op jit(solution)/shard_map/all_to_all | solution.py:186
  97.8 16.4 %collective-permute-start.8 = (bf16[1024,640]{1,0:T(8,128)(2,1)S(1)}, bf16[1024,640]{1,0:T(8,128)(2,1)S(1)}, u32[]{:S(2)}, u32[]{:S(2)}) collective-permute-start(bf16[1024,640]{1,0:T(8,128)(2,1)S(1)} %bitcast.23), channel_id=1, source_target_pairs={{0,128},{128,0},{1,129},{129,1},{2,130},{130,2},{3,131},{131,3},{4... | collective-permute-start | bytes 3932168 | tf_op jit(solution)/shard_map/ppermute | solution.py:195
  112.3 5.3 %collective-permute-start.10 = (bf16[1024,640]{1,0:T(8,128)(2,1)}, bf16[1024,640]{1,0:T(8,128)(2,1)}, u32[]{:S(2)}, u32[]{:S(2)}) collective-permute-start(bf16[1024,640]{1,0:T(8,128)(2,1)} %collective-permute-done.9.d2), channel_id=1, source_target_pairs={{0,128},{128,0},{1,129},{129,1},{2,130},{130,2},{3,131},{131,3},{4... | collective-permute-start | bytes 3932168 | tf_op jit(solution)/shard_map/ppermute | solution.py:195
  114.2 1.1 copy-start.5

commit v4 on v3

--- a/solution.py
+++ b/solution.py
@@ -19,7 +19,6 @@
 PIECES = 4
 PER = TENSOR // PIECES
 DOWN_PIECES = 4
-TOP = D // PIECES
 TENSOR_AXES = ("y", "xl")
 
 
@@ -30,7 +29,13 @@
     return jnp.sum(jnp.where(i == j, row, 0), axis=1, keepdims=True), i, j
 
 
-def dispatch_kernel(ids_ref, tokens_ref, out_ref):
+def dispatch_kernel(ids_ref, tokens_ref, gate_ref, upper_ref, out_ref, own_ref, sems):
+    copies = [
+        pltpu.make_async_copy(ref, own_ref.at[k], sems.at[k])
+        for k, ref in enumerate((gate_ref, upper_ref))
+    ]
+    for copy in copies:
+        copy.start()
     row = ids_ref[...]
     col, i, j = column_of(row)
     earlier = jnp.sum(jnp.where((col == row) & (i < j), 1, 0), axis=0, keepdims=True)
@@ -40,6 +45,8 @@
     out_ref[...] = jnp.dot(
         placing, tokens_ref[...], preferred_element_type=jnp.float32
     ).astype(jnp.bfloat16)
+    for copy in copies:
+        copy.wait()
 
 
 def combine_kernel(ids_ref, back_ref, out_ref):
@@ -64,16 +71,10 @@
     depth = held.shape[1] // pieces
     copies = []
     for piece in range(pieces):
-        for k, parts in enumerate(sources):
-            start, index = piece * depth, 0
-            while start >= parts[index].shape[0]:
-                start, index = start - parts[index].shape[0], index + 1
+        part = pl.ds(piece * depth, depth)
+        for k, source in enumerate(sources):
             copies.append(
-                pltpu.make_async_copy(
-                    parts[index].at[pl.ds(start, depth)],
-                    held.at[k, pl.ds(piece * depth, depth)],
-                    sems.at[piece, k],
-                )
+                pltpu.make_async_copy(source.at[part], held.at[k, part], sems.at[piece, k])
             )
     for copy in copies:
         copy.start()
@@ -87,8 +88,9 @@
     )
 
 
-def hidden_kernel(x_ref, g0, u0, g1, u1, g2, u2, v2, g3, u3, v3, out_ref, held, acc, sems):
-    weights = ((g0,), (u0,), (g1,), (u1,), (g2,), (u2, v2), (g3,), (u3, v3))
+def hidden_kernel(x_ref, own, near, far, *rest):
+    *last, out_ref, held, acc, sems = rest
+    weights = [pair.at[k] for pair in (own, near, far) for k in range(2)] + last
     wait = fetched(weights, held, sems, PIECES)
     squares, logit = 0.0, 0.0
     for piece in range(PIECES):
@@ -112,7 +114,7 @@
 
 
 def down_kernel(h_ref, d0, d1, d2, d3, out_ref, held, acc, sems):
-    wait = fetched(((d0,), (d1,), (d2,), (d3,)), held, sems, DOWN_PIECES)
+    wait = fetched((d0, d1, d2, d3), held, sems, DOWN_PIECES)
     each = TENSOR // DOWN_PIECES
     for piece in range(DOWN_PIECES):
         places = range(piece * each, (piece + 1) * each)
@@ -141,6 +143,19 @@
     return [pltpu.with_memory_space_constraint(a, pltpu.HBM) for a in arrays]
 
 
+def dispatched(ids, tokens, gate, upper):
+    return pl.pallas_call(
+        dispatch_kernel,
+        in_specs=[IN_VMEM, IN_VMEM, IN_HBM, IN_HBM],
+        out_specs=[IN_VMEM, IN_HBM],
+        out_shape=[
+            jax.ShapeDtypeStruct((SLOTS, FEAT), jnp.bfloat16),
+            jax.ShapeDtypeStruct((2, D, 128), jnp.bfloat16),
+        ],
+        scratch_shapes=[pltpu.SemaphoreType.DMA((2,))],
+    )(ids, tokens, *left_in_hbm((gate, upper)))
+
+
 def hidden_units(x, *weights):
     return pl.pallas_call(
         hidden_kernel,
@@ -222,23 +237,16 @@
     ids = expert_ids.reshape(1, TOK)
     gate, upper, down = gate_proj[0], up_proj[0], down_proj[0]
 
-    outgoing = pl.pallas_call(
-        dispatch_kernel, out_shape=jax.ShapeDtypeStruct((SLOTS, FEAT), jnp.bfloat16)
-    )(ids, tokens)
-    arrived = over_experts(outgoing)
+    outgoing, own = dispatched(ids, tokens, gate, upper)
+    arrived, token = tied(over_experts(outgoing), ids)
     side = side_rows(norm_gain, router)
 
-    gate_far = across_border(gate)
-    top_sent, side = tied(upper[:TOP], side)
-    top_far = across_border(top_sent)
-    arrived, gate_far, top_far = tied(arrived, gate_far, top_far)
-    rest_far = across_border(upper[TOP:])
-    rest_far, down_sent = tied(rest_far, down)
-    near = (other_core(gate), other_core(upper))
-    last = (other_core(gate_far), other_core(top_far), other_core(rest_far))
+    near = other_core(own)
+    far, down_sent, token = tied(across_border(own), down, token)
+    last = [other_core(far[k]) for k in range(2)]
 
     rows = gathered(jnp.concatenate([arrived, side], axis=0))
-    hidden = hidden_units(rows, gate, upper, *near, gate_far, top_far, rest_far, *last)
+    hidden = hidden_units(rows, own, near, far, *last)
 
     down_far = across_halves(down_sent)
     down_near, down_last = other_core(down), other_core(down_far)
@@ -246,7 +254,7 @@
     returned = over_experts(summed)
     return pl.pallas_call(
         combine_kernel, out_shape=jax.ShapeDtypeStruct((TOK, FEAT), jnp.bfloat16)
-    )(ids, returned)
+    )(token, returned)
 
 
 def solution(mesh):

time: 179 us -> 253 us (1.41)
  Pallas kernels: 13 us -> 93.2 us
  starting transfers between devices: 55 us -> 41.3 us
  waiting for transfers between devices: 64.7 us -> 75.3 us
    pallas_call x1, Pallas kernels: 2 us -> 82.2 us  [dispatched(): pl.pallas_call(dispatch_kernel, in_specs=[IN_VMEM, IN_VMEM, IN_HBM, IN_HB...]
    all_to_all x1, waiting for transfers between devices: 1.03 us -> 18.3 us  [over_experts(): return lax.all_to_all(parts, 'z', 0, 0, tiled=True).reshape(SLOTS, FEAT)]
    ppermute x3 -> x1, waiting for transfers between devices: 28.4 us -> 15.6 us  [across_border(): return lax.ppermute(array, ('xh', 'xl'), [(i, 3 - i) for i in range(4)])]
    ppermute x3 -> x1, starting transfers between devices: 12.2 us -> 4.67 us  [across_border(): return lax.ppermute(array, ('xh', 'xl'), [(i, 3 - i) for i in range(4)])]
    ppermute x1, waiting for transfers between devices: 12.5 us -> 17.3 us  [across_halves(): return lax.ppermute(array, 'xh', [(0, 1), (1, 0)])]
    ppermute x7 -> x5, starting transfers between devices: 14.1 us -> 10.1 us  [other_core(): return lax.ppermute(array, 'co', [(0, 1), (1, 0)])]
    squeeze x0 -> x1, local copies, waits for them, and re-layouts: none -> 3.33 us  [on_device(): last = [other_core(far[k]) for k in range(2)]]
    all_to_all x2, starting transfers between devices: 10.6 us -> 8.07 us  [gathered(): return lax.all_to_all(copies, TENSOR_AXES, 0, 0, tiled=True)]
  transfers between devices with their start and end apart: 14 -> 10, of which waited for: 7 -> 6; matrix products, arithmetic and copies ran while one was open for 3% -> 3% of each run, Pallas kernels for 4% -> 2%
where the time goes in v4:
time: 253 us; the launch traced here: 252 us
  Pallas kernels  93.2 us (37%)
  waiting for transfers between devices  75.3 us (30%)
  starting transfers between devices  41.3 us (16%)
  blocking collectives  34.9 us (14%)
  local copies, waits for them, and re-layouts  6.96 us (3%)
    pallas_call x1, Pallas kernels, dispatched(): pl.pallas_call(dispatch_kernel, in_specs=[IN_VMEM, IN_VMEM, IN_HBM, IN_HB...  82.2 us
    all_to_all x1, blocking collectives, over_experts(): return lax.all_to_all(parts, 'z', 0, 0, tiled=True).reshape(SLOTS, FEAT)  34.9 us
    all_to_all x2, waiting for transfers between devices, gathered(): return lax.all_to_all(copies, TENSOR_AXES, 0, 0, tiled=True)  20.8 us
    all_to_all x1, waiting for transfers between devices, over_experts(): return lax.all_to_all(parts, 'z', 0, 0, tiled=True).reshape(SLOTS, FEAT)  18.3 us
    ppermute x1, waiting for transfers between devices, across_halves(): return lax.ppermute(array, 'xh', [(0, 1), (1, 0)])  17.3 us
    ppermute x1, waiting for transfers between devices, across_border(): return lax.ppermute(array, ('xh', 'xl'), [(i, 3 - i) for i in range(4)])  15.6 us
    all_to_all x1, starting transfers between devices, over_experts(): return lax.all_to_all(parts, 'z', 0, 0, tiled=True).reshape(SLOTS, FEAT)  14.8 us
    ppermute x5, starting transfers between devices, other_core(): return lax.ppermute(array, 'co', [(0, 1), (1, 0)])  10.1 us
  transfers between devices with their start and end apart: 10, of which 6 were waited for; matrix products, arithmetic and copies ran while one was open for 3% of the time, Pallas kernels for 2%

profile of v4, /device:TPU:64, one launch (start us, length us, event | category | flops | bytes accessed | tf_op | source)
XLA Modules:
  0.0 251.9 jit_solution(7728753453289603394)
XLA Ops:
  0.0 0.0 copy-start.2
  0.0 0.0 copy-start.1
  0.0 82.2 %shard_map.73 = (bf16[256,640]{1,0:T(8,128)(2,1)}, bf16[2,5120,128]{2,1,0:T(8,128)(2,1)}) custom-call(s32[1,128]{1,0:T(1,128)} %bitcast.18, bf16[128,640]{1,0:T(8,128)(2,1)} %tokens_ref.1, bf16[5120,128]{1,0:T(8,128)(2,1)} %bitcast.13, bf16[5120,128]{1,0:T(8,128)(2,1)} %bitcast.14), custom_call_target="tpu_custom_call" | custom-call | tf_op jit(solution)/shard_map/pallas_call | solution.py:147
  82.2 4.7 %collective-permute-start = (bf16[2,5120,128]{2,1,0:T(8,128)(2,1)}, bf16[2,5120,128]{2,1,0:T(8,128)(2,1)}, u32[]{:S(2)}, u32[]{:S(2)}) collective-permute-start(bf16[2,5120,128]{2,1,0:T(8,128)(2,1)} %get-tuple-element.12.own), channel_id=1, source_target_pairs={{0,257},{1,256},{256,1},{257,0},{2,259},{3,258},{258,3},{259,2},{4... | collective-permute-start | bytes 7864328 | tf_op jit(solution)/shard_map/ppermute | solution.py:214
  86.9 14.8 %all-to-all-start = ((bf16[16,16,640]{2,1,0:T(8,128)(2,1)}), bf16[16,16,640]{2,1,0:T(8,128)(2,1)S(1)}, u32[]{:S(2)}, u32[]{:S(2)}) async-start(bf16[16,16,640]{2,1,0:T(8,128)(2,1)} %bitcast.17), calls=%async_computation | async-start | bytes 655360 | tf_op jit(solution)/shard_map/all_to_all | solution.py:206
  101.7 1.9 collective-permute-start.1
  103.6 0.0 copy-done.2
  103.7 0.0 copy-done.1
  103.7 0.1 select_reduce_fusion
  103.8 18.3 %all-to-all-done = bf16[16,16,640]{2,1,0:T(8,128)(2,1)S(1)} async-done(((bf16[16,16,640]{2,1,0:T(8,128)(2,1)}), bf16[16,16,640]{2,1,0:T(8,128)(2,1)S(1)}, u32[]{:S(2)}, u32[]{:S(2)}) %all-to-all-start) | async-done | bytes 327712 | tf_op jit(solution)/shard_map/all_to_all | solution.py:206
  122.1 0.3 concatenate.7
  122.5 1.7 broadcast_in_dim.27
  124.2 4.5 %all-to-all-start.1 = ((bf16[8,264,640]{2,1,0:T(8,128)(2,1)}), bf16[8,264,640]{2,1,0:T(8,128)(2,1)S(1)}, u32[]{:S(2)}, u32[]{:S(2)}) async-start(bf16[8,264,640]{2,1,0:T(8,128)(2,1)} %broadcast_in_dim.27), calls=%async_computation.1 | async-start | bytes 5406720 | tf_op jit(solution)/shard_map/all_to_all | solution.py:201
  128.7 15.6 %collective-permute-done.far = bf16[2,5120,128]{2,1,0:T(8,128)(2,1)} collective-permute-done((bf16[2,5120,128]{2,1,0:T(8,128)(2,1)}, bf16[2,5120,128]{2,1,0:T(8,128)(2,1)}, u32[]{:S(2)}, u32[]{:S(2)}) %collective-permute-start) | collective-permute-done | bytes 2621472 | tf_op jit(solution)/shard_map/ppermute | solution.py:214
  144.2 3.3 %slice_bitcast_fusion = (bf16[5120,128]{1,0:T(8,128)(2,1)}, bf16[5120,128]{1,0:T(8,128)(2,1)}) fusion(bf16[2,5120,128]{2,1,0:T(8,128)(2,1)} %collective-permute-done.far), kind=kLoop, calls=%fused_computation | loop fusion | bytes 5242880 | tf_op jit(solution)/shard_map/squeeze | solution.py:246
  147.6 1.9 collective-permute-start.2
  149.5 2.4 collective-permute-start.3
  151.9 3.7 %collective-permute-start.5 = (bf16[1024,640]{1,0:T(8,128)(2,1)}, bf16[1024,640]{1,0:T(8,128)(2,1)}, u32[]{:S(2)}, u32[]{:S(2)}) collective-permute-start(bf16[1024,640]{1,0:T(8,128)(2,1)} %bitcast.3.d0), channel_id=1, source_target_pairs={{0,256},{256,0},{1,257},{257,1},{2,258},{258,2},{3,259},{259,3},{4... | collective-permute-start | bytes 3932168 | tf_op jit(solution)/shard_map/ppermute | solution.py:218
  155.6 0.0 collective-permute-done.1.near
  155.7 2.2 all-to-all-done.1.x_ref
  157.8 0.0 collective-permute-done.2.rest_0_
  157.8 0.0 collective-permute-done.3.rest_1_
  157.8 5.1 %shard_map.74 = bf16[256,512]{1,0:T(8,128)(2,1)S(1)} custom-call(bf16[8,264,640]{2,1,0:T(8,128)(2,1)S(1)} %all-to-all-done.1.x_ref, bf16[2,5120,128]{2,1,0:T(8,128)(2,1)} %get-tuple-element.12.own, bf16[2,5120,128]{2,1,0:T(8,128)(2,1)} %collective-permute-done.1.near, bf16[2,5120,128]{2,1,0:T(8,128)(2,1)} %collective-permute-done.far, ...), custom_call_target="tpu_custom_call" | custom-call | flops 2684354560 | bytes 13107200 | tf_op jit(solution)/shard_map/pallas_call | solution.py:160
  163.0 1.5 broadcast_in_dim.28
  164.5 3.6 %all-to-all-start.2 = ((bf16[8,256,512]{2,1,0:T(8,128)(2,1)}), bf16[8,256,512]{2,1,0:T(8,128)(2,1)S(1)}, u32[]{:S(2)}, u32[]{:S(2)}) async-start(bf16[8,256,512]{2,1,0:T(8,128)(2,1)} %broadcast_in_dim.28), calls=%async_computation.2 | async-start | bytes 4194304 | tf_op jit(solution)/shard_map/all_to_all | solution.py:201
  168.1 1.9 collective-permute-start.4
  170.0 17.3 %collective-permute-done.5.d2 = bf16[1024,640]{1,0:T(8,128)(2,1)} collective-permute-done((bf16[1024,640]{1,0:T(8,128)(2,1)}, bf16[1024,640]{1,0:T(8,128)(2,1)}, u32[]{:S(2)}, u32[]{:S(2)}) %collective-permute-start.5) | collective-permute-done | bytes 1310752 | tf_op jit(solution)/shard_map/ppermute | solution.py:218
  187.3 1.9 collective-permute-start.6
  189.2 0.0 collective-permute-done.4.d1
  189.2 0.0 copy-start
  189.2 3.3 %collective-permute-done.6.d3 = bf16[1024,640]{1,0:T(8,128)(2,1)} collective-permute-done((bf16[1024,640]{1,0:T(8,128)(2,1)}, bf16[1024,640]{1,0:T(8,128)(2,1)}, u32[]{:S(2)}, u32[]{:S(2)}) %collective-permute-start.6) | collective-permute-done | bytes 1310752 | tf_op jit(solution)/shard_map/ppermute | solution.py:210
  192.5 18.7 %all-to-all-done.2.h_ref = bf16[8,256,512]{2,1,0:T(8,128)(2,1)S(1)} async-done(((bf16[8,256,512]{2,1,0:T(8,128)(2,1)}), bf16[8,256,512]{2,1,0:T(8,128)(2,1)S(1)}, u32[]{:S(2)}, u32[]{:S(2)}) %all-to-all-start.2) | async-done | bytes 2097184 | tf_op jit(solution)/shard_map/all_to_all | solution.py:201
  211.2 0.0 copy-done
  211.2 3.8 %shard_map.75 = bf16[256,640]{1,0:T(8,128)(2,1)S(1)} custom-call(bf16[8,256,512]{2,1,0:T(8,128)(2,1)S(1)} %all-to-all-done.2.h_ref, bf16[1024,640]{1,0:T(8,128)(2,1)} %bitcast.3.d0, bf16[1024,640]{1,0:T(8,128)(2,1)} %copy-done, bf16[1024,640]{1,0:T(8,128)(2,1)} %collective-permute-done.5.d2, bf16[1024,640]{1,0:T(8,128)(2,1)} %collective-permute-done.6.d3), custom_call_target="tpu_custom_call" | custom-call | flops 1342177280 | bytes 7340032 | tf_op jit(solution)/shard_map/pallas_call | solution.py:180
  215.1 34.9 %all_to_all.20 = bf16[16,16,640]{2,1,0:T(8,128)(2,1)} all-to-all(bf16[16,16,640]{2,1,0:T(8,128)(2,1)S(1)} %bitcast.12), channel_id=1, replica_groups=mesh['xh'=2,'co'=2,'z'=16,'y'=4,'xl'=2] {'z'}, dimensions={0} | all-to-all | bytes 655360 | tf_op jit(solution)/shard_map/all_to_all | solution.py:206
  249.9 2.0 shard_map.76
  (7 shorter events, 0.0 us)
Async XLA Ops:
  0.0 103.6 %copy-start.2 = (f32[640]{0:T(1024)S(1)}, f32[640]{0:T(1024)}, u32[]{:S(2)}) copy-start(f32[640]{0:T(1024)} %param.8) | copy-start | bytes 7684
  0.0 103.7 %copy-start.1 = (bf16[640,16]{0,1:T(8,128)(2,1)S(1)}, bf16[640,16]{0,1:T(8,128)(2,1)}, u32[]{:S(2)}) copy-start(bf16[640,16]{0,1:T(8,128)(2,1)} %param.9) | copy-start | bytes 61444
  82.2 62.0 %collective-permute-start = (bf16[2,5120,128]{2,1,0:T(8,128)(2,1)}, bf16[2,5120,128]{2,1,0:T(8,128)(2,1)}, u32[]{:S(2)}, u32[]{:S(2)}) collective-permute-start(bf16[2,5120,128]{2,1,0:T(8,128)(2,1)} %get-tuple-element.12.own), channel_id=1, source_target_pairs={{0,257},{1,256},{256,1},{257,0},{2,259},{3,258},{258,3},{259,2},{4... | collective-permute-start | bytes 7864328 | tf_op jit(solution)/shard_map/ppermute | solution.py:214
  86.9 35.2 %all-to-all-start = ((bf16[16,16,640]{2,1,0:T(8,128)(2,1)}), bf16[16,16,640]{2,1,0:T(8,128)(2,1)S(1)}, u32[]{:S(2)}, u32[]{:S(2)}) async-start(bf16[16,16,640]{2,1,0:T(8,128)(2,1)} %bitcast.17), calls=%async_computation | async-start | bytes 655360 | tf_op jit(solution)/shard_map/all_to_all | solution.py:206
  101.7 54.0 %collective-permute-start.1 = (bf16[2,5120,128]{2,1,0:T(8,128)(2,1)}, bf16[2,5120,128]{2,1,0:T(8,128)(2,1)}, u32[]{:S(2)}, u32[]{:S(2)}) collective-permute-start(bf16[2,5120,128]{2,1,0:T(8,128)(2,1)} %get-tuple-element.12.own), channel_id=1, source_target_pairs={{0,128},{128,0},{1,129},{129,1},{2,130},{130,2},{3,131},{131,3},{4... | collective-permute-start | bytes 7864328 | tf_op jit(solution)/shard_map/ppermute | solution.py:210
  124.2 33.6 %all-to-all-start.1 = ((bf16[8,264,640]{2,1,0:T(8,128)(2,1)}), bf16[8,264,640]{2,1,0:T(8,128)(2,1)S(1)}, u32[]{:S(2)}, u32[]{:S(2)}) async-start(bf16[8,264,640]{2,1,0:T(8,128)(2,1)} %broadcast_in_dim.27), calls=%async_computation.1 | async-start | bytes 5406720 | tf_op jit(solution)/shard_map/all_to_all | solution.py:201
  147.6 10.2 %collective-permute-start.2 = (bf16[5120,128]{1,0:T(8,128)(2,1)}, bf16[5120,128]{1,0:T(8,128)(2,1)}, u32[]{:S(2)}, u32[]{:S(2)}) collective-permute-start(bf16[5120,128]{1,0:T(8,128)(2,1)} %get-tuple-element.20), channel_id=1, source_target_pairs={{0,128},{128,0},{1,129},{129,1},{2,130},{130,2},{3,131},{131,3},{4... | collective-permute-start | bytes 3932168 | tf_op jit(solution)/shard_map/ppermute | solution.py:210
  149.5 8.3 %collective-permute-start.3 = (bf16[5120,128]{1,0:T(8,128)(2,1)}, bf16[5120,128]{1,0:T(8,128)(2,1)}, u32[]{:S(2)}, u32[]{:S(2)}) collective-permute-start(bf16[5120,128]{1,0:T(8,128)(2,1)} %get-tuple-element.19), channel_id=1, source_target_pairs={{0,128},{128,0},{1,129},{129,1},{2,130},{130,2},{3,131},{131,3},{4... | collective-permute-start | bytes 3932168 | tf_op jit(solution)/shard_map/ppermute | solution.py:210
  151.9 35.4 %collective-permute-start.5 = (bf16[1024,640]{1,0:T(8,128)(2,1)}, bf16[1024,640]{1,0:T(8,128)(2,1)}, u32[]{:S(2)}, u32[]{:S(2)}) collective-permute-start(bf16[1024,640]{1,0:T(8,128)(2,1)} %bitcast.3.d0), channel_id=1, source_target_pairs={{0,256},{256,0},{1,257},{257,1},{2,258},{258,2},{3,259},{259,3},{4... | collective-permute-start | bytes 3932168 | tf_op jit(solution)/shard_map/ppermute | solution.py:218
  164.5 46.7 %all-to-all-start.2 = ((bf16[8,256,512]{2,1,0:T(8,128)(2,1)}), bf16[8,256,512]{2,1,0:T(8,128)(2,1)S(1)}, u32[]{:S(2)}, u32[]{:S(2)}) async-start(bf16[8,256,512]{2,1,0:T(8,128)(2,1)} %broadcast_in_dim.28), calls=%async_computation.2 | async-start | bytes 4194304 | tf_op jit(solution)/shard_map/all_to_all | solution.py:201
  168.1 21.1 %collective-permute-start.4 = (bf16[1024,640]{1,0:T(8,128)(2,1)}, bf16[1024,640]{1,0:T(8,128)(2,1)S(1)}, u32[]{:S(2)}, u32[]{:S(2)}) collective-permute-start(bf16[1024,640]{1,0:T(8,128)(2,1)} %bitcast.3.d0), channel_id=1, source_target_pairs={{0,128},{128,0},{1,129},{129,1},{2,130},{130,2},{3,131},{131,3},{4... | collective-permute-start | bytes 3932168 | tf_op jit(solution)/shard_map/ppermute | solution.py:210
  187.3 5.3 %collective-permute-start.6 = (bf16[1024,640]{1,0:T(8,128)(2,1)}, bf16[1024,640]{1,0:T(8,128)(2,1)}, u32[]{:S(2)}, u32[]{:S(2)}) collective-permute-start(bf16[1024,640]{1,0:T(8,128)(2,1)} %collective-permute-done.5.d2), channel_id=1, source_target_pairs={{0,128},{128,0},{1,129},{129,1},{2,130},{130,2},{3,131},{131,3},{4... | collective-permute-start | bytes 3932168 | tf_op jit(solution)/shard_map/ppermute | solution.py:210
  189.2 22.0 %copy-start = (bf16[1024,640]{1,0:T(8,128)(2,1)}, bf16[1024,640]{1,0:T(8,128)(2,1)S(1)}, u32[]{:S(2)}) copy-start(bf16[1024,640]{1,0:T(8,128)(2,1)S(1)} %collective-permute-done.4.d1) | copy-start | bytes 3932164

commit v5 on v4

--- a/solution.py
+++ b/solution.py
@@ -17,6 +17,7 @@
 EXTRA = 8
 VMEM = 28 * 1024 * 1024
 PIECES = 4
+STAGES = 4
 PER = TENSOR // PIECES
 DOWN_PIECES = 4
 TENSOR_AXES = ("y", "xl")
@@ -29,12 +30,19 @@
     return jnp.sum(jnp.where(i == j, row, 0), axis=1, keepdims=True), i, j
 
 
-def dispatch_kernel(ids_ref, tokens_ref, gate_ref, upper_ref, out_ref, own_ref, sems):
-    copies = [
-        pltpu.make_async_copy(ref, own_ref.at[k], sems.at[k])
-        for k, ref in enumerate((gate_ref, upper_ref))
-    ]
-    for copy in copies:
+def dispatch_kernel(ids_ref, tokens_ref, gate_ref, upper_ref, out_ref, own_ref, held, sems):
+    depth = D // STAGES
+    inward, outward = [], []
+    for stage in range(STAGES):
+        part = pl.ds(stage * depth, depth)
+        for k, ref in enumerate((gate_ref, upper_ref)):
+            inward.append(
+                pltpu.make_async_copy(ref.at[part], held.at[k, part], sems.at[0, stage, k])
+            )
+            outward.append(
+                pltpu.make_async_copy(held.at[k, part], own_ref.at[k, part], sems.at[1, stage, k])
+            )
+    for copy in inward:
         copy.start()
     row = ids_ref[...]
     col, i, j = column_of(row)
@@ -42,10 +50,13 @@
     placed = row * CAP + earlier
     slot = lax.broadcasted_iota(jnp.int32, (SLOTS, TOK), 0)
     placing = (slot == placed).astype(jnp.float32).astype(jnp.bfloat16)
+    for first, second in zip(inward, outward):
+        first.wait()
+        second.start()
     out_ref[...] = jnp.dot(
         placing, tokens_ref[...], preferred_element_type=jnp.float32
     ).astype(jnp.bfloat16)
-    for copy in copies:
+    for copy in outward:
         copy.wait()
 
 
@@ -152,7 +163,10 @@
             jax.ShapeDtypeStruct((SLOTS, FEAT), jnp.bfloat16),
             jax.ShapeDtypeStruct((2, D, 128), jnp.bfloat16),
         ],
-        scratch_shapes=[pltpu.SemaphoreType.DMA((2,))],
+        scratch_shapes=[
+            pltpu.VMEM((2, D, 128), jnp.bfloat16),
+            pltpu.SemaphoreType.DMA((2, STAGES, 2)),
+        ],
     )(ids, tokens, *left_in_hbm((gate, upper)))
 
 
@@ -214,8 +228,8 @@
     return lax.ppermute(array, ("xh", "xl"), [(i, 3 - i) for i in range(4)])
 
 
-def across_halves(array):
-    return lax.ppermute(array, "xh", [(0, 1), (1, 0)])
+def across_pair(array):
+    return lax.ppermute(array, "xl", [(0, 1), (1, 0)])
 
 
 def tied(*arrays):
@@ -238,17 +252,17 @@
     gate, upper, down = gate_proj[0], up_proj[0], down_proj[0]
 
     outgoing, own = dispatched(ids, tokens, gate, upper)
-    arrived, token = tied(over_experts(outgoing), ids)
+    arrived, down_sent, token = tied(over_experts(outgoing), across_pair(down), ids)
     side = side_rows(norm_gain, router)
 
     near = other_core(own)
-    far, down_sent, token = tied(across_border(own), down, token)
+    far, down_sent, token = tied(across_border(own), down_sent, token)
     last = [other_core(far[k]) for k in range(2)]
 
     rows = gathered(jnp.concatenate([arrived, side], axis=0))
     hidden = hidden_units(rows, own, near, far, *last)
 
-    down_far = across_halves(down_sent)
+    down_far = across_border(down_sent)
     down_near, down_last = other_core(down), other_core(down_far)
     summed = down_sums(gathered(hidden), down, down_near, down_far, down_last)
     returned = over_experts(summed)

time: 253 us -> 159 us (0.63)
  the two profiles are of different devices: /device:TPU:64 before, /device:TPU:4 now
where the time goes in v5:
time: 159 us; the launch traced here: 158 us
  waiting for transfers between devices  56.9 us (36%)
  starting transfers between devices  41.7 us (26%)
  blocking collectives  35.5 us (22%)
  Pallas kernels  15.4 us (10%)
  local copies, waits for them, and re-layouts  8.09 us (5%)
    all_to_all x1, blocking collectives, over_experts(): return lax.all_to_all(parts, 'z', 0, 0, tiled=True).reshape(SLOTS, FEAT)  35.5 us
    ppermute x2, waiting for transfers between devices, across_border(): return lax.ppermute(array, ('xh', 'xl'), [(i, 3 - i) for i in range(4)])  27.2 us
    all_to_all x1, waiting for transfers between devices, over_experts(): return lax.all_to_all(parts, 'z', 0, 0, tiled=True).reshape(SLOTS, FEAT)  18.3 us
    ppermute x5, starting transfers between devices, other_core(): return lax.ppermute(array, 'co', [(0, 1), (1, 0)])  10.1 us
    all_to_all x1, starting transfers between devices, over_experts(): return lax.all_to_all(parts, 'z', 0, 0, tiled=True).reshape(SLOTS, FEAT)  9.84 us
    all_to_all x2, waiting for transfers between devices, gathered(): return lax.all_to_all(copies, TENSOR_AXES, 0, 0, tiled=True)  9.06 us
    all_to_all x2, starting transfers between devices, gathered(): return lax.all_to_all(copies, TENSOR_AXES, 0, 0, tiled=True)  8.53 us
    ppermute x1, starting transfers between devices, across_pair(): return lax.ppermute(array, 'xl', [(0, 1), (1, 0)])  8.42 us
  transfers between devices with their start and end apart: 11, of which 6 were waited for; matrix products, arithmetic and copies ran while one was open for 5% of the time, Pallas kernels for 3%

profile of v5, /device:TPU:4, one launch (start us, length us, event | category | flops | bytes accessed | tf_op | source)
XLA Modules:
  0.0 158.0 jit_solution(457223671288665129)
XLA Ops:
  0.0 0.0 copy-start
  0.0 0.0 copy-start.4
  0.0 0.0 copy-start.3
  0.0 4.4 %shard_map.73 = (bf16[256,640]{1,0:T(8,128)(2,1)}, bf16[2,5120,128]{2,1,0:T(8,128)(2,1)}) custom-call(s32[1,128]{1,0:T(1,128)} %bitcast.21, bf16[128,640]{1,0:T(8,128)(2,1)} %tokens_ref.1, bf16[5120,128]{1,0:T(8,128)(2,1)} %bitcast.13, bf16[5120,128]{1,0:T(8,128)(2,1)} %bitcast.14), custom_call_target="tpu_custom_call" | custom-call | tf_op jit(solution)/shard_map/pallas_call | solution.py:158
  4.5 2.4 %collective-permute-start = (bf16[2,5120,128]{2,1,0:T(8,128)(2,1)}, bf16[2,5120,128]{2,1,0:T(8,128)(2,1)}, u32[]{:S(2)}, u32[]{:S(2)}) collective-permute-start(bf16[2,5120,128]{2,1,0:T(8,128)(2,1)} %get-tuple-element.13.own), channel_id=1, source_target_pairs={{0,257},{1,256},{256,1},{257,0},{2,259},{3,258},{258,3},{259,2},{4... | collective-permute-start | bytes 7864328 | tf_op jit(solution)/shard_map/ppermute | solution.py:228
  6.9 0.0 copy-done
  6.9 8.4 %collective-permute-start.1 = (bf16[1024,640]{1,0:T(8,128)(2,1)S(1)}, bf16[1024,640]{1,0:T(8,128)(2,1)}, u32[]{:S(2)}, u32[]{:S(2)}) collective-permute-start(bf16[1024,640]{1,0:T(8,128)(2,1)S(1)} %bitcast.18), channel_id=1, source_target_pairs={{0,1},{1,0},{2,3},{3,2},{4,5},{5,4},{6,7},{7,6},{8,9},{9,8},{10,11... | collective-permute-start | bytes 3932168 | tf_op jit(solution)/shard_map/ppermute | solution.py:232
  15.3 9.8 %all-to-all-start = ((bf16[16,16,640]{2,1,0:T(8,128)(2,1)}), bf16[16,16,640]{2,1,0:T(8,128)(2,1)S(1)}, u32[]{:S(2)}, u32[]{:S(2)}) async-start(bf16[16,16,640]{2,1,0:T(8,128)(2,1)} %bitcast.20), calls=%async_computation | async-start | bytes 655360 | tf_op jit(solution)/shard_map/all_to_all | solution.py:220
  25.2 1.9 %collective-permute-start.2 = (bf16[2,5120,128]{2,1,0:T(8,128)(2,1)}, bf16[2,5120,128]{2,1,0:T(8,128)(2,1)}, u32[]{:S(2)}, u32[]{:S(2)}) collective-permute-start(bf16[2,5120,128]{2,1,0:T(8,128)(2,1)} %get-tuple-element.13.own), channel_id=1, source_target_pairs={{0,128},{128,0},{1,129},{129,1},{2,130},{130,2},{3,131},{131,3},{4... | collective-permute-start | bytes 7864328 | tf_op jit(solution)/shard_map/ppermute | solution.py:224
  27.1 0.0 copy-done.4
  27.2 0.0 copy-done.3
  27.2 0.1 select_reduce_fusion
  27.3 18.3 %all-to-all-done = bf16[16,16,640]{2,1,0:T(8,128)(2,1)S(1)} async-done(((bf16[16,16,640]{2,1,0:T(8,128)(2,1)}), bf16[16,16,640]{2,1,0:T(8,128)(2,1)S(1)}, u32[]{:S(2)}, u32[]{:S(2)}) %all-to-all-start) | async-done | bytes 327712 | tf_op jit(solution)/shard_map/all_to_all | solution.py:220
  45.6 0.0 collective-permute-done.1
  45.6 0.4 concatenate.7
  46.0 1.7 %broadcast_in_dim.27 = bf16[8,264,640]{2,1,0:T(8,128)(2,1)} broadcast(bf16[264,640]{1,0:T(8,128)(2,1)S(1)} %concatenate.7), dimensions={1,2} | broadcast | bytes 3041280 | tf_op jit(solution)/shard_map/broadcast_in_dim | solution.py:214
  47.7 4.8 %all-to-all-start.1 = ((bf16[8,264,640]{2,1,0:T(8,128)(2,1)}), bf16[8,264,640]{2,1,0:T(8,128)(2,1)S(1)}, u32[]{:S(2)}, u32[]{:S(2)}) async-start(bf16[8,264,640]{2,1,0:T(8,128)(2,1)} %broadcast_in_dim.27), calls=%async_computation.1 | async-start | bytes 5406720 | tf_op jit(solution)/shard_map/all_to_all | solution.py:215
  52.5 12.8 %collective-permute-done.far = bf16[2,5120,128]{2,1,0:T(8,128)(2,1)} collective-permute-done((bf16[2,5120,128]{2,1,0:T(8,128)(2,1)}, bf16[2,5120,128]{2,1,0:T(8,128)(2,1)}, u32[]{:S(2)}, u32[]{:S(2)}) %collective-permute-start) | collective-permute-done | bytes 2621472 | tf_op jit(solution)/shard_map/ppermute | solution.py:228
  65.3 3.4 %slice_bitcast_fusion = (bf16[5120,128]{1,0:T(8,128)(2,1)}, bf16[5120,128]{1,0:T(8,128)(2,1)}) fusion(bf16[2,5120,128]{2,1,0:T(8,128)(2,1)} %collective-permute-done.far), kind=kLoop, calls=%fused_computation | loop fusion | bytes 5242880 | tf_op jit(solution)/shard_map/squeeze | solution.py:260
  68.6 1.9 %collective-permute-start.3 = (bf16[5120,128]{1,0:T(8,128)(2,1)}, bf16[5120,128]{1,0:T(8,128)(2,1)}, u32[]{:S(2)}, u32[]{:S(2)}) collective-permute-start(bf16[5120,128]{1,0:T(8,128)(2,1)} %get-tuple-element.22), channel_id=1, source_target_pairs={{0,128},{128,0},{1,129},{129,1},{2,130},{130,2},{3,131},{131,3},{4... | collective-permute-start | bytes 3932168 | tf_op jit(solution)/shard_map/ppermute | solution.py:224
  70.5 2.4 %collective-permute-start.4 = (bf16[5120,128]{1,0:T(8,128)(2,1)}, bf16[5120,128]{1,0:T(8,128)(2,1)}, u32[]{:S(2)}, u32[]{:S(2)}) collective-permute-start(bf16[5120,128]{1,0:T(8,128)(2,1)} %get-tuple-element.21), channel_id=1, source_target_pairs={{0,128},{128,0},{1,129},{129,1},{2,130},{130,2},{3,131},{131,3},{4... | collective-permute-start | bytes 3932168 | tf_op jit(solution)/shard_map/ppermute | solution.py:224
  73.0 2.4 %collective-permute-start.6 = (bf16[1024,640]{1,0:T(8,128)(2,1)}, bf16[1024,640]{1,0:T(8,128)(2,1)}, u32[]{:S(2)}, u32[]{:S(2)}) collective-permute-start(bf16[1024,640]{1,0:T(8,128)(2,1)} %collective-permute-done.1), channel_id=1, source_target_pairs={{0,257},{1,256},{256,1},{257,0},{2,259},{3,258},{258,3},{259,2},{4... | collective-permute-start | bytes 3932168 | tf_op jit(solution)/shard_map/ppermute | solution.py:228
  75.4 0.0 collective-permute-done.2.near
  75.4 3.6 %all-to-all-done.1.x_ref = bf16[8,264,640]{2,1,0:T(8,128)(2,1)S(1)} async-done(((bf16[8,264,640]{2,1,0:T(8,128)(2,1)}), bf16[8,264,640]{2,1,0:T(8,128)(2,1)S(1)}, u32[]{:S(2)}, u32[]{:S(2)}) %all-to-all-start.1) | async-done | bytes 2703392 | tf_op jit(solution)/shard_map/all_to_all | solution.py:215
  79.0 0.0 collective-permute-done.3.rest_0_
  79.0 0.0 collective-permute-done.4.rest_1_
  79.0 5.1 %shard_map.74 = bf16[256,512]{1,0:T(8,128)(2,1)S(1)} custom-call(bf16[8,264,640]{2,1,0:T(8,128)(2,1)S(1)} %all-to-all-done.1.x_ref, bf16[2,5120,128]{2,1,0:T(8,128)(2,1)} %get-tuple-element.13.own, bf16[2,5120,128]{2,1,0:T(8,128)(2,1)} %collective-permute-done.2.near, bf16[2,5120,128]{2,1,0:T(8,128)(2,1)} %collective-permute-done.far, ...), custom_call_target="tpu_custom_call" | custom-call | flops 2684354560 | bytes 13107200 | tf_op jit(solution)/shard_map/pallas_call | solution.py:174
  84.2 1.5 broadcast_in_dim.28
  85.7 0.0 copy-start.1
  85.7 3.7 %all-to-all-start.2 = ((bf16[8,256,512]{2,1,0:T(8,128)(2,1)}), bf16[8,256,512]{2,1,0:T(8,128)(2,1)S(1)}, u32[]{:S(2)}, u32[]{:S(2)}) async-start(bf16[8,256,512]{2,1,0:T(8,128)(2,1)} %broadcast_in_dim.28), calls=%async_computation.2 | async-start | bytes 4194304 | tf_op jit(solution)/shard_map/all_to_all | solution.py:215
  89.5 0.0 copy-done.1
  89.5 1.9 %collective-permute-start.5 = (bf16[1024,640]{1,0:T(8,128)(2,1)S(1)}, bf16[1024,640]{1,0:T(8,128)(2,1)S(1)}, u32[]{:S(2)}, u32[]{:S(2)}) collective-permute-start(bf16[1024,640]{1,0:T(8,128)(2,1)S(1)} %bitcast.19), channel_id=1, source_target_pairs={{0,128},{128,0},{1,129},{129,1},{2,130},{130,2},{3,131},{131,3},{4... | collective-permute-start | bytes 3932168 | tf_op jit(solution)/shard_map/ppermute | solution.py:224
  91.4 14.5 %collective-permute-done.6.d2 = bf16[1024,640]{1,0:T(8,128)(2,1)} collective-permute-done((bf16[1024,640]{1,0:T(8,128)(2,1)}, bf16[1024,640]{1,0:T(8,128)(2,1)}, u32[]{:S(2)}, u32[]{:S(2)}) %collective-permute-start.6) | collective-permute-done | bytes 1310752 | tf_op jit(solution)/shard_map/ppermute | solution.py:228
  105.9 1.9 %collective-permute-start.7 = (bf16[1024,640]{1,0:T(8,128)(2,1)}, bf16[1024,640]{1,0:T(8,128)(2,1)}, u32[]{:S(2)}, u32[]{:S(2)}) collective-permute-start(bf16[1024,640]{1,0:T(8,128)(2,1)} %collective-permute-done.6.d2), channel_id=1, source_target_pairs={{0,128},{128,0},{1,129},{129,1},{2,130},{130,2},{3,131},{131,3},{4... | collective-permute-start | bytes 3932168 | tf_op jit(solution)/shard_map/ppermute | solution.py:224
  107.8 0.0 collective-permute-done.5.d1
  107.8 0.0 copy-start.2
  107.8 1.1 copy-done.2
  108.9 2.3 %collective-permute-done.7.d3 = bf16[1024,640]{1,0:T(8,128)(2,1)} collective-permute-done((bf16[1024,640]{1,0:T(8,128)(2,1)}, bf16[1024,640]{1,0:T(8,128)(2,1)}, u32[]{:S(2)}, u32[]{:S(2)}) %collective-permute-start.7) | collective-permute-done | bytes 1310752 | tf_op jit(solution)/shard_map/ppermute | solution.py:224
  111.1 5.5 %all-to-all-done.2.h_ref = bf16[8,256,512]{2,1,0:T(8,128)(2,1)S(1)} async-done(((bf16[8,256,512]{2,1,0:T(8,128)(2,1)}), bf16[8,256,512]{2,1,0:T(8,128)(2,1)S(1)}, u32[]{:S(2)}, u32[]{:S(2)}) %all-to-all-start.2) | async-done | bytes 2097184 | tf_op jit(solution)/shard_map/all_to_all | solution.py:215
  116.6 3.8 %shard_map.75 = bf16[256,640]{1,0:T(8,128)(2,1)S(1)} custom-call(bf16[8,256,512]{2,1,0:T(8,128)(2,1)S(1)} %all-to-all-done.2.h_ref, bf16[1024,640]{1,0:T(8,128)(2,1)} %bitcast.17, bf16[1024,640]{1,0:T(8,128)(2,1)} %copy-done.2, bf16[1024,640]{1,0:T(8,128)(2,1)} %collective-permute-done.6.d2, bf16[1024,640]{1,0:T(8,128)(2,1)} %collective-permute-done.7.d3), custom_call_target="tpu_custom_call" | custom-call | flops 1342177280 | bytes 7340032 | tf_op jit(solution)/shard_map/pallas_call | solution.py:194
  120.4 35.5 %all_to_all.20 = bf16[16,16,640]{2,1,0:T(8,128)(2,1)} all-to-all(bf16[16,16,640]{2,1,0:T(8,128)(2,1)S(1)} %bitcast.12), channel_id=1, replica_groups=mesh['xh'=2,'co'=2,'z'=16,'y'=4,'xl'=2] {'z'}, dimensions={0} | all-to-all | bytes 655360 | tf_op jit(solution)/shard_map/all_to_all | solution.py:220
  156.0 2.0 %shard_map.76 = bf16[128,640]{1,0:T(8,128)(2,1)} custom-call(s32[1,128]{1,0:T(1,128)} %bitcast.22, bf16[256,640]{1,0:T(8,128)(2,1)} %bitcast.16), custom_call_target="tpu_custom_call" | custom-call | tf_op jit(solution)/shard_map/pallas_call | solution.py:269
  (7 shorter events, 0.0 us)
Async XLA Ops:
  0.0 6.9 %copy-start = (bf16[1,1024,640]{2,1,0:T(8,128)(2,1)S(1)}, bf16[1,1024,640]{2,1,0:T(8,128)(2,1)}, u32[]{:S(2)}) copy-start(bf16[1,1024,640]{2,1,0:T(8,128)(2,1)} %param.13) | copy-start | bytes 3932164
  0.0 27.1 %copy-start.4 = (f32[640]{0:T(1024)S(1)}, f32[640]{0:T(1024)}, u32[]{:S(2)}) copy-start(f32[640]{0:T(1024)} %param.8) | copy-start | bytes 7684
  0.0 27.2 %copy-start.3 = (bf16[640,16]{0,1:T(8,128)(2,1)S(1)}, bf16[640,16]{0,1:T(8,128)(2,1)}, u32[]{:S(2)}) copy-start(bf16[640,16]{0,1:T(8,128)(2,1)} %param.9) | copy-start | bytes 61444
  4.5 60.8 %collective-permute-start = (bf16[2,5120,128]{2,1,0:T(8,128)(2,1)}, bf16[2,5120,128]{2,1,0:T(8,128)(2,1)}, u32[]{:S(2)}, u32[]{:S(2)}) collective-permute-start(bf16[2,5120,128]{2,1,0:T(8,128)(2,1)} %get-tuple-element.13.own), channel_id=1, source_target_pairs={{0,257},{1,256},{256,1},{257,0},{2,259},{3,258},{258,3},{259,2},{4... | collective-permute-start | bytes 7864328 | tf_op jit(solution)/shard_map/ppermute | solution.py:228
  6.9 38.7 %collective-permute-start.1 = (bf16[1024,640]{1,0:T(8,128)(2,1)S(1)}, bf16[1024,640]{1,0:T(8,128)(2,1)}, u32[]{:S(2)}, u32[]{:S(2)}) collective-permute-start(bf16[1024,640]{1,0:T(8,128)(2,1)S(1)} %bitcast.18), channel_id=1, source_target_pairs={{0,1},{1,0},{2,3},{3,2},{4,5},{5,4},{6,7},{7,6},{8,9},{9,8},{10,11... | collective-permute-start | bytes 3932168 | tf_op jit(solution)/shard_map/ppermute | solution.py:232
  15.3 30.3 %all-to-all-start = ((bf16[16,16,640]{2,1,0:T(8,128)(2,1)}), bf16[16,16,640]{2,1,0:T(8,128)(2,1)S(1)}, u32[]{:S(2)}, u32[]{:S(2)}) async-start(bf16[16,16,640]{2,1,0:T(8,128)(2,1)} %bitcast.20), calls=%async_computation | async-start | bytes 655360 | tf_op jit(solution)/shard_map/all_to_all | solution.py:220
  25.2 50.2 %collective-permute-start.2 = (bf16[2,5120,128]{2,1,0:T(8,128)(2,1)}, bf16[2,5120,128]{2,1,0:T(8,128)(2,1)}, u32[]{:S(2)}, u32[]{:S(2)}) collective-permute-start(bf16[2,5120,128]{2,1,0:T(8,128)(2,1)} %get-tuple-element.13.own), channel_id=1, source_target_pairs={{0,128},{128,0},{1,129},{129,1},{2,130},{130,2},{3,131},{131,3},{4... | collective-permute-start | bytes 7864328 | tf_op jit(solution)/shard_map/ppermute | solution.py:224
  47.7 31.3 %all-to-all-start.1 = ((bf16[8,264,640]{2,1,0:T(8,128)(2,1)}), bf16[8,264,640]{2,1,0:T(8,128)(2,1)S(1)}, u32[]{:S(2)}, u32[]{:S(2)}) async-start(bf16[8,264,640]{2,1,0:T(8,128)(2,1)} %broadcast_in_dim.27), calls=%async_computation.1 | async-start | bytes 5406720 | tf_op jit(solution)/shard_map/all_to_all | solution.py:215
  68.6 10.4 %collective-permute-start.3 = (bf16[5120,128]{1,0:T(8,128)(2,1)}, bf16[5120,128]{1,0:T(8,128)(2,1)}, u32[]{:S(2)}, u32[]{:S(2)}) collective-permute-start(bf16[5120,128]{1,0:T(8,128)(2,1)} %get-tuple-element.22), channel_id=1, source_target_pairs={{0,128},{128,0},{1,129},{129,1},{2,130},{130,2},{3,131},{131,3},{4... | collective-permute-start | bytes 3932168 | tf_op jit(solution)/shard_map/ppermute | solution.py:224
  70.5 8.5 %collective-permute-start.4 = (bf16[5120,128]{1,0:T(8,128)(2,1)}, bf16[5120,128]{1,0:T(8,128)(2,1)}, u32[]{:S(2)}, u32[]{:S(2)}) collective-permute-start(bf16[5120,128]{1,0:T(8,128)(2,1)} %get-tuple-element.21), channel_id=1, source_target_pairs={{0,128},{128,0},{1,129},{129,1},{2,130},{130,2},{3,131},{131,3},{4... | collective-permute-start | bytes 3932168 | tf_op jit(solution)/shard_map/ppermute | solution.py:224
  73.0 32.9 %collective-permute-start.6 = (bf16[1024,640]{1,0:T(8,128)(2,1)}, bf16[1024,640]{1,0:T(8,128)(2,1)}, u32[]{:S(2)}, u32[]{:S(2)}) collective-permute-start(bf16[1024,640]{1,0:T(8,128)(2,1)} %collective-permute-done.1), channel_id=1, source_target_pairs={{0,257},{1,256},{256,1},{257,0},{2,259},{3,258},{258,3},{259,2},{4... | collective-permute-start | bytes 3932168 | tf_op jit(solution)/shard_map/ppermute | solution.py:228
  85.7 3.7 %copy-start.1 = (bf16[1,1024,640]{2,1,0:T(8,128)(2,1)S(1)}, bf16[1,1024,640]{2,1,0:T(8,128)(2,1)}, u32[]{:S(2)}) copy-start(bf16[1,1024,640]{2,1,0:T(8,128)(2,1)} %param.13) | copy-start | bytes 3932164
  85.7 30.9 %all-to-all-start.2 = ((bf16[8,256,512]{2,1,0:T(8,128)(2,1)}), bf16[8,256,512]{2,1,0:T(8,128)(2,1)S(1)}, u32[]{:S(2)}, u32[]{:S(2)}) async-start(bf16[8,256,512]{2,1,0:T(8,128)(2,1)} %broadcast_in_dim.28), calls=%async_computation.2 | async-start | bytes 4194304 | tf_op jit(solution)/shard_map/all_to_all | solution.py:215
  89.5 18.3 %collective-permute-start.5 = (bf16[1024,640]{1,0:T(8,128)(2,1)S(1)}, bf16[1024,640]{1,0:T(8,128)(2,1)S(1)}, u32[]{:S(2)}, u32[]{:S(2)}) collective-permute-start(bf16[1024,640]{1,0:T(8,128)(2,1)S(1)} %bitcast.19), channel_id=1, source_target_pairs={{0,128},{128,0},{1,129},{129,1},{2,130},{130,2},{3,131},{131,3},{4... | collective-permute-start | bytes 3932168 | tf_op jit(solution)/shard_map/ppermute | solution.py:224
  105.9 5.3 %collective-permute-start.7 = (bf16[1024,640]{1,0:T(8,128)(2,1)}, bf16[1024,640]{1,0:T(8,128)(2,1)}, u32[]{:S(2)}, u32[]{:S(2)}) collective-permute-start(bf16[1024,640]{1,0:T(8,128)(2,1)} %collective-permute-done.6.d2), channel_id=1, source_target_pairs={{0,128},{128,0},{1,129},{129,1},{2,130},{130,2},{3,131},{131,3},{4... | collective-permute-start | bytes 3932168 | tf_op jit(solution)/shard_map/ppermute | solution.py:224
  107.8 1.1 copy-start.2

commit v6 on v3

--- a/solution.py
+++ b/solution.py
@@ -19,7 +19,6 @@
 PIECES = 4
 PER = TENSOR // PIECES
 DOWN_PIECES = 4
-TOP = D // PIECES
 TENSOR_AXES = ("y", "xl")
 
 
@@ -64,16 +63,10 @@
     depth = held.shape[1] // pieces
     copies = []
     for piece in range(pieces):
-        for k, parts in enumerate(sources):
-            start, index = piece * depth, 0
-            while start >= parts[index].shape[0]:
-                start, index = start - parts[index].shape[0], index + 1
+        part = pl.ds(piece * depth, depth)
+        for k, source in enumerate(sources):
             copies.append(
-                pltpu.make_async_copy(
-                    parts[index].at[pl.ds(start, depth)],
-                    held.at[k, pl.ds(piece * depth, depth)],
-                    sems.at[piece, k],
-                )
+                pltpu.make_async_copy(source.at[part], held.at[k, part], sems.at[piece, k])
             )
     for copy in copies:
         copy.start()
@@ -87,8 +80,8 @@
     )
 
 
-def hidden_kernel(x_ref, g0, u0, g1, u1, g2, u2, v2, g3, u3, v3, out_ref, held, acc, sems):
-    weights = ((g0,), (u0,), (g1,), (u1,), (g2,), (u2, v2), (g3,), (u3, v3))
+def hidden_kernel(x_ref, *rest):
+    *weights, out_ref, held, acc, made, sems, out_sems = rest
     wait = fetched(weights, held, sems, PIECES)
     squares, logit = 0.0, 0.0
     for piece in range(PIECES):
@@ -108,11 +101,18 @@
     for k in range(4):
         gate = acc[:, 256 * k : 256 * k + 128] * scale
         upper = acc[:, 256 * k + 128 : 256 * k + 256] * scale
-        out_ref[:, 128 * k : 128 * k + 128] = (jax.nn.silu(gate) * upper).astype(jnp.bfloat16)
+        made[:, 128 * k : 128 * k + 128] = (jax.nn.silu(gate) * upper).astype(jnp.bfloat16)
+    copies = [
+        pltpu.make_async_copy(made, out_ref.at[k], out_sems.at[k]) for k in range(TENSOR)
+    ]
+    for copy in copies:
+        copy.start()
+    for copy in copies:
+        copy.wait()
 
 
 def down_kernel(h_ref, d0, d1, d2, d3, out_ref, held, acc, sems):
-    wait = fetched(((d0,), (d1,), (d2,), (d3,)), held, sems, DOWN_PIECES)
+    wait = fetched((d0, d1, d2, d3), held, sems, DOWN_PIECES)
     each = TENSOR // DOWN_PIECES
     for piece in range(DOWN_PIECES):
         places = range(piece * each, (piece + 1) * each)
@@ -141,16 +141,18 @@
     return [pltpu.with_memory_space_constraint(a, pltpu.HBM) for a in arrays]
 
 
-def hidden_units(x, *weights):
+def hidden_copies(x, *weights):
     return pl.pallas_call(
         hidden_kernel,
         in_specs=[IN_VMEM] + [IN_HBM] * len(weights),
-        out_specs=IN_VMEM,
-        out_shape=jax.ShapeDtypeStruct((SLOTS, 512), jnp.bfloat16),
+        out_specs=IN_HBM,
+        out_shape=jax.ShapeDtypeStruct((TENSOR, SLOTS, 512), jnp.bfloat16),
         scratch_shapes=[
             pltpu.VMEM((8, D, 128), jnp.bfloat16),
             pltpu.VMEM((SLOTS, 1024), jnp.float32),
+            pltpu.VMEM((SLOTS, 512), jnp.bfloat16),
             pltpu.SemaphoreType.DMA((PIECES, 8)),
+            pltpu.SemaphoreType.DMA((TENSOR,)),
         ],
         compiler_params=PARAMS,
         cost_estimate=pl.CostEstimate(
@@ -181,8 +183,7 @@
     )(hidden, *left_in_hbm(weights))
 
 
-def gathered(array):
-    copies = jnp.broadcast_to(array[None], (TENSOR, *array.shape))
+def gathered(copies):
     return lax.all_to_all(copies, TENSOR_AXES, 0, 0, tiled=True)
 
 
@@ -199,8 +200,8 @@
     return lax.ppermute(array, ("xh", "xl"), [(i, 3 - i) for i in range(4)])
 
 
-def across_halves(array):
-    return lax.ppermute(array, "xh", [(0, 1), (1, 0)])
+def across_pair(array):
+    return lax.ppermute(array, "xl", [(0, 1), (1, 0)])
 
 
 def tied(*arrays):
@@ -225,28 +226,28 @@
     outgoing = pl.pallas_call(
         dispatch_kernel, out_shape=jax.ShapeDtypeStruct((SLOTS, FEAT), jnp.bfloat16)
     )(ids, tokens)
-    arrived = over_experts(outgoing)
+    pair = (gate, upper)
+    arrived, gate_far, down_sent, token = tied(
+        over_experts(outgoing), across_border(gate), across_pair(down), ids
+    )
     side = side_rows(norm_gain, router)
 
-    gate_far = across_border(gate)
-    top_sent, side = tied(upper[:TOP], side)
-    top_far = across_border(top_sent)
-    arrived, gate_far, top_far = tied(arrived, gate_far, top_far)
-    rest_far = across_border(upper[TOP:])
-    rest_far, down_sent = tied(rest_far, down)
-    near = (other_core(gate), other_core(upper))
-    last = (other_core(gate_far), other_core(top_far), other_core(rest_far))
-
-    rows = gathered(jnp.concatenate([arrived, side], axis=0))
-    hidden = hidden_units(rows, gate, upper, *near, gate_far, top_far, rest_far, *last)
-
-    down_far = across_halves(down_sent)
+    near = [other_core(a) for a in pair]
+    upper_far, down_sent, token = tied(across_border(upper), down_sent, token)
+    far = (gate_far, upper_far)
+    last = [other_core(a) for a in far]
+
+    sent = jnp.concatenate([arrived, side], axis=0)
+    rows = gathered(jnp.broadcast_to(sent[None], (TENSOR, *sent.shape)))
+    hidden = hidden_copies(rows, *pair, *near, *far, *last)
+
+    down_far = across_border(down_sent)
     down_near, down_last = other_core(down), other_core(down_far)
     summed = down_sums(gathered(hidden), down, down_near, down_far, down_last)
     returned = over_experts(summed)
     return pl.pallas_call(
         combine_kernel, out_shape=jax.ShapeDtypeStruct((TOK, FEAT), jnp.bfloat16)
-    )(ids, returned)
+    )(token, returned)
 
 
 def solution(mesh):

time: 179 us -> 155 us (0.87)
  the two profiles are of different devices: /device:TPU:64 before, /device:TPU:10 now
where the time goes in v6:
time: 155 us
  starting transfers between devices  51.7 us (33%)
  waiting for transfers between devices  41.1 us (27%)
  blocking collectives  38.6 us (25%)
  Pallas kernels  13.2 us (9%)
  local copies, waits for them, and re-layouts  8.13 us (5%)
  other arithmetic  1.59 us (1%)
    all_to_all x1, blocking collectives, over_experts(): return lax.all_to_all(parts, 'z', 0, 0, tiled=True).reshape(SLOTS, FEAT)  38.6 us
    all_to_all x1, waiting for transfers between devices, over_experts(): return lax.all_to_all(parts, 'z', 0, 0, tiled=True).reshape(SLOTS, FEAT)  16.8 us
    all_to_all x1, starting transfers between devices, over_experts(): return lax.all_to_all(parts, 'z', 0, 0, tiled=True).reshape(SLOTS, FEAT)  15.2 us
    all_to_all x2, waiting for transfers between devices, gathered(): return lax.all_to_all(copies, TENSOR_AXES, 0, 0, tiled=True)  13.8 us
    ppermute x6, starting transfers between devices, other_core(): return lax.ppermute(array, 'co', [(0, 1), (1, 0)])  12.5 us
    all_to_all x2, starting transfers between devices, gathered(): return lax.all_to_all(copies, TENSOR_AXES, 0, 0, tiled=True)  11.6 us
    ppermute x3, starting transfers between devices, across_border(): return lax.ppermute(array, ('xh', 'xl'), [(i, 3 - i) for i in range(4)])  8.71 us
    ppermute x3, waiting for transfers between devices, across_border(): return lax.ppermute(array, ('xh', 'xl'), [(i, 3 - i) for i in range(4)])  8.25 us
  transfers between devices with their start and end apart: 13, of which 6 were waited for; matrix products, arithmetic and copies ran while one was open for 2% of the time, Pallas kernels for 5%

profile of v6, /device:TPU:10, one launch (start us, length us, event | category | flops | bytes accessed | tf_op | source)
XLA Modules:
  0.0 154.6 jit_solution(16756981485410390502)
XLA Ops:
  0.0 3.4 %collective-permute-start.1 = (bf16[5120,128]{1,0:T(8,128)(2,1)}, bf16[5120,128]{1,0:T(8,128)(2,1)S(1)}, u32[]{:S(2)}, u32[]{:S(2)}) collective-permute-start(bf16[5120,128]{1,0:T(8,128)(2,1)} %bitcast.9), channel_id=1, source_target_pairs={{0,257},{1,256},{256,1},{257,0},{2,259},{3,258},{258,3},{259,2},{4... | collective-permute-start | bytes 3932168 | tf_op jit(solution)/shard_map/ppermute | solution.py:200
  3.4 3.7 %collective-permute-start.2 = (bf16[1024,640]{1,0:T(8,128)(2,1)}, bf16[1024,640]{1,0:T(8,128)(2,1)S(1)}, u32[]{:S(2)}, u32[]{:S(2)}) collective-permute-start(bf16[1024,640]{1,0:T(8,128)(2,1)} %bitcast.18), channel_id=1, source_target_pairs={{0,1},{1,0},{2,3},{3,2},{4,5},{5,4},{6,7},{7,6},{8,9},{9,8},{10,11... | collective-permute-start | bytes 3932168 | tf_op jit(solution)/shard_map/ppermute | solution.py:204
  7.1 2.0 %shard_map.73 = bf16[256,640]{1,0:T(8,128)(2,1)} custom-call(s32[1,128]{1,0:T(1,128)} %bitcast.21, bf16[128,640]{1,0:T(8,128)(2,1)} %tokens_ref.1), custom_call_target="tpu_custom_call" | custom-call | tf_op jit(solution)/shard_map/pallas_call | solution.py:226
  9.1 15.2 %all-to-all-start = ((bf16[16,16,640]{2,1,0:T(8,128)(2,1)}), bf16[16,16,640]{2,1,0:T(8,128)(2,1)S(1)}, u32[]{:S(2)}, u32[]{:S(2)}) async-start(bf16[16,16,640]{2,1,0:T(8,128)(2,1)} %bitcast.16), calls=%async_computation | async-start | bytes 655360 | tf_op jit(solution)/shard_map/all_to_all | solution.py:192
  24.3 1.9 %collective-permute-start = (bf16[5120,128]{1,0:T(8,128)(2,1)}, bf16[5120,128]{1,0:T(8,128)(2,1)}, u32[]{:S(2)}, u32[]{:S(2)}) collective-permute-start(bf16[5120,128]{1,0:T(8,128)(2,1)} %bitcast.12), channel_id=1, source_target_pairs={{0,257},{1,256},{256,1},{257,0},{2,259},{3,258},{258,3},{259,2},{4... | collective-permute-start | bytes 3932168 | tf_op jit(solution)/shard_map/ppermute | solution.py:200
  26.3 0.8 subtract_convert_fusion
  27.1 0.8 select_reduce_fusion
  27.9 16.8 %all-to-all-done = bf16[16,16,640]{2,1,0:T(8,128)(2,1)S(1)} async-done(((bf16[16,16,640]{2,1,0:T(8,128)(2,1)}), bf16[16,16,640]{2,1,0:T(8,128)(2,1)S(1)}, u32[]{:S(2)}, u32[]{:S(2)}) %all-to-all-start) | async-done | bytes 327712 | tf_op jit(solution)/shard_map/all_to_all | solution.py:192
  44.7 0.0 collective-permute-done.1.rest_4_
  44.7 0.0 copy-start.1
  44.7 0.0 collective-permute-done.2
  44.8 0.0 copy-start.7
  44.8 1.1 copy-done.1
  45.8 0.3 concatenate.7
  46.2 1.7 %broadcast_in_dim.21 = bf16[8,264,640]{2,1,0:T(8,128)(2,1)} broadcast(bf16[264,640]{1,0:T(8,128)(2,1)S(1)} %concatenate.7), dimensions={1,2} | broadcast | bytes 3041280 | tf_op jit(solution)/shard_map/broadcast_in_dim | solution.py:241
  47.9 0.0 copy-done.7
  47.9 5.8 %all-to-all-start.1 = ((bf16[8,264,640]{2,1,0:T(8,128)(2,1)}), bf16[8,264,640]{2,1,0:T(8,128)(2,1)S(1)}, u32[]{:S(2)}, u32[]{:S(2)}) async-start(bf16[8,264,640]{2,1,0:T(8,128)(2,1)} %broadcast_in_dim.21), calls=%async_computation.1 | async-start | bytes 5406720 | tf_op jit(solution)/shard_map/all_to_all | solution.py:187
  53.7 1.9 %collective-permute-start.3 = (bf16[5120,128]{1,0:T(8,128)(2,1)}, bf16[5120,128]{1,0:T(8,128)(2,1)S(1)}, u32[]{:S(2)}, u32[]{:S(2)}) collective-permute-start(bf16[5120,128]{1,0:T(8,128)(2,1)} %bitcast.10), channel_id=1, source_target_pairs={{0,128},{128,0},{1,129},{129,1},{2,130},{130,2},{3,131},{131,3},{4... | collective-permute-start | bytes 3932168 | tf_op jit(solution)/shard_map/ppermute | solution.py:196
  55.6 2.4 %collective-permute-start.4 = (bf16[5120,128]{1,0:T(8,128)(2,1)}, bf16[5120,128]{1,0:T(8,128)(2,1)S(1)}, u32[]{:S(2)}, u32[]{:S(2)}) collective-permute-start(bf16[5120,128]{1,0:T(8,128)(2,1)} %bitcast.13), channel_id=1, source_target_pairs={{0,128},{128,0},{1,129},{129,1},{2,130},{130,2},{3,131},{131,3},{4... | collective-permute-start | bytes 3932168 | tf_op jit(solution)/shard_map/ppermute | solution.py:196
  58.1 2.7 %collective-permute-done.rest_5_ = bf16[5120,128]{1,0:T(8,128)(2,1)} collective-permute-done((bf16[5120,128]{1,0:T(8,128)(2,1)}, bf16[5120,128]{1,0:T(8,128)(2,1)}, u32[]{:S(2)}, u32[]{:S(2)}) %collective-permute-start) | collective-permute-done | bytes 1310752 | tf_op jit(solution)/shard_map/ppermute | solution.py:200
  60.8 1.9 %collective-permute-start.6 = (bf16[5120,128]{1,0:T(8,128)(2,1)}, bf16[5120,128]{1,0:T(8,128)(2,1)S(1)}, u32[]{:S(2)}, u32[]{:S(2)}) collective-permute-start(bf16[5120,128]{1,0:T(8,128)(2,1)} %collective-permute-done.rest_5_), channel_id=1, source_target_pairs={{0,128},{128,0},{1,129},{129,1},{2,130},{130,2},{3,131},{131,3},{4... | collective-permute-start | bytes 3932168 | tf_op jit(solution)/shard_map/ppermute | solution.py:196
  62.7 2.4 %collective-permute-start.5 = (bf16[5120,128]{1,0:T(8,128)(2,1)}, bf16[5120,128]{1,0:T(8,128)(2,1)}, u32[]{:S(2)}, u32[]{:S(2)}) collective-permute-start(bf16[5120,128]{1,0:T(8,128)(2,1)} %copy-done.1), channel_id=1, source_target_pairs={{0,128},{128,0},{1,129},{129,1},{2,130},{130,2},{3,131},{131,3},{4... | collective-permute-start | bytes 3932168 | tf_op jit(solution)/shard_map/ppermute | solution.py:196
  65.1 3.4 %collective-permute-start.8 = (bf16[1024,640]{1,0:T(8,128)(2,1)}, bf16[1024,640]{1,0:T(8,128)(2,1)}, u32[]{:S(2)}, u32[]{:S(2)}) collective-permute-start(bf16[1024,640]{1,0:T(8,128)(2,1)} %copy-done.7), channel_id=1, source_target_pairs={{0,257},{1,256},{256,1},{257,0},{2,259},{3,258},{258,3},{259,2},{4... | collective-permute-start | bytes 3932168 | tf_op jit(solution)/shard_map/ppermute | solution.py:200
  68.5 0.0 collective-permute-done.3.rest_2_
  68.6 0.0 copy-start.2
  68.6 0.0 collective-permute-done.4.rest_3_
  68.6 0.0 copy-start.3
  68.6 0.0 collective-permute-done.6.rest_7_
  68.6 1.0 copy-done.2
  69.6 0.4 copy-done.3
  70.0 0.0 copy-start.4
  70.0 1.1 copy-done.4
  71.2 0.0 collective-permute-done.5.rest_6_
  71.2 6.9 %all-to-all-done.1.x_ref = bf16[8,264,640]{2,1,0:T(8,128)(2,1)S(1)} async-done(((bf16[8,264,640]{2,1,0:T(8,128)(2,1)}), bf16[8,264,640]{2,1,0:T(8,128)(2,1)S(1)}, u32[]{:S(2)}, u32[]{:S(2)}) %all-to-all-start.1) | async-done | bytes 2703392 | tf_op jit(solution)/shard_map/all_to_all | solution.py:187
  78.1 5.4 %shard_map.74 = bf16[8,256,512]{2,1,0:T(8,128)(2,1)S(1)} custom-call(bf16[8,264,640]{2,1,0:T(8,128)(2,1)S(1)} %all-to-all-done.1.x_ref, bf16[5120,128]{1,0:T(8,128)(2,1)} %bitcast.11, bf16[5120,128]{1,0:T(8,128)(2,1)} %bitcast.14, bf16[5120,128]{1,0:T(8,128)(2,1)} %copy-done.2, bf16[5120,128]{1,0:T(8,128)(2,1)} %copy-done.3, bf16[5120,128]{1,0:T(8,128)(2,1)} %copy-done.1, ...), custom_call_target="tpu_custom_call" | custom-call | flops 2684354560 | bytes 13107200 | tf_op jit(solution)/shard_map/pallas_call | solution.py:145
  83.5 0.0 copy-start
  83.5 1.3 copy-done
  84.8 0.0 copy-start.5
  84.8 5.8 %all-to-all-start.2 = ((bf16[8,256,512]{2,1,0:T(8,128)(2,1)}), bf16[8,256,512]{2,1,0:T(8,128)(2,1)S(1)}, u32[]{:S(2)}, u32[]{:S(2)}) async-start(bf16[8,256,512]{2,1,0:T(8,128)(2,1)} %copy-done), calls=%async_computation.2 | async-start | bytes 4194304 | tf_op jit(solution)/shard_map/all_to_all | solution.py:187
  90.6 0.0 copy-done.5
  90.6 1.9 %collective-permute-start.7 = (bf16[1024,640]{1,0:T(8,128)(2,1)S(1)}, bf16[1024,640]{1,0:T(8,128)(2,1)S(1)}, u32[]{:S(2)}, u32[]{:S(2)}) collective-permute-start(bf16[1024,640]{1,0:T(8,128)(2,1)S(1)} %bitcast.20), channel_id=1, source_target_pairs={{0,128},{128,0},{1,129},{129,1},{2,130},{130,2},{3,131},{131,3},{4... | collective-permute-start | bytes 3932168 | tf_op jit(solution)/shard_map/ppermute | solution.py:196
  92.5 5.5 %collective-permute-done.8.d2 = bf16[1024,640]{1,0:T(8,128)(2,1)} collective-permute-done((bf16[1024,640]{1,0:T(8,128)(2,1)}, bf16[1024,640]{1,0:T(8,128)(2,1)}, u32[]{:S(2)}, u32[]{:S(2)}) %collective-permute-start.8) | collective-permute-done | bytes 1310752 | tf_op jit(solution)/shard_map/ppermute | solution.py:200
  98.0 1.9 %collective-permute-start.9 = (bf16[1024,640]{1,0:T(8,128)(2,1)}, bf16[1024,640]{1,0:T(8,128)(2,1)}, u32[]{:S(2)}, u32[]{:S(2)}) collective-permute-start(bf16[1024,640]{1,0:T(8,128)(2,1)} %collective-permute-done.8.d2), channel_id=1, source_target_pairs={{0,128},{128,0},{1,129},{129,1},{2,130},{130,2},{3,131},{131,3},{4... | collective-permute-start | bytes 3932168 | tf_op jit(solution)/shard_map/ppermute | solution.py:196
  100.0 0.0 collective-permute-done.7.d1
  100.0 0.0 copy-start.6
  100.0 1.1 copy-done.6
  101.1 2.3 %collective-permute-done.9.d3 = bf16[1024,640]{1,0:T(8,128)(2,1)} collective-permute-done((bf16[1024,640]{1,0:T(8,128)(2,1)}, bf16[1024,640]{1,0:T(8,128)(2,1)}, u32[]{:S(2)}, u32[]{:S(2)}) %collective-permute-start.9) | collective-permute-done | bytes 1310752 | tf_op jit(solution)/shard_map/ppermute | solution.py:196
  103.3 6.8 %all-to-all-done.2.h_ref = bf16[8,256,512]{2,1,0:T(8,128)(2,1)S(1)} async-done(((bf16[8,256,512]{2,1,0:T(8,128)(2,1)}), bf16[8,256,512]{2,1,0:T(8,128)(2,1)S(1)}, u32[]{:S(2)}, u32[]{:S(2)}) %all-to-all-start.2) | async-done | bytes 2097184 | tf_op jit(solution)/shard_map/all_to_all | solution.py:187
  110.1 3.8 %shard_map.75 = bf16[256,640]{1,0:T(8,128)(2,1)S(1)} custom-call(bf16[8,256,512]{2,1,0:T(8,128)(2,1)S(1)} %all-to-all-done.2.h_ref, bf16[1024,640]{1,0:T(8,128)(2,1)} %bitcast.19, bf16[1024,640]{1,0:T(8,128)(2,1)} %copy-done.6, bf16[1024,640]{1,0:T(8,128)(2,1)} %collective-permute-done.8.d2, bf16[1024,640]{1,0:T(8,128)(2,1)} %collective-permute-done.9.d3), custom_call_target="tpu_custom_call" | custom-call | flops 1342177280 | bytes 7340032 | tf_op jit(solution)/shard_map/pallas_call | solution.py:167
  114.0 38.6 %all_to_all.20 = bf16[16,16,640]{2,1,0:T(8,128)(2,1)} all-to-all(bf16[16,16,640]{2,1,0:T(8,128)(2,1)S(1)} %bitcast.8), channel_id=1, replica_groups=mesh['xh'=2,'co'=2,'z'=16,'y'=4,'xl'=2] {'z'}, dimensions={0} | all-to-all | bytes 655360 | tf_op jit(solution)/shard_map/all_to_all | solution.py:192
  152.6 2.0 %shard_map.76 = bf16[128,640]{1,0:T(8,128)(2,1)} custom-call(s32[1,128]{1,0:T(1,128)} %bitcast.22, bf16[256,640]{1,0:T(8,128)(2,1)} %bitcast.17), custom_call_target="tpu_custom_call" | custom-call | tf_op jit(solution)/shard_map/pallas_call | solution.py:248
  (6 shorter events, 0.0 us)
Async XLA Ops:
  0.0 44.7 %collective-permute-start.1 = (bf16[5120,128]{1,0:T(8,128)(2,1)}, bf16[5120,128]{1,0:T(8,128)(2,1)S(1)}, u32[]{:S(2)}, u32[]{:S(2)}) collective-permute-start(bf16[5120,128]{1,0:T(8,128)(2,1)} %bitcast.9), channel_id=1, source_target_pairs={{0,257},{1,256},{256,1},{257,0},{2,259},{3,258},{258,3},{259,2},{4... | collective-permute-start | bytes 3932168 | tf_op jit(solution)/shard_map/ppermute | solution.py:200
  3.4 41.4 %collective-permute-start.2 = (bf16[1024,640]{1,0:T(8,128)(2,1)}, bf16[1024,640]{1,0:T(8,128)(2,1)S(1)}, u32[]{:S(2)}, u32[]{:S(2)}) collective-permute-start(bf16[1024,640]{1,0:T(8,128)(2,1)} %bitcast.18), channel_id=1, source_target_pairs={{0,1},{1,0},{2,3},{3,2},{4,5},{5,4},{6,7},{7,6},{8,9},{9,8},{10,11... | collective-permute-start | bytes 3932168 | tf_op jit(solution)/shard_map/ppermute | solution.py:204
  9.1 35.6 %all-to-all-start = ((bf16[16,16,640]{2,1,0:T(8,128)(2,1)}), bf16[16,16,640]{2,1,0:T(8,128)(2,1)S(1)}, u32[]{:S(2)}, u32[]{:S(2)}) async-start(bf16[16,16,640]{2,1,0:T(8,128)(2,1)} %bitcast.16), calls=%async_computation | async-start | bytes 655360 | tf_op jit(solution)/shard_map/all_to_all | solution.py:192
  24.3 36.5 %collective-permute-start = (bf16[5120,128]{1,0:T(8,128)(2,1)}, bf16[5120,128]{1,0:T(8,128)(2,1)}, u32[]{:S(2)}, u32[]{:S(2)}) collective-permute-start(bf16[5120,128]{1,0:T(8,128)(2,1)} %bitcast.12), channel_id=1, source_target_pairs={{0,257},{1,256},{256,1},{257,0},{2,259},{3,258},{258,3},{259,2},{4... | collective-permute-start | bytes 3932168 | tf_op jit(solution)/shard_map/ppermute | solution.py:200
  44.7 1.1 copy-start.1
  44.8 3.2 %copy-start.7 = (bf16[1024,640]{1,0:T(8,128)(2,1)}, bf16[1024,640]{1,0:T(8,128)(2,1)S(1)}, u32[]{:S(2)}) copy-start(bf16[1024,640]{1,0:T(8,128)(2,1)S(1)} %collective-permute-done.2) | copy-start | bytes 3932164
  47.9 30.2 %all-to-all-start.1 = ((bf16[8,264,640]{2,1,0:T(8,128)(2,1)}), bf16[8,264,640]{2,1,0:T(8,128)(2,1)S(1)}, u32[]{:S(2)}, u32[]{:S(2)}) async-start(bf16[8,264,640]{2,1,0:T(8,128)(2,1)} %broadcast_in_dim.21), calls=%async_computation.1 | async-start | bytes 5406720 | tf_op jit(solution)/shard_map/all_to_all | solution.py:187
  53.7 14.8 %collective-permute-start.3 = (bf16[5120,128]{1,0:T(8,128)(2,1)}, bf16[5120,128]{1,0:T(8,128)(2,1)S(1)}, u32[]{:S(2)}, u32[]{:S(2)}) collective-permute-start(bf16[5120,128]{1,0:T(8,128)(2,1)} %bitcast.10), channel_id=1, source_target_pairs={{0,128},{128,0},{1,129},{129,1},{2,130},{130,2},{3,131},{131,3},{4... | collective-permute-start | bytes 3932168 | tf_op jit(solution)/shard_map/ppermute | solution.py:196
  55.6 12.9 %collective-permute-start.4 = (bf16[5120,128]{1,0:T(8,128)(2,1)}, bf16[5120,128]{1,0:T(8,128)(2,1)S(1)}, u32[]{:S(2)}, u32[]{:S(2)}) collective-permute-start(bf16[5120,128]{1,0:T(8,128)(2,1)} %bitcast.13), channel_id=1, source_target_pairs={{0,128},{128,0},{1,129},{129,1},{2,130},{130,2},{3,131},{131,3},{4... | collective-permute-start | bytes 3932168 | tf_op jit(solution)/shard_map/ppermute | solution.py:196
  60.8 7.8 %collective-permute-start.6 = (bf16[5120,128]{1,0:T(8,128)(2,1)}, bf16[5120,128]{1,0:T(8,128)(2,1)S(1)}, u32[]{:S(2)}, u32[]{:S(2)}) collective-permute-start(bf16[5120,128]{1,0:T(8,128)(2,1)} %collective-permute-done.rest_5_), channel_id=1, source_target_pairs={{0,128},{128,0},{1,129},{129,1},{2,130},{130,2},{3,131},{131,3},{4... | collective-permute-start | bytes 3932168 | tf_op jit(solution)/shard_map/ppermute | solution.py:196
  62.7 8.4 %collective-permute-start.5 = (bf16[5120,128]{1,0:T(8,128)(2,1)}, bf16[5120,128]{1,0:T(8,128)(2,1)}, u32[]{:S(2)}, u32[]{:S(2)}) collective-permute-start(bf16[5120,128]{1,0:T(8,128)(2,1)} %copy-done.1), channel_id=1, source_target_pairs={{0,128},{128,0},{1,129},{129,1},{2,130},{130,2},{3,131},{131,3},{4... | collective-permute-start | bytes 3932168 | tf_op jit(solution)/shard_map/ppermute | solution.py:196
  65.1 32.9 %collective-permute-start.8 = (bf16[1024,640]{1,0:T(8,128)(2,1)}, bf16[1024,640]{1,0:T(8,128)(2,1)}, u32[]{:S(2)}, u32[]{:S(2)}) collective-permute-start(bf16[1024,640]{1,0:T(8,128)(2,1)} %copy-done.7), channel_id=1, source_target_pairs={{0,257},{1,256},{256,1},{257,0},{2,259},{3,258},{258,3},{259,2},{4... | collective-permute-start | bytes 3932168 | tf_op jit(solution)/shard_map/ppermute | solution.py:200
  68.6 1.1 copy-start.2
  68.6 1.5 copy-start.3
  70.0 1.1 copy-start.4
  83.5 1.3 copy-start
  84.8 5.8 %copy-start.5 = (bf16[1,1024,640]{2,1,0:T(8,128)(2,1)S(1)}, bf16[1,1024,640]{2,1,0:T(8,128)(2,1)}, u32[]{:S(2)}) copy-start(bf16[1,1024,640]{2,1,0:T(8,128)(2,1)} %param.13) | copy-start | bytes 3932164
  84.8 25.3 %all-to-all-start.2 = ((bf16[8,256,512]{2,1,0:T(8,128)(2,1)}), bf16[8,256,512]{2,1,0:T(8,128)(2,1)S(1)}, u32[]{:S(2)}, u32[]{:S(2)}) async-start(bf16[8,256,512]{2,1,0:T(8,128)(2,1)} %copy-done), calls=%async_computation.2 | async-start | bytes 4194304 | tf_op jit(solution)/shard_map/all_to_all | solution.py:187
  90.6 9.3 %collective-permute-start.7 = (bf16[1024,640]{1,0:T(8,128)(2,1)S(1)}, bf16[1024,640]{1,0:T(8,128)(2,1)S(1)}, u32[]{:S(2)}, u32[]{:S(2)}) collective-permute-start(bf16[1024,640]{1,0:T(8,128)(2,1)S(1)} %bitcast.20), channel_id=1, source_target_pairs={{0,128},{128,0},{1,129},{129,1},{2,130},{130,2},{3,131},{131,3},{4... | collective-permute-start | bytes 3932168 | tf_op jit(solution)/shard_map/ppermute | solution.py:196
  98.0 5.3 %collective-permute-start.9 = (bf16[1024,640]{1,0:T(8,128)(2,1)}, bf16[1024,640]{1,0:T(8,128)(2,1)}, u32[]{:S(2)}, u32[]{:S(2)}) collective-permute-start(bf16[1024,640]{1,0:T(8,128)(2,1)} %collective-permute-done.8.d2), channel_id=1, source_target_pairs={{0,128},{128,0},{1,129},{129,1},{2,130},{130,2},{3,131},{131,3},{4... | collective-permute-start | bytes 3932168 | tf_op jit(solution)/shard_map/ppermute | solution.py:196
  100.0 1.1 copy-start.6

commit v7 on v6

--- a/solution.py
+++ b/solution.py
@@ -14,7 +14,7 @@
 TOK = 128
 FEAT = 640
 TENSOR = 8
-EXTRA = 8
+EXTRA = 16
 VMEM = 28 * 1024 * 1024
 PIECES = 4
 PER = TENSOR // PIECES
@@ -135,6 +135,7 @@
 IN_VMEM = pl.BlockSpec(memory_space=pltpu.VMEM)
 IN_HBM = pl.BlockSpec(memory_space=pl.ANY)
 PARAMS = pltpu.CompilerParams(vmem_limit_bytes=VMEM)
+SMALL = pltpu.CompilerParams(vmem_limit_bytes=8 * 1024 * 1024)
 
 
 def left_in_hbm(arrays):
@@ -146,7 +147,7 @@
         hidden_kernel,
         in_specs=[IN_VMEM] + [IN_HBM] * len(weights),
         out_specs=IN_HBM,
-        out_shape=jax.ShapeDtypeStruct((TENSOR, SLOTS, 512), jnp.bfloat16),
+        out_shape=pltpu.HBM((TENSOR, SLOTS, 512), jnp.bfloat16),
         scratch_shapes=[
             pltpu.VMEM((8, D, 128), jnp.bfloat16),
             pltpu.VMEM((SLOTS, 1024), jnp.float32),
@@ -161,6 +162,30 @@
             transcendentals=SLOTS * 512,
         ),
     )(x, *left_in_hbm(weights))
+
+
+def spread_kernel(rows_ref, side_ref, out_ref, sems):
+    copies = []
+    for k in range(TENSOR):
+        for n, (ref, part) in enumerate(
+            ((rows_ref, pl.ds(0, SLOTS)), (side_ref, pl.ds(SLOTS, EXTRA)))
+        ):
+            copies.append(pltpu.make_async_copy(ref, out_ref.at[k, part], sems.at[n, k]))
+    for copy in copies:
+        copy.start()
+    for copy in copies:
+        copy.wait()
+
+
+def row_copies(rows, side):
+    return pl.pallas_call(
+        spread_kernel,
+        in_specs=[IN_VMEM, IN_VMEM],
+        out_specs=IN_HBM,
+        out_shape=pltpu.HBM((TENSOR, SLOTS + EXTRA, FEAT), jnp.bfloat16),
+        scratch_shapes=[pltpu.SemaphoreType.DMA((2, TENSOR))],
+        compiler_params=SMALL,
+    )(rows, side)
 
 
 def down_sums(hidden, *weights):
@@ -237,8 +262,7 @@
     far = (gate_far, upper_far)
     last = [other_core(a) for a in far]
 
-    sent = jnp.concatenate([arrived, side], axis=0)
-    rows = gathered(jnp.broadcast_to(sent[None], (TENSOR, *sent.shape)))
+    rows = gathered(row_copies(arrived, side))
     hidden = hidden_copies(rows, *pair, *near, *far, *last)
 
     down_far = across_border(down_sent)
@@ -246,7 +270,9 @@
     summed = down_sums(gathered(hidden), down, down_near, down_far, down_last)
     returned = over_experts(summed)
     return pl.pallas_call(
-        combine_kernel, out_shape=jax.ShapeDtypeStruct((TOK, FEAT), jnp.bfloat16)
+        combine_kernel,
+        out_shape=jax.ShapeDtypeStruct((TOK, FEAT), jnp.bfloat16),
+        compiler_params=SMALL,
     )(token, returned)
 
 

time: 155 us -> 154 us (level)
  local copies, waits for them, and re-layouts: 8.13 us -> 4.32 us
  Pallas kernels: 13.2 us -> 15.2 us
    pallas_call x0 -> x1, Pallas kernels: none -> 1.82 us  [row_copies(): pl.pallas_call(spread_kernel, in_specs=[IN_VMEM, IN_VMEM], out_specs=IN_H...]
    unnamed x16, local copies, waits for them, and re-layouts: 6.01 us -> 4.23 us
    broadcast_in_dim x1 -> x0, local copies, waits for them, and re-layouts: 1.74 us -> none  [on_device(): rows = gathered(jnp.broadcast_to(sent[None], (TENSOR, *sent.shape)))]
  transfers between devices with their start and end apart: 13 -> 13, of which waited for: 6 -> 6; matrix products, arithmetic and copies ran while one was open for 2% -> 1% of each run, Pallas kernels for 5% -> 7%
where the time goes in v7:
time: 154 us; the launch traced here: 153 us
  starting transfers between devices  51.9 us (34%)
  waiting for transfers between devices  41.6 us (27%)
  blocking collectives  38.6 us (25%)
  Pallas kernels  15.2 us (10%)
  local copies, waits for them, and re-layouts  4.32 us (3%)
  other arithmetic  1.59 us (1%)
    all_to_all x1, blocking collectives, over_experts(): return lax.all_to_all(parts, 'z', 0, 0, tiled=True).reshape(SLOTS, FEAT)  38.6 us
    all_to_all x1, waiting for transfers between devices, over_experts(): return lax.all_to_all(parts, 'z', 0, 0, tiled=True).reshape(SLOTS, FEAT)  16.8 us
    all_to_all x1, starting transfers between devices, over_experts(): return lax.all_to_all(parts, 'z', 0, 0, tiled=True).reshape(SLOTS, FEAT)  15.2 us
    all_to_all x2, waiting for transfers between devices, gathered(): return lax.all_to_all(copies, TENSOR_AXES, 0, 0, tiled=True)  13.8 us
    ppermute x6, starting transfers between devices, other_core(): return lax.ppermute(array, 'co', [(0, 1), (1, 0)])  12.6 us
    all_to_all x2, starting transfers between devices, gathered(): return lax.all_to_all(copies, TENSOR_AXES, 0, 0, tiled=True)  11.6 us
    ppermute x3, waiting for transfers between devices, across_border(): return lax.ppermute(array, ('xh', 'xl'), [(i, 3 - i) for i in range(4)])  8.85 us
    ppermute x3, starting transfers between devices, across_border(): return lax.ppermute(array, ('xh', 'xl'), [(i, 3 - i) for i in range(4)])  8.71 us
  transfers between devices with their start and end apart: 13, of which 6 were waited for; matrix products, arithmetic and copies ran while one was open for 1% of the time, Pallas kernels for 7%

profile of v7, /device:TPU:10, one launch (start us, length us, event | category | flops | bytes accessed | tf_op | source)
XLA Modules:
  0.0 153.5 jit_solution(13327235435968725643)
XLA Ops:
  0.0 3.4 %collective-permute-start.1 = (bf16[5120,128]{1,0:T(8,128)(2,1)}, bf16[5120,128]{1,0:T(8,128)(2,1)S(1)}, u32[]{:S(2)}, u32[]{:S(2)}) collective-permute-start(bf16[5120,128]{1,0:T(8,128)(2,1)} %bitcast.14), channel_id=1, source_target_pairs={{0,257},{1,256},{256,1},{257,0},{2,259},{3,258},{258,3},{259,2},{4... | collective-permute-start | bytes 3932168 | tf_op jit(solution)/shard_map/ppermute | solution.py:225
  3.4 3.7 %collective-permute-start.2 = (bf16[1024,640]{1,0:T(8,128)(2,1)}, bf16[1024,640]{1,0:T(8,128)(2,1)S(1)}, u32[]{:S(2)}, u32[]{:S(2)}) collective-permute-start(bf16[1024,640]{1,0:T(8,128)(2,1)} %bitcast.20), channel_id=1, source_target_pairs={{0,1},{1,0},{2,3},{3,2},{4,5},{5,4},{6,7},{7,6},{8,9},{9,8},{10,11... | collective-permute-start | bytes 3932168 | tf_op jit(solution)/shard_map/ppermute | solution.py:229
  7.1 2.0 %shard_map.73 = bf16[256,640]{1,0:T(8,128)(2,1)} custom-call(s32[1,128]{1,0:T(1,128)} %bitcast.11, bf16[128,640]{1,0:T(8,128)(2,1)} %tokens_ref.1), custom_call_target="tpu_custom_call" | custom-call | tf_op jit(solution)/shard_map/pallas_call | solution.py:251
  9.1 15.2 %all-to-all-start = ((bf16[16,16,640]{2,1,0:T(8,128)(2,1)}), bf16[16,16,640]{2,1,0:T(8,128)(2,1)S(1)}, u32[]{:S(2)}, u32[]{:S(2)}) async-start(bf16[16,16,640]{2,1,0:T(8,128)(2,1)} %bitcast.13), calls=%async_computation | async-start | bytes 655360 | tf_op jit(solution)/shard_map/all_to_all | solution.py:217
  24.3 1.9 %collective-permute-start = (bf16[5120,128]{1,0:T(8,128)(2,1)}, bf16[5120,128]{1,0:T(8,128)(2,1)}, u32[]{:S(2)}, u32[]{:S(2)}) collective-permute-start(bf16[5120,128]{1,0:T(8,128)(2,1)} %bitcast.17), channel_id=1, source_target_pairs={{0,257},{1,256},{256,1},{257,0},{2,259},{3,258},{258,3},{259,2},{4... | collective-permute-start | bytes 3932168 | tf_op jit(solution)/shard_map/ppermute | solution.py:225
  26.3 0.8 subtract_convert_fusion
  27.1 0.8 select_reduce_fusion
  27.9 0.1 stack.24.side_ref
  28.0 16.8 %all-to-all-done = bf16[16,16,640]{2,1,0:T(8,128)(2,1)S(1)} async-done(((bf16[16,16,640]{2,1,0:T(8,128)(2,1)}), bf16[16,16,640]{2,1,0:T(8,128)(2,1)S(1)}, u32[]{:S(2)}, u32[]{:S(2)}) %all-to-all-start) | async-done | bytes 327712 | tf_op jit(solution)/shard_map/all_to_all | solution.py:217
  44.7 0.0 collective-permute-done.1.rest_4_
  44.7 0.0 copy-start.2
  44.7 0.0 collective-permute-done.2
  44.8 0.0 copy-start.7
  44.8 1.8 %shard_map.74 = bf16[8,272,640]{2,1,0:T(8,128)(2,1)} custom-call(bf16[256,640]{1,0:T(8,128)(2,1)S(1)} %bitcast.8, bf16[16,640]{1,0:T(8,128)(2,1)S(1)} %stack.24.side_ref), custom_call_target="tpu_custom_call" | custom-call | tf_op jit(solution)/shard_map/pallas_call | solution.py:181
  46.6 0.2 copy-done.2
  46.7 0.4 copy-done.7
  47.2 5.8 %all-to-all-start.1 = ((bf16[8,272,640]{2,1,0:T(8,128)(2,1)}), bf16[8,272,640]{2,1,0:T(8,128)(2,1)S(1)}, u32[]{:S(2)}, u32[]{:S(2)}) async-start(bf16[8,272,640]{2,1,0:T(8,128)(2,1)} %shard_map.74), calls=%async_computation.1 | async-start | bytes 5570560 | tf_op jit(solution)/shard_map/all_to_all | solution.py:212
  53.0 1.9 %collective-permute-start.3 = (bf16[5120,128]{1,0:T(8,128)(2,1)}, bf16[5120,128]{1,0:T(8,128)(2,1)S(1)}, u32[]{:S(2)}, u32[]{:S(2)}) collective-permute-start(bf16[5120,128]{1,0:T(8,128)(2,1)} %bitcast.15), channel_id=1, source_target_pairs={{0,128},{128,0},{1,129},{129,1},{2,130},{130,2},{3,131},{131,3},{4... | collective-permute-start | bytes 3932168 | tf_op jit(solution)/shard_map/ppermute | solution.py:221
  54.9 2.4 %collective-permute-start.4 = (bf16[5120,128]{1,0:T(8,128)(2,1)}, bf16[5120,128]{1,0:T(8,128)(2,1)S(1)}, u32[]{:S(2)}, u32[]{:S(2)}) collective-permute-start(bf16[5120,128]{1,0:T(8,128)(2,1)} %bitcast.18), channel_id=1, source_target_pairs={{0,128},{128,0},{1,129},{129,1},{2,130},{130,2},{3,131},{131,3},{4... | collective-permute-start | bytes 3932168 | tf_op jit(solution)/shard_map/ppermute | solution.py:221
  57.3 3.5 %collective-permute-done.rest_5_ = bf16[5120,128]{1,0:T(8,128)(2,1)} collective-permute-done((bf16[5120,128]{1,0:T(8,128)(2,1)}, bf16[5120,128]{1,0:T(8,128)(2,1)}, u32[]{:S(2)}, u32[]{:S(2)}) %collective-permute-start) | collective-permute-done | bytes 1310752 | tf_op jit(solution)/shard_map/ppermute | solution.py:225
  60.8 1.9 %collective-permute-start.6 = (bf16[5120,128]{1,0:T(8,128)(2,1)}, bf16[5120,128]{1,0:T(8,128)(2,1)S(1)}, u32[]{:S(2)}, u32[]{:S(2)}) collective-permute-start(bf16[5120,128]{1,0:T(8,128)(2,1)} %collective-permute-done.rest_5_), channel_id=1, source_target_pairs={{0,128},{128,0},{1,129},{129,1},{2,130},{130,2},{3,131},{131,3},{4... | collective-permute-start | bytes 3932168 | tf_op jit(solution)/shard_map/ppermute | solution.py:221
  62.7 2.4 %collective-permute-start.5 = (bf16[5120,128]{1,0:T(8,128)(2,1)}, bf16[5120,128]{1,0:T(8,128)(2,1)}, u32[]{:S(2)}, u32[]{:S(2)}) collective-permute-start(bf16[5120,128]{1,0:T(8,128)(2,1)} %copy-done.2), channel_id=1, source_target_pairs={{0,128},{128,0},{1,129},{129,1},{2,130},{130,2},{3,131},{131,3},{4... | collective-permute-start | bytes 3932168 | tf_op jit(solution)/shard_map/ppermute | solution.py:221
  65.1 3.4 %collective-permute-start.8 = (bf16[1024,640]{1,0:T(8,128)(2,1)}, bf16[1024,640]{1,0:T(8,128)(2,1)}, u32[]{:S(2)}, u32[]{:S(2)}) collective-permute-start(bf16[1024,640]{1,0:T(8,128)(2,1)} %copy-done.7), channel_id=1, source_target_pairs={{0,257},{1,256},{256,1},{257,0},{2,259},{3,258},{258,3},{259,2},{4... | collective-permute-start | bytes 3932168 | tf_op jit(solution)/shard_map/ppermute | solution.py:225
  68.5 0.0 collective-permute-done.3.rest_2_
  68.6 0.0 copy-start.3
  68.6 0.0 collective-permute-done.4.rest_3_
  68.6 0.0 copy-start.4
  68.6 0.0 collective-permute-done.6.rest_7_
  68.6 1.1 copy-done.3
  69.7 0.4 copy-done.4
  70.0 0.0 copy-start.5
  70.0 1.1 copy-done.5
  71.1 0.0 collective-permute-done.5.rest_6_
  71.2 7.1 %all-to-all-done.1.x_ref = bf16[8,272,640]{2,1,0:T(8,128)(2,1)S(1)} async-done(((bf16[8,272,640]{2,1,0:T(8,128)(2,1)}), bf16[8,272,640]{2,1,0:T(8,128)(2,1)S(1)}, u32[]{:S(2)}, u32[]{:S(2)}) %all-to-all-start.1) | async-done | bytes 2785312 | tf_op jit(solution)/shard_map/all_to_all | solution.py:212
  78.2 6.5 %shard_map.75 = bf16[8,256,512]{2,1,0:T(8,128)(2,1)} custom-call(bf16[8,272,640]{2,1,0:T(8,128)(2,1)S(1)} %all-to-all-done.1.x_ref, bf16[5120,128]{1,0:T(8,128)(2,1)} %bitcast.16, bf16[5120,128]{1,0:T(8,128)(2,1)} %bitcast.19, bf16[5120,128]{1,0:T(8,128)(2,1)} %copy-done.3, bf16[5120,128]{1,0:T(8,128)(2,1)} %copy-done.4, bf16[5120,128]{1,0:T(8,128)(2,1)} %copy-done.2, ...), custom_call_target="tpu_custom_call" | custom-call | flops 2684354560 | bytes 13107200 | tf_op jit(solution)/shard_map/pallas_call | solution.py:146
  84.8 0.0 copy-start.1
  84.8 5.8 %all-to-all-start.2 = ((bf16[8,256,512]{2,1,0:T(8,128)(2,1)}), bf16[8,256,512]{2,1,0:T(8,128)(2,1)S(1)}, u32[]{:S(2)}, u32[]{:S(2)}) async-start(bf16[8,256,512]{2,1,0:T(8,128)(2,1)} %shard_map.75), calls=%async_computation.2 | async-start | bytes 4194304 | tf_op jit(solution)/shard_map/all_to_all | solution.py:212
  90.6 0.0 copy-done.1
  90.6 0.0 copy-start
  90.6 2.0 %collective-permute-start.7 = (bf16[1024,640]{1,0:T(8,128)(2,1)S(1)}, bf16[1024,640]{1,0:T(8,128)(2,1)S(1)}, u32[]{:S(2)}, u32[]{:S(2)}) collective-permute-start(bf16[1024,640]{1,0:T(8,128)(2,1)S(1)} %bitcast.22), channel_id=1, source_target_pairs={{0,128},{128,0},{1,129},{129,1},{2,130},{130,2},{3,131},{131,3},{4... | collective-permute-start | bytes 3932168 | tf_op jit(solution)/shard_map/ppermute | solution.py:221
  92.7 5.4 %collective-permute-done.8.d2 = bf16[1024,640]{1,0:T(8,128)(2,1)} collective-permute-done((bf16[1024,640]{1,0:T(8,128)(2,1)}, bf16[1024,640]{1,0:T(8,128)(2,1)}, u32[]{:S(2)}, u32[]{:S(2)}) %collective-permute-start.8) | collective-permute-done | bytes 1310752 | tf_op jit(solution)/shard_map/ppermute | solution.py:225
  98.0 1.9 %collective-permute-start.9 = (bf16[1024,640]{1,0:T(8,128)(2,1)}, bf16[1024,640]{1,0:T(8,128)(2,1)}, u32[]{:S(2)}, u32[]{:S(2)}) collective-permute-start(bf16[1024,640]{1,0:T(8,128)(2,1)} %collective-permute-done.8.d2), channel_id=1, source_target_pairs={{0,128},{128,0},{1,129},{129,1},{2,130},{130,2},{3,131},{131,3},{4... | collective-permute-start | bytes 3932168 | tf_op jit(solution)/shard_map/ppermute | solution.py:221
  100.0 0.0 collective-permute-done.7.d1
  100.0 0.0 copy-start.6
  100.0 1.1 copy-done.6
  101.1 2.2 %collective-permute-done.9.d3 = bf16[1024,640]{1,0:T(8,128)(2,1)} collective-permute-done((bf16[1024,640]{1,0:T(8,128)(2,1)}, bf16[1024,640]{1,0:T(8,128)(2,1)}, u32[]{:S(2)}, u32[]{:S(2)}) %collective-permute-start.9) | collective-permute-done | bytes 1310752 | tf_op jit(solution)/shard_map/ppermute | solution.py:221
  103.3 6.7 %all-to-all-done.2.h_ref = bf16[8,256,512]{2,1,0:T(8,128)(2,1)S(1)} async-done(((bf16[8,256,512]{2,1,0:T(8,128)(2,1)}), bf16[8,256,512]{2,1,0:T(8,128)(2,1)S(1)}, u32[]{:S(2)}, u32[]{:S(2)}) %all-to-all-start.2) | async-done | bytes 2097184 | tf_op jit(solution)/shard_map/all_to_all | solution.py:212
  110.0 3.8 %shard_map.76 = bf16[256,640]{1,0:T(8,128)(2,1)S(1)} custom-call(bf16[8,256,512]{2,1,0:T(8,128)(2,1)S(1)} %all-to-all-done.2.h_ref, bf16[1024,640]{1,0:T(8,128)(2,1)} %bitcast.21, bf16[1024,640]{1,0:T(8,128)(2,1)} %copy-done.6, bf16[1024,640]{1,0:T(8,128)(2,1)} %collective-permute-done.8.d2, bf16[1024,640]{1,0:T(8,128)(2,1)} %collective-permute-done.9.d3), custom_call_target="tpu_custom_call" | custom-call | flops 1342177280 | bytes 7340032 | tf_op jit(solution)/shard_map/pallas_call | solution.py:192
  113.8 38.6 %all_to_all.20 = bf16[16,16,640]{2,1,0:T(8,128)(2,1)S(1)} all-to-all(bf16[16,16,640]{2,1,0:T(8,128)(2,1)S(1)} %bitcast.10), channel_id=1, replica_groups=mesh['xh'=2,'co'=2,'z'=16,'y'=4,'xl'=2] {'z'}, dimensions={0} | all-to-all | bytes 655360 | tf_op jit(solution)/shard_map/all_to_all | solution.py:217
  152.5 0.0 copy-done
  152.5 1.0 shard_map.77
  (7 shorter events, 0.0 us)
Async XLA Ops:
  0.0 44.7 %collective-permute-start.1 = (bf16[5120,128]{1,0:T(8,128)(2,1)}, bf16[5120,128]{1,0:T(8,128)(2,1)S(1)}, u32[]{:S(2)}, u32[]{:S(2)}) collective-permute-start(bf16[5120,128]{1,0:T(8,128)(2,1)} %bitcast.14), channel_id=1, source_target_pairs={{0,257},{1,256},{256,1},{257,0},{2,259},{3,258},{258,3},{259,2},{4... | collective-permute-start | bytes 3932168 | tf_op jit(solution)/shard_map/ppermute | solution.py:225
  3.4 41.4 %collective-permute-start.2 = (bf16[1024,640]{1,0:T(8,128)(2,1)}, bf16[1024,640]{1,0:T(8,128)(2,1)S(1)}, u32[]{:S(2)}, u32[]{:S(2)}) collective-permute-start(bf16[1024,640]{1,0:T(8,128)(2,1)} %bitcast.20), channel_id=1, source_target_pairs={{0,1},{1,0},{2,3},{3,2},{4,5},{5,4},{6,7},{7,6},{8,9},{9,8},{10,11... | collective-permute-start | bytes 3932168 | tf_op jit(solution)/shard_map/ppermute | solution.py:229
  9.1 35.6 %all-to-all-start = ((bf16[16,16,640]{2,1,0:T(8,128)(2,1)}), bf16[16,16,640]{2,1,0:T(8,128)(2,1)S(1)}, u32[]{:S(2)}, u32[]{:S(2)}) async-start(bf16[16,16,640]{2,1,0:T(8,128)(2,1)} %bitcast.13), calls=%async_computation | async-start | bytes 655360 | tf_op jit(solution)/shard_map/all_to_all | solution.py:217
  24.3 36.5 %collective-permute-start = (bf16[5120,128]{1,0:T(8,128)(2,1)}, bf16[5120,128]{1,0:T(8,128)(2,1)}, u32[]{:S(2)}, u32[]{:S(2)}) collective-permute-start(bf16[5120,128]{1,0:T(8,128)(2,1)} %bitcast.17), channel_id=1, source_target_pairs={{0,257},{1,256},{256,1},{257,0},{2,259},{3,258},{258,3},{259,2},{4... | collective-permute-start | bytes 3932168 | tf_op jit(solution)/shard_map/ppermute | solution.py:225
  44.7 2.0 %copy-start.2 = (bf16[5120,128]{1,0:T(8,128)(2,1)}, bf16[5120,128]{1,0:T(8,128)(2,1)S(1)}, u32[]{:S(2)}) copy-start(bf16[5120,128]{1,0:T(8,128)(2,1)S(1)} %collective-permute-done.1.rest_4_) | copy-start | bytes 3932164
  44.8 2.4 %copy-start.7 = (bf16[1024,640]{1,0:T(8,128)(2,1)}, bf16[1024,640]{1,0:T(8,128)(2,1)S(1)}, u32[]{:S(2)}) copy-start(bf16[1024,640]{1,0:T(8,128)(2,1)S(1)} %collective-permute-done.2) | copy-start | bytes 3932164
  47.2 31.1 %all-to-all-start.1 = ((bf16[8,272,640]{2,1,0:T(8,128)(2,1)}), bf16[8,272,640]{2,1,0:T(8,128)(2,1)S(1)}, u32[]{:S(2)}, u32[]{:S(2)}) async-start(bf16[8,272,640]{2,1,0:T(8,128)(2,1)} %shard_map.74), calls=%async_computation.1 | async-start | bytes 5570560 | tf_op jit(solution)/shard_map/all_to_all | solution.py:212
  53.0 15.6 %collective-permute-start.3 = (bf16[5120,128]{1,0:T(8,128)(2,1)}, bf16[5120,128]{1,0:T(8,128)(2,1)S(1)}, u32[]{:S(2)}, u32[]{:S(2)}) collective-permute-start(bf16[5120,128]{1,0:T(8,128)(2,1)} %bitcast.15), channel_id=1, source_target_pairs={{0,128},{128,0},{1,129},{129,1},{2,130},{130,2},{3,131},{131,3},{4... | collective-permute-start | bytes 3932168 | tf_op jit(solution)/shard_map/ppermute | solution.py:221
  54.9 13.7 %collective-permute-start.4 = (bf16[5120,128]{1,0:T(8,128)(2,1)}, bf16[5120,128]{1,0:T(8,128)(2,1)S(1)}, u32[]{:S(2)}, u32[]{:S(2)}) collective-permute-start(bf16[5120,128]{1,0:T(8,128)(2,1)} %bitcast.18), channel_id=1, source_target_pairs={{0,128},{128,0},{1,129},{129,1},{2,130},{130,2},{3,131},{131,3},{4... | collective-permute-start | bytes 3932168 | tf_op jit(solution)/shard_map/ppermute | solution.py:221
  60.8 7.8 %collective-permute-start.6 = (bf16[5120,128]{1,0:T(8,128)(2,1)}, bf16[5120,128]{1,0:T(8,128)(2,1)S(1)}, u32[]{:S(2)}, u32[]{:S(2)}) collective-permute-start(bf16[5120,128]{1,0:T(8,128)(2,1)} %collective-permute-done.rest_5_), channel_id=1, source_target_pairs={{0,128},{128,0},{1,129},{129,1},{2,130},{130,2},{3,131},{131,3},{4... | collective-permute-start | bytes 3932168 | tf_op jit(solution)/shard_map/ppermute | solution.py:221
  62.7 8.4 %collective-permute-start.5 = (bf16[5120,128]{1,0:T(8,128)(2,1)}, bf16[5120,128]{1,0:T(8,128)(2,1)}, u32[]{:S(2)}, u32[]{:S(2)}) collective-permute-start(bf16[5120,128]{1,0:T(8,128)(2,1)} %copy-done.2), channel_id=1, source_target_pairs={{0,128},{128,0},{1,129},{129,1},{2,130},{130,2},{3,131},{131,3},{4... | collective-permute-start | bytes 3932168 | tf_op jit(solution)/shard_map/ppermute | solution.py:221
  65.1 32.9 %collective-permute-start.8 = (bf16[1024,640]{1,0:T(8,128)(2,1)}, bf16[1024,640]{1,0:T(8,128)(2,1)}, u32[]{:S(2)}, u32[]{:S(2)}) collective-permute-start(bf16[1024,640]{1,0:T(8,128)(2,1)} %copy-done.7), channel_id=1, source_target_pairs={{0,257},{1,256},{256,1},{257,0},{2,259},{3,258},{258,3},{259,2},{4... | collective-permute-start | bytes 3932168 | tf_op jit(solution)/shard_map/ppermute | solution.py:225
  68.6 1.1 copy-start.3
  68.6 1.4 copy-start.4
  70.0 1.1 copy-start.5
  84.8 5.8 %copy-start.1 = (bf16[1,1024,640]{2,1,0:T(8,128)(2,1)S(1)}, bf16[1,1024,640]{2,1,0:T(8,128)(2,1)}, u32[]{:S(2)}) copy-start(bf16[1,1024,640]{2,1,0:T(8,128)(2,1)} %param.13) | copy-start | bytes 3932164
  84.8 25.2 %all-to-all-start.2 = ((bf16[8,256,512]{2,1,0:T(8,128)(2,1)}), bf16[8,256,512]{2,1,0:T(8,128)(2,1)S(1)}, u32[]{:S(2)}, u32[]{:S(2)}) async-start(bf16[8,256,512]{2,1,0:T(8,128)(2,1)} %shard_map.75), calls=%async_computation.2 | async-start | bytes 4194304 | tf_op jit(solution)/shard_map/all_to_all | solution.py:212
  90.6 61.8 %copy-start = (s32[128,1]{0,1:T(1,128)S(1)}, s32[128,1]{0,1:T(1,128)}, u32[]{:S(2)}) copy-start(s32[128,1]{0,1:T(1,128)} %param.10) | copy-start | bytes 1540
  90.6 9.3 %collective-permute-start.7 = (bf16[1024,640]{1,0:T(8,128)(2,1)S(1)}, bf16[1024,640]{1,0:T(8,128)(2,1)S(1)}, u32[]{:S(2)}, u32[]{:S(2)}) collective-permute-start(bf16[1024,640]{1,0:T(8,128)(2,1)S(1)} %bitcast.22), channel_id=1, source_target_pairs={{0,128},{128,0},{1,129},{129,1},{2,130},{130,2},{3,131},{131,3},{4... | collective-permute-start | bytes 3932168 | tf_op jit(solution)/shard_map/ppermute | solution.py:221
  98.0 5.3 %collective-permute-start.9 = (bf16[1024,640]{1,0:T(8,128)(2,1)}, bf16[1024,640]{1,0:T(8,128)(2,1)}, u32[]{:S(2)}, u32[]{:S(2)}) collective-permute-start(bf16[1024,640]{1,0:T(8,128)(2,1)} %collective-permute-done.8.d2), channel_id=1, source_target_pairs={{0,128},{128,0},{1,129},{129,1},{2,130},{130,2},{3,131},{131,3},{4... | collective-permute-start | bytes 3932168 | tf_op jit(solution)/shard_map/ppermute | solution.py:221
  100.0 1.1 copy-start.6

commit v8 on v7

--- a/solution.py
+++ b/solution.py
@@ -16,9 +16,9 @@
 TENSOR = 8
 EXTRA = 16
 VMEM = 28 * 1024 * 1024
-PIECES = 4
+PIECES = 2
 PER = TENSOR // PIECES
-DOWN_PIECES = 4
+DOWN_PIECES = 2
 TENSOR_AXES = ("y", "xl")
 
 
@@ -29,16 +29,29 @@
     return jnp.sum(jnp.where(i == j, row, 0), axis=1, keepdims=True), i, j
 
 
-def dispatch_kernel(ids_ref, tokens_ref, out_ref):
+def dispatch_kernel(ids_ref, tokens_ref, out_ref, held, made, sems):
+    inward = pltpu.make_async_copy(tokens_ref, held, sems.at[0])
+    inward.start()
     row = ids_ref[...]
     col, i, j = column_of(row)
     earlier = jnp.sum(jnp.where((col == row) & (i < j), 1, 0), axis=0, keepdims=True)
     placed = row * CAP + earlier
     slot = lax.broadcasted_iota(jnp.int32, (SLOTS, TOK), 0)
     placing = (slot == placed).astype(jnp.float32).astype(jnp.bfloat16)
-    out_ref[...] = jnp.dot(
-        placing, tokens_ref[...], preferred_element_type=jnp.float32
-    ).astype(jnp.bfloat16)
+    inward.wait()
+    half, outward = SLOTS // 2, []
+    for k in range(2):
+        made[k] = jnp.dot(
+            placing[half * k : half * k + half], held[...], preferred_element_type=jnp.float32
+        ).astype(jnp.bfloat16)
+        outward.append(
+            pltpu.make_async_copy(
+                made.at[k], out_ref.at[pl.ds(half * k, half)], sems.at[1 + k]
+            )
+        )
+        outward[k].start()
+    for copy in outward:
+        copy.wait()
 
 
 def combine_kernel(ids_ref, back_ref, out_ref):
@@ -249,8 +262,16 @@
     gate, upper, down = gate_proj[0], up_proj[0], down_proj[0]
 
     outgoing = pl.pallas_call(
-        dispatch_kernel, out_shape=jax.ShapeDtypeStruct((SLOTS, FEAT), jnp.bfloat16)
-    )(ids, tokens)
+        dispatch_kernel,
+        in_specs=[IN_VMEM, IN_HBM],
+        out_specs=IN_HBM,
+        out_shape=pltpu.HBM((SLOTS, FEAT), jnp.bfloat16),
+        scratch_shapes=[
+            pltpu.VMEM((TOK, FEAT), jnp.bfloat16),
+            pltpu.VMEM((2, SLOTS // 2, FEAT), jnp.bfloat16),
+            pltpu.SemaphoreType.DMA((3,)),
+        ],
+    )(ids, *left_in_hbm((tokens,)))
     pair = (gate, upper)
     arrived, gate_far, down_sent, token = tied(
         over_experts(outgoing), across_border(gate), across_pair(down), ids

time: 154 us -> 155 us (level)
    ppermute x3, waiting for transfers between devices: 8.85 us -> 7.14 us  [across_border(): return lax.ppermute(array, ('xh', 'xl'), [(i, 3 - i) for i in range(4)])]
where the time goes in v8:
time: 155 us
  starting transfers between devices  51.9 us (33%)
  waiting for transfers between devices  41.1 us (27%)
  blocking collectives  39.2 us (25%)
  Pallas kernels  16.3 us (11%)
  local copies, waits for them, and re-layouts  4.32 us (3%)
  other arithmetic  1.59 us (1%)
    all_to_all x1, blocking collectives, over_experts(): return lax.all_to_all(parts, 'z', 0, 0, tiled=True).reshape(SLOTS, FEAT)  39.2 us
    all_to_all x1, waiting for transfers between devices, over_experts(): return lax.all_to_all(parts, 'z', 0, 0, tiled=True).reshape(SLOTS, FEAT)  16.8 us
    all_to_all x1, starting transfers between devices, over_experts(): return lax.all_to_all(parts, 'z', 0, 0, tiled=True).reshape(SLOTS, FEAT)  15.2 us
    all_to_all x2, waiting for transfers between devices, gathered(): return lax.all_to_all(copies, TENSOR_AXES, 0, 0, tiled=True)  15 us
    ppermute x6, starting transfers between devices, other_core(): return lax.ppermute(array, 'co', [(0, 1), (1, 0)])  12.6 us
    all_to_all x2, starting transfers between devices, gathered(): return lax.all_to_all(copies, TENSOR_AXES, 0, 0, tiled=True)  11.6 us
    ppermute x3, starting transfers between devices, across_border(): return lax.ppermute(array, ('xh', 'xl'), [(i, 3 - i) for i in range(4)])  8.71 us
    pallas_call x1, Pallas kernels, hidden_copies(): pl.pallas_call(hidden_kernel, in_specs=[IN_VMEM] + [IN_HBM] * len(weights...  7.18 us
  transfers between devices with their start and end apart: 13, of which 6 were waited for; matrix products, arithmetic and copies ran while one was open for 1% of the time, Pallas kernels for 7%

profile of v8, /device:TPU:10, one launch (start us, length us, event | category | flops | bytes accessed | tf_op | source)
XLA Modules:
  0.0 154.6 jit_solution(7221162931214140555)
XLA Ops:
  0.0 3.4 %collective-permute-start.1 = (bf16[5120,128]{1,0:T(8,128)(2,1)}, bf16[5120,128]{1,0:T(8,128)(2,1)S(1)}, u32[]{:S(2)}, u32[]{:S(2)}) collective-permute-start(bf16[5120,128]{1,0:T(8,128)(2,1)} %bitcast.14), channel_id=1, source_target_pairs={{0,257},{1,256},{256,1},{257,0},{2,259},{3,258},{258,3},{259,2},{4... | collective-permute-start | bytes 3932168 | tf_op jit(solution)/shard_map/ppermute | solution.py:238
  3.4 3.7 %collective-permute-start.2 = (bf16[1024,640]{1,0:T(8,128)(2,1)}, bf16[1024,640]{1,0:T(8,128)(2,1)S(1)}, u32[]{:S(2)}, u32[]{:S(2)}) collective-permute-start(bf16[1024,640]{1,0:T(8,128)(2,1)} %bitcast.20), channel_id=1, source_target_pairs={{0,1},{1,0},{2,3},{3,2},{4,5},{5,4},{6,7},{7,6},{8,9},{9,8},{10,11... | collective-permute-start | bytes 3932168 | tf_op jit(solution)/shard_map/ppermute | solution.py:242
  7.1 2.5 %shard_map.73 = bf16[256,640]{1,0:T(8,128)(2,1)} custom-call(s32[1,128]{1,0:T(1,128)} %bitcast.11, bf16[128,640]{1,0:T(8,128)(2,1)} %tokens_ref.1), custom_call_target="tpu_custom_call" | custom-call | tf_op jit(solution)/shard_map/pallas_call | solution.py:264
  9.6 15.2 %all-to-all-start = ((bf16[16,16,640]{2,1,0:T(8,128)(2,1)}), bf16[16,16,640]{2,1,0:T(8,128)(2,1)S(1)}, u32[]{:S(2)}, u32[]{:S(2)}) async-start(bf16[16,16,640]{2,1,0:T(8,128)(2,1)} %bitcast.13), calls=%async_computation | async-start | bytes 655360 | tf_op jit(solution)/shard_map/all_to_all | solution.py:230
  24.9 1.9 %collective-permute-start = (bf16[5120,128]{1,0:T(8,128)(2,1)}, bf16[5120,128]{1,0:T(8,128)(2,1)}, u32[]{:S(2)}, u32[]{:S(2)}) collective-permute-start(bf16[5120,128]{1,0:T(8,128)(2,1)} %bitcast.17), channel_id=1, source_target_pairs={{0,257},{1,256},{256,1},{257,0},{2,259},{3,258},{258,3},{259,2},{4... | collective-permute-start | bytes 3932168 | tf_op jit(solution)/shard_map/ppermute | solution.py:238
  26.8 0.8 subtract_convert_fusion
  27.6 0.8 select_reduce_fusion
  28.5 0.1 stack.24.side_ref
  28.5 16.8 %all-to-all-done = bf16[16,16,640]{2,1,0:T(8,128)(2,1)S(1)} async-done(((bf16[16,16,640]{2,1,0:T(8,128)(2,1)}), bf16[16,16,640]{2,1,0:T(8,128)(2,1)S(1)}, u32[]{:S(2)}, u32[]{:S(2)}) %all-to-all-start) | async-done | bytes 327712 | tf_op jit(solution)/shard_map/all_to_all | solution.py:230
  45.3 0.0 collective-permute-done.1.rest_4_
  45.3 0.0 copy-start.2
  45.3 0.0 collective-permute-done.2
  45.3 0.0 copy-start.7
  45.3 1.8 %shard_map.74 = bf16[8,272,640]{2,1,0:T(8,128)(2,1)} custom-call(bf16[256,640]{1,0:T(8,128)(2,1)S(1)} %bitcast.8, bf16[16,640]{1,0:T(8,128)(2,1)S(1)} %stack.24.side_ref), custom_call_target="tpu_custom_call" | custom-call | tf_op jit(solution)/shard_map/pallas_call | solution.py:194
  47.1 0.2 copy-done.2
  47.3 0.4 copy-done.7
  47.7 5.8 %all-to-all-start.1 = ((bf16[8,272,640]{2,1,0:T(8,128)(2,1)}), bf16[8,272,640]{2,1,0:T(8,128)(2,1)S(1)}, u32[]{:S(2)}, u32[]{:S(2)}) async-start(bf16[8,272,640]{2,1,0:T(8,128)(2,1)} %shard_map.74), calls=%async_computation.1 | async-start | bytes 5570560 | tf_op jit(solution)/shard_map/all_to_all | solution.py:225
  53.5 1.9 %collective-permute-start.3 = (bf16[5120,128]{1,0:T(8,128)(2,1)}, bf16[5120,128]{1,0:T(8,128)(2,1)S(1)}, u32[]{:S(2)}, u32[]{:S(2)}) collective-permute-start(bf16[5120,128]{1,0:T(8,128)(2,1)} %bitcast.15), channel_id=1, source_target_pairs={{0,128},{128,0},{1,129},{129,1},{2,130},{130,2},{3,131},{131,3},{4... | collective-permute-start | bytes 3932168 | tf_op jit(solution)/shard_map/ppermute | solution.py:234
  55.4 2.4 %collective-permute-start.4 = (bf16[5120,128]{1,0:T(8,128)(2,1)}, bf16[5120,128]{1,0:T(8,128)(2,1)S(1)}, u32[]{:S(2)}, u32[]{:S(2)}) collective-permute-start(bf16[5120,128]{1,0:T(8,128)(2,1)} %bitcast.18), channel_id=1, source_target_pairs={{0,128},{128,0},{1,129},{129,1},{2,130},{130,2},{3,131},{131,3},{4... | collective-permute-start | bytes 3932168 | tf_op jit(solution)/shard_map/ppermute | solution.py:234
  57.9 3.0 %collective-permute-done.rest_5_ = bf16[5120,128]{1,0:T(8,128)(2,1)} collective-permute-done((bf16[5120,128]{1,0:T(8,128)(2,1)}, bf16[5120,128]{1,0:T(8,128)(2,1)}, u32[]{:S(2)}, u32[]{:S(2)}) %collective-permute-start) | collective-permute-done | bytes 1310752 | tf_op jit(solution)/shard_map/ppermute | solution.py:238
  60.8 1.9 %collective-permute-start.6 = (bf16[5120,128]{1,0:T(8,128)(2,1)}, bf16[5120,128]{1,0:T(8,128)(2,1)S(1)}, u32[]{:S(2)}, u32[]{:S(2)}) collective-permute-start(bf16[5120,128]{1,0:T(8,128)(2,1)} %collective-permute-done.rest_5_), channel_id=1, source_target_pairs={{0,128},{128,0},{1,129},{129,1},{2,130},{130,2},{3,131},{131,3},{4... | collective-permute-start | bytes 3932168 | tf_op jit(solution)/shard_map/ppermute | solution.py:234
  62.7 2.4 %collective-permute-start.5 = (bf16[5120,128]{1,0:T(8,128)(2,1)}, bf16[5120,128]{1,0:T(8,128)(2,1)}, u32[]{:S(2)}, u32[]{:S(2)}) collective-permute-start(bf16[5120,128]{1,0:T(8,128)(2,1)} %copy-done.2), channel_id=1, source_target_pairs={{0,128},{128,0},{1,129},{129,1},{2,130},{130,2},{3,131},{131,3},{4... | collective-permute-start | bytes 3932168 | tf_op jit(solution)/shard_map/ppermute | solution.py:234
  65.1 3.4 %collective-permute-start.8 = (bf16[1024,640]{1,0:T(8,128)(2,1)}, bf16[1024,640]{1,0:T(8,128)(2,1)}, u32[]{:S(2)}, u32[]{:S(2)}) collective-permute-start(bf16[1024,640]{1,0:T(8,128)(2,1)} %copy-done.7), channel_id=1, source_target_pairs={{0,257},{1,256},{256,1},{257,0},{2,259},{3,258},{258,3},{259,2},{4... | collective-permute-start | bytes 3932168 | tf_op jit(solution)/shard_map/ppermute | solution.py:238
  68.5 0.0 collective-permute-done.3.rest_2_
  68.6 0.0 copy-start.3
  68.6 0.0 collective-permute-done.4.rest_3_
  68.6 0.0 copy-start.4
  68.6 0.0 collective-permute-done.6.rest_7_
  68.6 1.1 copy-done.3
  69.7 0.4 copy-done.4
  70.0 0.0 copy-start.5
  70.0 1.1 copy-done.5
  71.1 0.0 collective-permute-done.5.rest_6_
  71.2 7.6 %all-to-all-done.1.x_ref = bf16[8,272,640]{2,1,0:T(8,128)(2,1)S(1)} async-done(((bf16[8,272,640]{2,1,0:T(8,128)(2,1)}), bf16[8,272,640]{2,1,0:T(8,128)(2,1)S(1)}, u32[]{:S(2)}, u32[]{:S(2)}) %all-to-all-start.1) | async-done | bytes 2785312 | tf_op jit(solution)/shard_map/all_to_all | solution.py:225
  78.8 7.2 %shard_map.75 = bf16[8,256,512]{2,1,0:T(8,128)(2,1)} custom-call(bf16[8,272,640]{2,1,0:T(8,128)(2,1)S(1)} %all-to-all-done.1.x_ref, bf16[5120,128]{1,0:T(8,128)(2,1)} %bitcast.16, bf16[5120,128]{1,0:T(8,128)(2,1)} %bitcast.19, bf16[5120,128]{1,0:T(8,128)(2,1)} %copy-done.3, bf16[5120,128]{1,0:T(8,128)(2,1)} %copy-done.4, bf16[5120,128]{1,0:T(8,128)(2,1)} %copy-done.2, ...), custom_call_target="tpu_custom_call" | custom-call | flops 2684354560 | bytes 13107200 | tf_op jit(solution)/shard_map/pallas_call | solution.py:159
  86.0 0.0 copy-start.1
  86.0 5.8 %all-to-all-start.2 = ((bf16[8,256,512]{2,1,0:T(8,128)(2,1)}), bf16[8,256,512]{2,1,0:T(8,128)(2,1)S(1)}, u32[]{:S(2)}, u32[]{:S(2)}) async-start(bf16[8,256,512]{2,1,0:T(8,128)(2,1)} %shard_map.75), calls=%async_computation.2 | async-start | bytes 4194304 | tf_op jit(solution)/shard_map/all_to_all | solution.py:225
  91.8 0.0 copy-done.1
  91.8 0.0 copy-start
  91.8 2.0 %collective-permute-start.7 = (bf16[1024,640]{1,0:T(8,128)(2,1)S(1)}, bf16[1024,640]{1,0:T(8,128)(2,1)S(1)}, u32[]{:S(2)}, u32[]{:S(2)}) collective-permute-start(bf16[1024,640]{1,0:T(8,128)(2,1)S(1)} %bitcast.22), channel_id=1, source_target_pairs={{0,128},{128,0},{1,129},{129,1},{2,130},{130,2},{3,131},{131,3},{4... | collective-permute-start | bytes 3932168 | tf_op jit(solution)/shard_map/ppermute | solution.py:234
  93.9 4.2 %collective-permute-done.8.d2 = bf16[1024,640]{1,0:T(8,128)(2,1)} collective-permute-done((bf16[1024,640]{1,0:T(8,128)(2,1)}, bf16[1024,640]{1,0:T(8,128)(2,1)}, u32[]{:S(2)}, u32[]{:S(2)}) %collective-permute-start.8) | collective-permute-done | bytes 1310752 | tf_op jit(solution)/shard_map/ppermute | solution.py:238
  98.0 1.9 %collective-permute-start.9 = (bf16[1024,640]{1,0:T(8,128)(2,1)}, bf16[1024,640]{1,0:T(8,128)(2,1)}, u32[]{:S(2)}, u32[]{:S(2)}) collective-permute-start(bf16[1024,640]{1,0:T(8,128)(2,1)} %collective-permute-done.8.d2), channel_id=1, source_target_pairs={{0,128},{128,0},{1,129},{129,1},{2,130},{130,2},{3,131},{131,3},{4... | collective-permute-start | bytes 3932168 | tf_op jit(solution)/shard_map/ppermute | solution.py:234
  100.0 0.0 collective-permute-done.7.d1
  100.0 0.0 copy-start.6
  100.0 1.1 copy-done.6
  101.1 2.2 %collective-permute-done.9.d3 = bf16[1024,640]{1,0:T(8,128)(2,1)} collective-permute-done((bf16[1024,640]{1,0:T(8,128)(2,1)}, bf16[1024,640]{1,0:T(8,128)(2,1)}, u32[]{:S(2)}, u32[]{:S(2)}) %collective-permute-start.9) | collective-permute-done | bytes 1310752 | tf_op jit(solution)/shard_map/ppermute | solution.py:234
  103.3 7.3 %all-to-all-done.2.h_ref = bf16[8,256,512]{2,1,0:T(8,128)(2,1)S(1)} async-done(((bf16[8,256,512]{2,1,0:T(8,128)(2,1)}), bf16[8,256,512]{2,1,0:T(8,128)(2,1)S(1)}, u32[]{:S(2)}, u32[]{:S(2)}) %all-to-all-start.2) | async-done | bytes 2097184 | tf_op jit(solution)/shard_map/all_to_all | solution.py:225
  110.6 3.8 %shard_map.76 = bf16[256,640]{1,0:T(8,128)(2,1)S(1)} custom-call(bf16[8,256,512]{2,1,0:T(8,128)(2,1)S(1)} %all-to-all-done.2.h_ref, bf16[1024,640]{1,0:T(8,128)(2,1)} %bitcast.21, bf16[1024,640]{1,0:T(8,128)(2,1)} %copy-done.6, bf16[1024,640]{1,0:T(8,128)(2,1)} %collective-permute-done.8.d2, bf16[1024,640]{1,0:T(8,128)(2,1)} %collective-permute-done.9.d3), custom_call_target="tpu_custom_call" | custom-call | flops 1342177280 | bytes 7340032 | tf_op jit(solution)/shard_map/pallas_call | solution.py:205
  114.4 39.2 %all_to_all.20 = bf16[16,16,640]{2,1,0:T(8,128)(2,1)S(1)} all-to-all(bf16[16,16,640]{2,1,0:T(8,128)(2,1)S(1)} %bitcast.10), channel_id=1, replica_groups=mesh['xh'=2,'co'=2,'z'=16,'y'=4,'xl'=2] {'z'}, dimensions={0} | all-to-all | bytes 655360 | tf_op jit(solution)/shard_map/all_to_all | solution.py:230
  153.6 0.0 copy-done
  153.6 1.0 shard_map.77
  (7 shorter events, 0.0 us)
Async XLA Ops:
  0.0 45.3 %collective-permute-start.1 = (bf16[5120,128]{1,0:T(8,128)(2,1)}, bf16[5120,128]{1,0:T(8,128)(2,1)S(1)}, u32[]{:S(2)}, u32[]{:S(2)}) collective-permute-start(bf16[5120,128]{1,0:T(8,128)(2,1)} %bitcast.14), channel_id=1, source_target_pairs={{0,257},{1,256},{256,1},{257,0},{2,259},{3,258},{258,3},{259,2},{4... | collective-permute-start | bytes 3932168 | tf_op jit(solution)/shard_map/ppermute | solution.py:238
  3.4 41.9 %collective-permute-start.2 = (bf16[1024,640]{1,0:T(8,128)(2,1)}, bf16[1024,640]{1,0:T(8,128)(2,1)S(1)}, u32[]{:S(2)}, u32[]{:S(2)}) collective-permute-start(bf16[1024,640]{1,0:T(8,128)(2,1)} %bitcast.20), channel_id=1, source_target_pairs={{0,1},{1,0},{2,3},{3,2},{4,5},{5,4},{6,7},{7,6},{8,9},{9,8},{10,11... | collective-permute-start | bytes 3932168 | tf_op jit(solution)/shard_map/ppermute | solution.py:242
  9.6 35.6 %all-to-all-start = ((bf16[16,16,640]{2,1,0:T(8,128)(2,1)}), bf16[16,16,640]{2,1,0:T(8,128)(2,1)S(1)}, u32[]{:S(2)}, u32[]{:S(2)}) async-start(bf16[16,16,640]{2,1,0:T(8,128)(2,1)} %bitcast.13), calls=%async_computation | async-start | bytes 655360 | tf_op jit(solution)/shard_map/all_to_all | solution.py:230
  24.9 35.9 %collective-permute-start = (bf16[5120,128]{1,0:T(8,128)(2,1)}, bf16[5120,128]{1,0:T(8,128)(2,1)}, u32[]{:S(2)}, u32[]{:S(2)}) collective-permute-start(bf16[5120,128]{1,0:T(8,128)(2,1)} %bitcast.17), channel_id=1, source_target_pairs={{0,257},{1,256},{256,1},{257,0},{2,259},{3,258},{258,3},{259,2},{4... | collective-permute-start | bytes 3932168 | tf_op jit(solution)/shard_map/ppermute | solution.py:238
  45.3 2.0 %copy-start.2 = (bf16[5120,128]{1,0:T(8,128)(2,1)}, bf16[5120,128]{1,0:T(8,128)(2,1)S(1)}, u32[]{:S(2)}) copy-start(bf16[5120,128]{1,0:T(8,128)(2,1)S(1)} %collective-permute-done.1.rest_4_) | copy-start | bytes 3932164
  45.3 2.4 %copy-start.7 = (bf16[1024,640]{1,0:T(8,128)(2,1)}, bf16[1024,640]{1,0:T(8,128)(2,1)S(1)}, u32[]{:S(2)}) copy-start(bf16[1024,640]{1,0:T(8,128)(2,1)S(1)} %collective-permute-done.2) | copy-start | bytes 3932164
  47.7 31.1 %all-to-all-start.1 = ((bf16[8,272,640]{2,1,0:T(8,128)(2,1)}), bf16[8,272,640]{2,1,0:T(8,128)(2,1)S(1)}, u32[]{:S(2)}, u32[]{:S(2)}) async-start(bf16[8,272,640]{2,1,0:T(8,128)(2,1)} %shard_map.74), calls=%async_computation.1 | async-start | bytes 5570560 | tf_op jit(solution)/shard_map/all_to_all | solution.py:225
  53.5 15.0 %collective-permute-start.3 = (bf16[5120,128]{1,0:T(8,128)(2,1)}, bf16[5120,128]{1,0:T(8,128)(2,1)S(1)}, u32[]{:S(2)}, u32[]{:S(2)}) collective-permute-start(bf16[5120,128]{1,0:T(8,128)(2,1)} %bitcast.15), channel_id=1, source_target_pairs={{0,128},{128,0},{1,129},{129,1},{2,130},{130,2},{3,131},{131,3},{4... | collective-permute-start | bytes 3932168 | tf_op jit(solution)/shard_map/ppermute | solution.py:234
  55.4 13.1 %collective-permute-start.4 = (bf16[5120,128]{1,0:T(8,128)(2,1)}, bf16[5120,128]{1,0:T(8,128)(2,1)S(1)}, u32[]{:S(2)}, u32[]{:S(2)}) collective-permute-start(bf16[5120,128]{1,0:T(8,128)(2,1)} %bitcast.18), channel_id=1, source_target_pairs={{0,128},{128,0},{1,129},{129,1},{2,130},{130,2},{3,131},{131,3},{4... | collective-permute-start | bytes 3932168 | tf_op jit(solution)/shard_map/ppermute | solution.py:234
  60.8 7.8 %collective-permute-start.6 = (bf16[5120,128]{1,0:T(8,128)(2,1)}, bf16[5120,128]{1,0:T(8,128)(2,1)S(1)}, u32[]{:S(2)}, u32[]{:S(2)}) collective-permute-start(bf16[5120,128]{1,0:T(8,128)(2,1)} %collective-permute-done.rest_5_), channel_id=1, source_target_pairs={{0,128},{128,0},{1,129},{129,1},{2,130},{130,2},{3,131},{131,3},{4... | collective-permute-start | bytes 3932168 | tf_op jit(solution)/shard_map/ppermute | solution.py:234
  62.7 8.4 %collective-permute-start.5 = (bf16[5120,128]{1,0:T(8,128)(2,1)}, bf16[5120,128]{1,0:T(8,128)(2,1)}, u32[]{:S(2)}, u32[]{:S(2)}) collective-permute-start(bf16[5120,128]{1,0:T(8,128)(2,1)} %copy-done.2), channel_id=1, source_target_pairs={{0,128},{128,0},{1,129},{129,1},{2,130},{130,2},{3,131},{131,3},{4... | collective-permute-start | bytes 3932168 | tf_op jit(solution)/shard_map/ppermute | solution.py:234
  65.1 32.9 %collective-permute-start.8 = (bf16[1024,640]{1,0:T(8,128)(2,1)}, bf16[1024,640]{1,0:T(8,128)(2,1)}, u32[]{:S(2)}, u32[]{:S(2)}) collective-permute-start(bf16[1024,640]{1,0:T(8,128)(2,1)} %copy-done.7), channel_id=1, source_target_pairs={{0,257},{1,256},{256,1},{257,0},{2,259},{3,258},{258,3},{259,2},{4... | collective-permute-start | bytes 3932168 | tf_op jit(solution)/shard_map/ppermute | solution.py:238
  68.6 1.1 copy-start.3
  68.6 1.4 copy-start.4
  70.0 1.1 copy-start.5
  86.0 5.8 %copy-start.1 = (bf16[1,1024,640]{2,1,0:T(8,128)(2,1)S(1)}, bf16[1,1024,640]{2,1,0:T(8,128)(2,1)}, u32[]{:S(2)}) copy-start(bf16[1,1024,640]{2,1,0:T(8,128)(2,1)} %param.13) | copy-start | bytes 3932164
  86.0 24.7 %all-to-all-start.2 = ((bf16[8,256,512]{2,1,0:T(8,128)(2,1)}), bf16[8,256,512]{2,1,0:T(8,128)(2,1)S(1)}, u32[]{:S(2)}, u32[]{:S(2)}) async-start(bf16[8,256,512]{2,1,0:T(8,128)(2,1)} %shard_map.75), calls=%async_computation.2 | async-start | bytes 4194304 | tf_op jit(solution)/shard_map/all_to_all | solution.py:225
  91.8 61.8 %copy-start = (s32[128,1]{0,1:T(1,128)S(1)}, s32[128,1]{0,1:T(1,128)}, u32[]{:S(2)}) copy-start(s32[128,1]{0,1:T(1,128)} %param.10) | copy-start | bytes 1540
  91.8 8.2 %collective-permute-start.7 = (bf16[1024,640]{1,0:T(8,128)(2,1)S(1)}, bf16[1024,640]{1,0:T(8,128)(2,1)S(1)}, u32[]{:S(2)}, u32[]{:S(2)}) collective-permute-start(bf16[1024,640]{1,0:T(8,128)(2,1)S(1)} %bitcast.22), channel_id=1, source_target_pairs={{0,128},{128,0},{1,129},{129,1},{2,130},{130,2},{3,131},{131,3},{4... | collective-permute-start | bytes 3932168 | tf_op jit(solution)/shard_map/ppermute | solution.py:234
  98.0 5.3 %collective-permute-start.9 = (bf16[1024,640]{1,0:T(8,128)(2,1)}, bf16[1024,640]{1,0:T(8,128)(2,1)}, u32[]{:S(2)}, u32[]{:S(2)}) collective-permute-start(bf16[1024,640]{1,0:T(8,128)(2,1)} %collective-permute-done.8.d2), channel_id=1, source_target_pairs={{0,128},{128,0},{1,129},{129,1},{2,130},{130,2},{3,131},{131,3},{4... | collective-permute-start | bytes 3932168 | tf_op jit(solution)/shard_map/ppermute | solution.py:234
  100.0 1.1 copy-start.6

commit v9 on v7

--- a/solution.py
+++ b/solution.py
@@ -73,10 +73,10 @@
     return lambda piece: [c.wait() for c in copies[len(sources) * piece :][: len(sources)]]
 
 
-def weighed(held, piece):
+def weighed(held, piece, places):
     depth = PER * FEAT
     return jnp.concatenate(
-        [held[k, piece * depth : (piece + 1) * depth, :] for k in range(8)], axis=1
+        [held[k, piece * depth : (piece + 1) * depth, :] for k in places], axis=1
     )
 
 
@@ -91,22 +91,30 @@
             squares += jnp.sum(rows * rows, axis=1, keepdims=True)
             logit += jnp.sum(values * router, axis=1, keepdims=True)
             parts.append(values.astype(jnp.bfloat16))
+        values = jnp.concatenate(parts, axis=1)
         wait(piece)
-        term = jnp.dot(
-            jnp.concatenate(parts, axis=1), weighed(held, piece), preferred_element_type=jnp.float32
-        )
-        acc[...] = term if piece == 0 else acc[...] + term
+        if piece < PIECES - 1:
+            term = jnp.dot(
+                values, weighed(held, piece, range(8)), preferred_element_type=jnp.float32
+            )
+            acc[...] = term if piece == 0 else acc[...] + term
     rstd = lax.rsqrt(squares / D + EPSILON)
     scale = rstd * jax.nn.sigmoid(logit * rstd)
-    for k in range(4):
-        gate = acc[:, 256 * k : 256 * k + 128] * scale
-        upper = acc[:, 256 * k + 128 : 256 * k + 256] * scale
-        made[:, 128 * k : 128 * k + 128] = (jax.nn.silu(gate) * upper).astype(jnp.bfloat16)
-    copies = [
-        pltpu.make_async_copy(made, out_ref.at[k], out_sems.at[k]) for k in range(TENSOR)
-    ]
-    for copy in copies:
-        copy.start()
+    copies = []
+    for q in range(4):
+        term = acc[:, 256 * q : 256 * q + 256] + jnp.dot(
+            values,
+            weighed(held, PIECES - 1, (2 * q, 2 * q + 1)),
+            preferred_element_type=jnp.float32,
+        )
+        gate, upper = term[:, :128] * scale, term[:, 128:] * scale
+        made[q] = (jax.nn.silu(gate) * upper).astype(jnp.bfloat16)
+        for k in range(TENSOR):
+            copy = pltpu.make_async_copy(
+                made.at[q], out_ref.at[k, :, pl.ds(128 * q, 128)], out_sems.at[q, k]
+            )
+            copy.start()
+            copies.append(copy)
     for copy in copies:
         copy.wait()
 
@@ -151,9 +159,9 @@
         scratch_shapes=[
             pltpu.VMEM((8, D, 128), jnp.bfloat16),
             pltpu.VMEM((SLOTS, 1024), jnp.float32),
-            pltpu.VMEM((SLOTS, 512), jnp.bfloat16),
+            pltpu.VMEM((4, SLOTS, 128), jnp.bfloat16),
             pltpu.SemaphoreType.DMA((PIECES, 8)),
-            pltpu.SemaphoreType.DMA((TENSOR,)),
+            pltpu.SemaphoreType.DMA((4, TENSOR)),
         ],
         compiler_params=PARAMS,
         cost_estimate=pl.CostEstimate(

time: 154 us -> 154 us (level)
  no operation moved by 1% of the time
where the time goes in v9:
time: 154 us; the launch traced here: 153 us
  starting transfers between devices  51.9 us (34%)
  waiting for transfers between devices  41.6 us (27%)
  blocking collectives  38.6 us (25%)
  Pallas kernels  15.1 us (10%)
  local copies, waits for them, and re-layouts  4.32 us (3%)
  other arithmetic  1.59 us (1%)
    all_to_all x1, blocking collectives, over_experts(): return lax.all_to_all(parts, 'z', 0, 0, tiled=True).reshape(SLOTS, FEAT)  38.6 us
    all_to_all x1, waiting for transfers between devices, over_experts(): return lax.all_to_all(parts, 'z', 0, 0, tiled=True).reshape(SLOTS, FEAT)  16.8 us
    all_to_all x1, starting transfers between devices, over_experts(): return lax.all_to_all(parts, 'z', 0, 0, tiled=True).reshape(SLOTS, FEAT)  15.2 us
    all_to_all x2, waiting for transfers between devices, gathered(): return lax.all_to_all(copies, TENSOR_AXES, 0, 0, tiled=True)  13.7 us
    ppermute x6, starting transfers between devices, other_core(): return lax.ppermute(array, 'co', [(0, 1), (1, 0)])  12.6 us
    all_to_all x2, starting transfers between devices, gathered(): return lax.all_to_all(copies, TENSOR_AXES, 0, 0, tiled=True)  11.6 us
    ppermute x3, waiting for transfers between devices, across_border(): return lax.ppermute(array, ('xh', 'xl'), [(i, 3 - i) for i in range(4)])  8.95 us
    ppermute x3, starting transfers between devices, across_border(): return lax.ppermute(array, ('xh', 'xl'), [(i, 3 - i) for i in range(4)])  8.71 us
  transfers between devices with their start and end apart: 13, of which 6 were waited for; matrix products, arithmetic and copies ran while one was open for 1% of the time, Pallas kernels for 7%

profile of v9, /device:TPU:10, one launch (start us, length us, event | category | flops | bytes accessed | tf_op | source)
XLA Modules:
  0.0 153.4 jit_solution(14952329053314648622)
XLA Ops:
  0.0 3.4 %collective-permute-start.1 = (bf16[5120,128]{1,0:T(8,128)(2,1)}, bf16[5120,128]{1,0:T(8,128)(2,1)S(1)}, u32[]{:S(2)}, u32[]{:S(2)}) collective-permute-start(bf16[5120,128]{1,0:T(8,128)(2,1)} %bitcast.14), channel_id=1, source_target_pairs={{0,257},{1,256},{256,1},{257,0},{2,259},{3,258},{258,3},{259,2},{4... | collective-permute-start | bytes 3932168 | tf_op jit(solution)/shard_map/ppermute | solution.py:233
  3.4 3.7 %collective-permute-start.2 = (bf16[1024,640]{1,0:T(8,128)(2,1)}, bf16[1024,640]{1,0:T(8,128)(2,1)S(1)}, u32[]{:S(2)}, u32[]{:S(2)}) collective-permute-start(bf16[1024,640]{1,0:T(8,128)(2,1)} %bitcast.20), channel_id=1, source_target_pairs={{0,1},{1,0},{2,3},{3,2},{4,5},{5,4},{6,7},{7,6},{8,9},{9,8},{10,11... | collective-permute-start | bytes 3932168 | tf_op jit(solution)/shard_map/ppermute | solution.py:237
  7.1 2.0 %shard_map.73 = bf16[256,640]{1,0:T(8,128)(2,1)} custom-call(s32[1,128]{1,0:T(1,128)} %bitcast.11, bf16[128,640]{1,0:T(8,128)(2,1)} %tokens_ref.1), custom_call_target="tpu_custom_call" | custom-call | tf_op jit(solution)/shard_map/pallas_call | solution.py:259
  9.1 15.2 %all-to-all-start = ((bf16[16,16,640]{2,1,0:T(8,128)(2,1)}), bf16[16,16,640]{2,1,0:T(8,128)(2,1)S(1)}, u32[]{:S(2)}, u32[]{:S(2)}) async-start(bf16[16,16,640]{2,1,0:T(8,128)(2,1)} %bitcast.13), calls=%async_computation | async-start | bytes 655360 | tf_op jit(solution)/shard_map/all_to_all | solution.py:225
  24.3 1.9 %collective-permute-start = (bf16[5120,128]{1,0:T(8,128)(2,1)}, bf16[5120,128]{1,0:T(8,128)(2,1)}, u32[]{:S(2)}, u32[]{:S(2)}) collective-permute-start(bf16[5120,128]{1,0:T(8,128)(2,1)} %bitcast.17), channel_id=1, source_target_pairs={{0,257},{1,256},{256,1},{257,0},{2,259},{3,258},{258,3},{259,2},{4... | collective-permute-start | bytes 3932168 | tf_op jit(solution)/shard_map/ppermute | solution.py:233
  26.3 0.8 subtract_convert_fusion
  27.1 0.8 select_reduce_fusion
  27.9 0.1 stack.24.side_ref
  28.0 16.8 %all-to-all-done = bf16[16,16,640]{2,1,0:T(8,128)(2,1)S(1)} async-done(((bf16[16,16,640]{2,1,0:T(8,128)(2,1)}), bf16[16,16,640]{2,1,0:T(8,128)(2,1)S(1)}, u32[]{:S(2)}, u32[]{:S(2)}) %all-to-all-start) | async-done | bytes 327712 | tf_op jit(solution)/shard_map/all_to_all | solution.py:225
  44.7 0.0 collective-permute-done.1.rest_4_
  44.7 0.0 copy-start.2
  44.7 0.0 collective-permute-done.2
  44.8 0.0 copy-start.7
  44.8 1.8 %shard_map.74 = bf16[8,272,640]{2,1,0:T(8,128)(2,1)} custom-call(bf16[256,640]{1,0:T(8,128)(2,1)S(1)} %bitcast.8, bf16[16,640]{1,0:T(8,128)(2,1)S(1)} %stack.24.side_ref), custom_call_target="tpu_custom_call" | custom-call | tf_op jit(solution)/shard_map/pallas_call | solution.py:189
  46.6 0.2 copy-done.2
  46.7 0.4 copy-done.7
  47.2 5.8 %all-to-all-start.1 = ((bf16[8,272,640]{2,1,0:T(8,128)(2,1)}), bf16[8,272,640]{2,1,0:T(8,128)(2,1)S(1)}, u32[]{:S(2)}, u32[]{:S(2)}) async-start(bf16[8,272,640]{2,1,0:T(8,128)(2,1)} %shard_map.74), calls=%async_computation.1 | async-start | bytes 5570560 | tf_op jit(solution)/shard_map/all_to_all | solution.py:220
  53.0 1.9 %collective-permute-start.3 = (bf16[5120,128]{1,0:T(8,128)(2,1)}, bf16[5120,128]{1,0:T(8,128)(2,1)S(1)}, u32[]{:S(2)}, u32[]{:S(2)}) collective-permute-start(bf16[5120,128]{1,0:T(8,128)(2,1)} %bitcast.15), channel_id=1, source_target_pairs={{0,128},{128,0},{1,129},{129,1},{2,130},{130,2},{3,131},{131,3},{4... | collective-permute-start | bytes 3932168 | tf_op jit(solution)/shard_map/ppermute | solution.py:229
  54.9 2.4 %collective-permute-start.4 = (bf16[5120,128]{1,0:T(8,128)(2,1)}, bf16[5120,128]{1,0:T(8,128)(2,1)S(1)}, u32[]{:S(2)}, u32[]{:S(2)}) collective-permute-start(bf16[5120,128]{1,0:T(8,128)(2,1)} %bitcast.18), channel_id=1, source_target_pairs={{0,128},{128,0},{1,129},{129,1},{2,130},{130,2},{3,131},{131,3},{4... | collective-permute-start | bytes 3932168 | tf_op jit(solution)/shard_map/ppermute | solution.py:229
  57.3 3.5 %collective-permute-done.rest_5_ = bf16[5120,128]{1,0:T(8,128)(2,1)} collective-permute-done((bf16[5120,128]{1,0:T(8,128)(2,1)}, bf16[5120,128]{1,0:T(8,128)(2,1)}, u32[]{:S(2)}, u32[]{:S(2)}) %collective-permute-start) | collective-permute-done | bytes 1310752 | tf_op jit(solution)/shard_map/ppermute | solution.py:233
  60.8 1.9 %collective-permute-start.6 = (bf16[5120,128]{1,0:T(8,128)(2,1)}, bf16[5120,128]{1,0:T(8,128)(2,1)S(1)}, u32[]{:S(2)}, u32[]{:S(2)}) collective-permute-start(bf16[5120,128]{1,0:T(8,128)(2,1)} %collective-permute-done.rest_5_), channel_id=1, source_target_pairs={{0,128},{128,0},{1,129},{129,1},{2,130},{130,2},{3,131},{131,3},{4... | collective-permute-start | bytes 3932168 | tf_op jit(solution)/shard_map/ppermute | solution.py:229
  62.7 2.4 %collective-permute-start.5 = (bf16[5120,128]{1,0:T(8,128)(2,1)}, bf16[5120,128]{1,0:T(8,128)(2,1)}, u32[]{:S(2)}, u32[]{:S(2)}) collective-permute-start(bf16[5120,128]{1,0:T(8,128)(2,1)} %copy-done.2), channel_id=1, source_target_pairs={{0,128},{128,0},{1,129},{129,1},{2,130},{130,2},{3,131},{131,3},{4... | collective-permute-start | bytes 3932168 | tf_op jit(solution)/shard_map/ppermute | solution.py:229
  65.1 3.4 %collective-permute-start.8 = (bf16[1024,640]{1,0:T(8,128)(2,1)}, bf16[1024,640]{1,0:T(8,128)(2,1)}, u32[]{:S(2)}, u32[]{:S(2)}) collective-permute-start(bf16[1024,640]{1,0:T(8,128)(2,1)} %copy-done.7), channel_id=1, source_target_pairs={{0,257},{1,256},{256,1},{257,0},{2,259},{3,258},{258,3},{259,2},{4... | collective-permute-start | bytes 3932168 | tf_op jit(solution)/shard_map/ppermute | solution.py:233
  68.5 0.0 collective-permute-done.3.rest_2_
  68.6 0.0 copy-start.3
  68.6 0.0 collective-permute-done.4.rest_3_
  68.6 0.0 copy-start.4
  68.6 0.0 collective-permute-done.6.rest_7_
  68.6 1.1 copy-done.3
  69.7 0.4 copy-done.4
  70.0 0.0 copy-start.5
  70.0 1.1 copy-done.5
  71.1 0.0 collective-permute-done.5.rest_6_
  71.2 7.1 %all-to-all-done.1.x_ref = bf16[8,272,640]{2,1,0:T(8,128)(2,1)S(1)} async-done(((bf16[8,272,640]{2,1,0:T(8,128)(2,1)}), bf16[8,272,640]{2,1,0:T(8,128)(2,1)S(1)}, u32[]{:S(2)}, u32[]{:S(2)}) %all-to-all-start.1) | async-done | bytes 2785312 | tf_op jit(solution)/shard_map/all_to_all | solution.py:220
  78.2 6.4 %shard_map.75 = bf16[8,256,512]{2,1,0:T(8,128)(2,1)} custom-call(bf16[8,272,640]{2,1,0:T(8,128)(2,1)S(1)} %all-to-all-done.1.x_ref, bf16[5120,128]{1,0:T(8,128)(2,1)} %bitcast.16, bf16[5120,128]{1,0:T(8,128)(2,1)} %bitcast.19, bf16[5120,128]{1,0:T(8,128)(2,1)} %copy-done.3, bf16[5120,128]{1,0:T(8,128)(2,1)} %copy-done.4, bf16[5120,128]{1,0:T(8,128)(2,1)} %copy-done.2, ...), custom_call_target="tpu_custom_call" | custom-call | flops 2684354560 | bytes 13107200 | tf_op jit(solution)/shard_map/pallas_call | solution.py:154
  84.7 0.0 copy-start.1
  84.7 5.8 %all-to-all-start.2 = ((bf16[8,256,512]{2,1,0:T(8,128)(2,1)}), bf16[8,256,512]{2,1,0:T(8,128)(2,1)S(1)}, u32[]{:S(2)}, u32[]{:S(2)}) async-start(bf16[8,256,512]{2,1,0:T(8,128)(2,1)} %shard_map.75), calls=%async_computation.2 | async-start | bytes 4194304 | tf_op jit(solution)/shard_map/all_to_all | solution.py:220
  90.5 0.0 copy-done.1
  90.5 0.0 copy-start
  90.5 2.0 %collective-permute-start.7 = (bf16[1024,640]{1,0:T(8,128)(2,1)S(1)}, bf16[1024,640]{1,0:T(8,128)(2,1)S(1)}, u32[]{:S(2)}, u32[]{:S(2)}) collective-permute-start(bf16[1024,640]{1,0:T(8,128)(2,1)S(1)} %bitcast.22), channel_id=1, source_target_pairs={{0,128},{128,0},{1,129},{129,1},{2,130},{130,2},{3,131},{131,3},{4... | collective-permute-start | bytes 3932168 | tf_op jit(solution)/shard_map/ppermute | solution.py:229
  92.6 5.5 %collective-permute-done.8.d2 = bf16[1024,640]{1,0:T(8,128)(2,1)} collective-permute-done((bf16[1024,640]{1,0:T(8,128)(2,1)}, bf16[1024,640]{1,0:T(8,128)(2,1)}, u32[]{:S(2)}, u32[]{:S(2)}) %collective-permute-start.8) | collective-permute-done | bytes 1310752 | tf_op jit(solution)/shard_map/ppermute | solution.py:233
  98.0 1.9 %collective-permute-start.9 = (bf16[1024,640]{1,0:T(8,128)(2,1)}, bf16[1024,640]{1,0:T(8,128)(2,1)}, u32[]{:S(2)}, u32[]{:S(2)}) collective-permute-start(bf16[1024,640]{1,0:T(8,128)(2,1)} %collective-permute-done.8.d2), channel_id=1, source_target_pairs={{0,128},{128,0},{1,129},{129,1},{2,130},{130,2},{3,131},{131,3},{4... | collective-permute-start | bytes 3932168 | tf_op jit(solution)/shard_map/ppermute | solution.py:229
  100.0 0.0 collective-permute-done.7.d1
  100.0 0.0 copy-start.6
  100.0 1.1 copy-done.6
  101.1 2.2 %collective-permute-done.9.d3 = bf16[1024,640]{1,0:T(8,128)(2,1)} collective-permute-done((bf16[1024,640]{1,0:T(8,128)(2,1)}, bf16[1024,640]{1,0:T(8,128)(2,1)}, u32[]{:S(2)}, u32[]{:S(2)}) %collective-permute-start.9) | collective-permute-done | bytes 1310752 | tf_op jit(solution)/shard_map/ppermute | solution.py:229
  103.3 6.6 %all-to-all-done.2.h_ref = bf16[8,256,512]{2,1,0:T(8,128)(2,1)S(1)} async-done(((bf16[8,256,512]{2,1,0:T(8,128)(2,1)}), bf16[8,256,512]{2,1,0:T(8,128)(2,1)S(1)}, u32[]{:S(2)}, u32[]{:S(2)}) %all-to-all-start.2) | async-done | bytes 2097184 | tf_op jit(solution)/shard_map/all_to_all | solution.py:220
  109.9 3.8 %shard_map.76 = bf16[256,640]{1,0:T(8,128)(2,1)S(1)} custom-call(bf16[8,256,512]{2,1,0:T(8,128)(2,1)S(1)} %all-to-all-done.2.h_ref, bf16[1024,640]{1,0:T(8,128)(2,1)} %bitcast.21, bf16[1024,640]{1,0:T(8,128)(2,1)} %copy-done.6, bf16[1024,640]{1,0:T(8,128)(2,1)} %collective-permute-done.8.d2, bf16[1024,640]{1,0:T(8,128)(2,1)} %collective-permute-done.9.d3), custom_call_target="tpu_custom_call" | custom-call | flops 1342177280 | bytes 7340032 | tf_op jit(solution)/shard_map/pallas_call | solution.py:200
  113.7 38.6 %all_to_all.20 = bf16[16,16,640]{2,1,0:T(8,128)(2,1)S(1)} all-to-all(bf16[16,16,640]{2,1,0:T(8,128)(2,1)S(1)} %bitcast.10), channel_id=1, replica_groups=mesh['xh'=2,'co'=2,'z'=16,'y'=4,'xl'=2] {'z'}, dimensions={0} | all-to-all | bytes 655360 | tf_op jit(solution)/shard_map/all_to_all | solution.py:225
  152.4 0.0 copy-done
  152.4 1.0 shard_map.77
  (7 shorter events, 0.0 us)
Async XLA Ops:
  0.0 44.7 %collective-permute-start.1 = (bf16[5120,128]{1,0:T(8,128)(2,1)}, bf16[5120,128]{1,0:T(8,128)(2,1)S(1)}, u32[]{:S(2)}, u32[]{:S(2)}) collective-permute-start(bf16[5120,128]{1,0:T(8,128)(2,1)} %bitcast.14), channel_id=1, source_target_pairs={{0,257},{1,256},{256,1},{257,0},{2,259},{3,258},{258,3},{259,2},{4... | collective-permute-start | bytes 3932168 | tf_op jit(solution)/shard_map/ppermute | solution.py:233
  3.4 41.4 %collective-permute-start.2 = (bf16[1024,640]{1,0:T(8,128)(2,1)}, bf16[1024,640]{1,0:T(8,128)(2,1)S(1)}, u32[]{:S(2)}, u32[]{:S(2)}) collective-permute-start(bf16[1024,640]{1,0:T(8,128)(2,1)} %bitcast.20), channel_id=1, source_target_pairs={{0,1},{1,0},{2,3},{3,2},{4,5},{5,4},{6,7},{7,6},{8,9},{9,8},{10,11... | collective-permute-start | bytes 3932168 | tf_op jit(solution)/shard_map/ppermute | solution.py:237
  9.1 35.6 %all-to-all-start = ((bf16[16,16,640]{2,1,0:T(8,128)(2,1)}), bf16[16,16,640]{2,1,0:T(8,128)(2,1)S(1)}, u32[]{:S(2)}, u32[]{:S(2)}) async-start(bf16[16,16,640]{2,1,0:T(8,128)(2,1)} %bitcast.13), calls=%async_computation | async-start | bytes 655360 | tf_op jit(solution)/shard_map/all_to_all | solution.py:225
  24.3 36.5 %collective-permute-start = (bf16[5120,128]{1,0:T(8,128)(2,1)}, bf16[5120,128]{1,0:T(8,128)(2,1)}, u32[]{:S(2)}, u32[]{:S(2)}) collective-permute-start(bf16[5120,128]{1,0:T(8,128)(2,1)} %bitcast.17), channel_id=1, source_target_pairs={{0,257},{1,256},{256,1},{257,0},{2,259},{3,258},{258,3},{259,2},{4... | collective-permute-start | bytes 3932168 | tf_op jit(solution)/shard_map/ppermute | solution.py:233
  44.7 2.0 %copy-start.2 = (bf16[5120,128]{1,0:T(8,128)(2,1)}, bf16[5120,128]{1,0:T(8,128)(2,1)S(1)}, u32[]{:S(2)}) copy-start(bf16[5120,128]{1,0:T(8,128)(2,1)S(1)} %collective-permute-done.1.rest_4_) | copy-start | bytes 3932164
  44.8 2.4 %copy-start.7 = (bf16[1024,640]{1,0:T(8,128)(2,1)}, bf16[1024,640]{1,0:T(8,128)(2,1)S(1)}, u32[]{:S(2)}) copy-start(bf16[1024,640]{1,0:T(8,128)(2,1)S(1)} %collective-permute-done.2) | copy-start | bytes 3932164
  47.2 31.1 %all-to-all-start.1 = ((bf16[8,272,640]{2,1,0:T(8,128)(2,1)}), bf16[8,272,640]{2,1,0:T(8,128)(2,1)S(1)}, u32[]{:S(2)}, u32[]{:S(2)}) async-start(bf16[8,272,640]{2,1,0:T(8,128)(2,1)} %shard_map.74), calls=%async_computation.1 | async-start | bytes 5570560 | tf_op jit(solution)/shard_map/all_to_all | solution.py:220
  53.0 15.6 %collective-permute-start.3 = (bf16[5120,128]{1,0:T(8,128)(2,1)}, bf16[5120,128]{1,0:T(8,128)(2,1)S(1)}, u32[]{:S(2)}, u32[]{:S(2)}) collective-permute-start(bf16[5120,128]{1,0:T(8,128)(2,1)} %bitcast.15), channel_id=1, source_target_pairs={{0,128},{128,0},{1,129},{129,1},{2,130},{130,2},{3,131},{131,3},{4... | collective-permute-start | bytes 3932168 | tf_op jit(solution)/shard_map/ppermute | solution.py:229
  54.9 13.7 %collective-permute-start.4 = (bf16[5120,128]{1,0:T(8,128)(2,1)}, bf16[5120,128]{1,0:T(8,128)(2,1)S(1)}, u32[]{:S(2)}, u32[]{:S(2)}) collective-permute-start(bf16[5120,128]{1,0:T(8,128)(2,1)} %bitcast.18), channel_id=1, source_target_pairs={{0,128},{128,0},{1,129},{129,1},{2,130},{130,2},{3,131},{131,3},{4... | collective-permute-start | bytes 3932168 | tf_op jit(solution)/shard_map/ppermute | solution.py:229
  60.8 7.8 %collective-permute-start.6 = (bf16[5120,128]{1,0:T(8,128)(2,1)}, bf16[5120,128]{1,0:T(8,128)(2,1)S(1)}, u32[]{:S(2)}, u32[]{:S(2)}) collective-permute-start(bf16[5120,128]{1,0:T(8,128)(2,1)} %collective-permute-done.rest_5_), channel_id=1, source_target_pairs={{0,128},{128,0},{1,129},{129,1},{2,130},{130,2},{3,131},{131,3},{4... | collective-permute-start | bytes 3932168 | tf_op jit(solution)/shard_map/ppermute | solution.py:229
  62.7 8.4 %collective-permute-start.5 = (bf16[5120,128]{1,0:T(8,128)(2,1)}, bf16[5120,128]{1,0:T(8,128)(2,1)}, u32[]{:S(2)}, u32[]{:S(2)}) collective-permute-start(bf16[5120,128]{1,0:T(8,128)(2,1)} %copy-done.2), channel_id=1, source_target_pairs={{0,128},{128,0},{1,129},{129,1},{2,130},{130,2},{3,131},{131,3},{4... | collective-permute-start | bytes 3932168 | tf_op jit(solution)/shard_map/ppermute | solution.py:229
  65.1 32.9 %collective-permute-start.8 = (bf16[1024,640]{1,0:T(8,128)(2,1)}, bf16[1024,640]{1,0:T(8,128)(2,1)}, u32[]{:S(2)}, u32[]{:S(2)}) collective-permute-start(bf16[1024,640]{1,0:T(8,128)(2,1)} %copy-done.7), channel_id=1, source_target_pairs={{0,257},{1,256},{256,1},{257,0},{2,259},{3,258},{258,3},{259,2},{4... | collective-permute-start | bytes 3932168 | tf_op jit(solution)/shard_map/ppermute | solution.py:233
  68.6 1.1 copy-start.3
  68.6 1.4 copy-start.4
  70.0 1.1 copy-start.5
  84.7 5.8 %copy-start.1 = (bf16[1,1024,640]{2,1,0:T(8,128)(2,1)S(1)}, bf16[1,1024,640]{2,1,0:T(8,128)(2,1)}, u32[]{:S(2)}) copy-start(bf16[1,1024,640]{2,1,0:T(8,128)(2,1)} %param.13) | copy-start | bytes 3932164
  84.7 25.2 %all-to-all-start.2 = ((bf16[8,256,512]{2,1,0:T(8,128)(2,1)}), bf16[8,256,512]{2,1,0:T(8,128)(2,1)S(1)}, u32[]{:S(2)}, u32[]{:S(2)}) async-start(bf16[8,256,512]{2,1,0:T(8,128)(2,1)} %shard_map.75), calls=%async_computation.2 | async-start | bytes 4194304 | tf_op jit(solution)/shard_map/all_to_all | solution.py:220
  90.5 61.8 %copy-start = (s32[128,1]{0,1:T(1,128)S(1)}, s32[128,1]{0,1:T(1,128)}, u32[]{:S(2)}) copy-start(s32[128,1]{0,1:T(1,128)} %param.10) | copy-start | bytes 1540
  90.5 9.4 %collective-permute-start.7 = (bf16[1024,640]{1,0:T(8,128)(2,1)S(1)}, bf16[1024,640]{1,0:T(8,128)(2,1)S(1)}, u32[]{:S(2)}, u32[]{:S(2)}) collective-permute-start(bf16[1024,640]{1,0:T(8,128)(2,1)S(1)} %bitcast.22), channel_id=1, source_target_pairs={{0,128},{128,0},{1,129},{129,1},{2,130},{130,2},{3,131},{131,3},{4... | collective-permute-start | bytes 3932168 | tf_op jit(solution)/shard_map/ppermute | solution.py:229
  98.0 5.3 %collective-permute-start.9 = (bf16[1024,640]{1,0:T(8,128)(2,1)}, bf16[1024,640]{1,0:T(8,128)(2,1)}, u32[]{:S(2)}, u32[]{:S(2)}) collective-permute-start(bf16[1024,640]{1,0:T(8,128)(2,1)} %collective-permute-done.8.d2), channel_id=1, source_target_pairs={{0,128},{128,0},{1,129},{129,1},{2,130},{130,2},{3,131},{131,3},{4... | collective-permute-start | bytes 3932168 | tf_op jit(solution)/shard_map/ppermute | solution.py:229
  100.0 1.1 copy-start.6

commit v10 on v7

--- a/solution.py
+++ b/solution.py
@@ -252,10 +252,9 @@
         dispatch_kernel, out_shape=jax.ShapeDtypeStruct((SLOTS, FEAT), jnp.bfloat16)
     )(ids, tokens)
     pair = (gate, upper)
-    arrived, gate_far, down_sent, token = tied(
-        over_experts(outgoing), across_border(gate), across_pair(down), ids
-    )
+    arrived, gate_far, token = tied(over_experts(outgoing), across_border(gate), ids)
     side = side_rows(norm_gain, router)
+    down_sent = across_pair(down)
 
     near = [other_core(a) for a in pair]
     upper_far, down_sent, token = tied(across_border(upper), down_sent, token)

time: 154 us -> 160 us (1.039)
  the two profiles are of different devices: /device:TPU:10 before, /device:TPU:14 now
where the time goes in v10:
time: 160 us
  waiting for transfers between devices  54.4 us (34%)
  starting transfers between devices  52 us (32%)
  blocking collectives  32.4 us (20%)
  Pallas kernels  15.2 us (10%)
  local copies, waits for them, and re-layouts  3.98 us (2%)
    all_to_all x1, blocking collectives, over_experts(): return lax.all_to_all(parts, 'z', 0, 0, tiled=True).reshape(SLOTS, FEAT)  32.4 us
    all_to_all x2, waiting for transfers between devices, gathered(): return lax.all_to_all(copies, TENSOR_AXES, 0, 0, tiled=True)  30.5 us
    all_to_all x1, starting transfers between devices, over_experts(): return lax.all_to_all(parts, 'z', 0, 0, tiled=True).reshape(SLOTS, FEAT)  15.2 us
    ppermute x6, starting transfers between devices, other_core(): return lax.ppermute(array, 'co', [(0, 1), (1, 0)])  13.1 us
    all_to_all x2, starting transfers between devices, gathered(): return lax.all_to_all(copies, TENSOR_AXES, 0, 0, tiled=True)  12.3 us
    all_to_all x1, waiting for transfers between devices, over_experts(): return lax.all_to_all(parts, 'z', 0, 0, tiled=True).reshape(SLOTS, FEAT)  12.1 us
    ppermute x3, waiting for transfers between devices, across_border(): return lax.ppermute(array, ('xh', 'xl'), [(i, 3 - i) for i in range(4)])  9.86 us
    ppermute x3, starting transfers between devices, across_border(): return lax.ppermute(array, ('xh', 'xl'), [(i, 3 - i) for i in range(4)])  9.43 us
  transfers between devices with their start and end apart: 13, of which 6 were waited for; matrix products, arithmetic and copies ran while one was open for 1% of the time, Pallas kernels for 6%

profile of v10, /device:TPU:14, one launch (start us, length us, event | category | flops | bytes accessed | tf_op | source)
XLA Modules:
  0.0 159.7 jit_solution(10722198538187266466)
XLA Ops:
  0.0 2.4 %collective-permute-start.2 = (bf16[5120,128]{1,0:T(8,128)(2,1)}, bf16[5120,128]{1,0:T(8,128)(2,1)S(1)}, u32[]{:S(2)}, u32[]{:S(2)}) collective-permute-start(bf16[5120,128]{1,0:T(8,128)(2,1)} %bitcast.14), channel_id=1, source_target_pairs={{0,257},{1,256},{256,1},{257,0},{2,259},{3,258},{258,3},{259,2},{4... | collective-permute-start | bytes 3932168 | tf_op jit(solution)/shard_map/ppermute | solution.py:225
  2.4 2.0 %shard_map.73 = bf16[256,640]{1,0:T(8,128)(2,1)} custom-call(s32[1,128]{1,0:T(1,128)} %bitcast.11, bf16[128,640]{1,0:T(8,128)(2,1)} %tokens_ref.1), custom_call_target="tpu_custom_call" | custom-call | tf_op jit(solution)/shard_map/pallas_call | solution.py:251
  4.4 15.2 %all-to-all-start = ((bf16[16,16,640]{2,1,0:T(8,128)(2,1)}), bf16[16,16,640]{2,1,0:T(8,128)(2,1)S(1)}, u32[]{:S(2)}, u32[]{:S(2)}) async-start(bf16[16,16,640]{2,1,0:T(8,128)(2,1)} %bitcast.13), calls=%async_computation | async-start | bytes 655360 | tf_op jit(solution)/shard_map/all_to_all | solution.py:217
  19.6 4.7 %collective-permute-start = (bf16[5120,128]{1,0:T(8,128)(2,1)}, bf16[5120,128]{1,0:T(8,128)(2,1)}, u32[]{:S(2)}, u32[]{:S(2)}) collective-permute-start(bf16[5120,128]{1,0:T(8,128)(2,1)} %bitcast.17), channel_id=1, source_target_pairs={{0,257},{1,256},{256,1},{257,0},{2,259},{3,258},{258,3},{259,2},{4... | collective-permute-start | bytes 3932168 | tf_op jit(solution)/shard_map/ppermute | solution.py:225
  24.3 1.9 %collective-permute-start.1 = (bf16[1024,640]{1,0:T(8,128)(2,1)}, bf16[1024,640]{1,0:T(8,128)(2,1)}, u32[]{:S(2)}, u32[]{:S(2)}) collective-permute-start(bf16[1024,640]{1,0:T(8,128)(2,1)} %bitcast.20), channel_id=1, source_target_pairs={{0,1},{1,0},{2,3},{3,2},{4,5},{5,4},{6,7},{7,6},{8,9},{9,8},{10,11... | collective-permute-start | bytes 3932168 | tf_op jit(solution)/shard_map/ppermute | solution.py:229
  26.2 0.8 subtract_convert_fusion
  27.0 0.8 select_reduce_fusion
  27.9 0.1 stack.24.side_ref
  27.9 12.1 %all-to-all-done = bf16[16,16,640]{2,1,0:T(8,128)(2,1)S(1)} async-done(((bf16[16,16,640]{2,1,0:T(8,128)(2,1)}), bf16[16,16,640]{2,1,0:T(8,128)(2,1)S(1)}, u32[]{:S(2)}, u32[]{:S(2)}) %all-to-all-start) | async-done | bytes 327712 | tf_op jit(solution)/shard_map/all_to_all | solution.py:217
  40.0 0.0 collective-permute-done.2.rest_4_
  40.0 0.0 copy-start.2
  40.0 1.7 %shard_map.74 = bf16[8,272,640]{2,1,0:T(8,128)(2,1)} custom-call(bf16[256,640]{1,0:T(8,128)(2,1)S(1)} %bitcast.8, bf16[16,640]{1,0:T(8,128)(2,1)S(1)} %stack.24.side_ref), custom_call_target="tpu_custom_call" | custom-call | tf_op jit(solution)/shard_map/pallas_call | solution.py:181
  41.8 0.2 copy-done.2
  42.0 5.8 %all-to-all-start.1 = ((bf16[8,272,640]{2,1,0:T(8,128)(2,1)}), bf16[8,272,640]{2,1,0:T(8,128)(2,1)S(1)}, u32[]{:S(2)}, u32[]{:S(2)}) async-start(bf16[8,272,640]{2,1,0:T(8,128)(2,1)} %shard_map.74), calls=%async_computation.1 | async-start | bytes 5570560 | tf_op jit(solution)/shard_map/all_to_all | solution.py:212
  47.8 1.9 %collective-permute-start.3 = (bf16[5120,128]{1,0:T(8,128)(2,1)}, bf16[5120,128]{1,0:T(8,128)(2,1)S(1)}, u32[]{:S(2)}, u32[]{:S(2)}) collective-permute-start(bf16[5120,128]{1,0:T(8,128)(2,1)} %bitcast.15), channel_id=1, source_target_pairs={{0,128},{128,0},{1,129},{129,1},{2,130},{130,2},{3,131},{131,3},{4... | collective-permute-start | bytes 3932168 | tf_op jit(solution)/shard_map/ppermute | solution.py:221
  49.7 2.4 %collective-permute-start.4 = (bf16[5120,128]{1,0:T(8,128)(2,1)}, bf16[5120,128]{1,0:T(8,128)(2,1)S(1)}, u32[]{:S(2)}, u32[]{:S(2)}) collective-permute-start(bf16[5120,128]{1,0:T(8,128)(2,1)} %bitcast.18), channel_id=1, source_target_pairs={{0,128},{128,0},{1,129},{129,1},{2,130},{130,2},{3,131},{131,3},{4... | collective-permute-start | bytes 3932168 | tf_op jit(solution)/shard_map/ppermute | solution.py:221
  52.2 9.9 %collective-permute-done.rest_5_ = bf16[5120,128]{1,0:T(8,128)(2,1)} collective-permute-done((bf16[5120,128]{1,0:T(8,128)(2,1)}, bf16[5120,128]{1,0:T(8,128)(2,1)}, u32[]{:S(2)}, u32[]{:S(2)}) %collective-permute-start) | collective-permute-done | bytes 1310752 | tf_op jit(solution)/shard_map/ppermute | solution.py:225
  62.0 0.0 collective-permute-done.1
  62.0 1.9 %collective-permute-start.6 = (bf16[5120,128]{1,0:T(8,128)(2,1)}, bf16[5120,128]{1,0:T(8,128)(2,1)S(1)}, u32[]{:S(2)}, u32[]{:S(2)}) collective-permute-start(bf16[5120,128]{1,0:T(8,128)(2,1)} %collective-permute-done.rest_5_), channel_id=1, source_target_pairs={{0,128},{128,0},{1,129},{129,1},{2,130},{130,2},{3,131},{131,3},{4... | collective-permute-start | bytes 3932168 | tf_op jit(solution)/shard_map/ppermute | solution.py:221
  63.9 2.4 %collective-permute-start.5 = (bf16[5120,128]{1,0:T(8,128)(2,1)}, bf16[5120,128]{1,0:T(8,128)(2,1)}, u32[]{:S(2)}, u32[]{:S(2)}) collective-permute-start(bf16[5120,128]{1,0:T(8,128)(2,1)} %copy-done.2), channel_id=1, source_target_pairs={{0,128},{128,0},{1,129},{129,1},{2,130},{130,2},{3,131},{131,3},{4... | collective-permute-start | bytes 3932168 | tf_op jit(solution)/shard_map/ppermute | solution.py:221
  66.4 2.4 %collective-permute-start.8 = (bf16[1024,640]{1,0:T(8,128)(2,1)}, bf16[1024,640]{1,0:T(8,128)(2,1)}, u32[]{:S(2)}, u32[]{:S(2)}) collective-permute-start(bf16[1024,640]{1,0:T(8,128)(2,1)} %collective-permute-done.1), channel_id=1, source_target_pairs={{0,257},{1,256},{256,1},{257,0},{2,259},{3,258},{258,3},{259,2},{4... | collective-permute-start | bytes 3932168 | tf_op jit(solution)/shard_map/ppermute | solution.py:225
  68.7 0.0 collective-permute-done.3.rest_2_
  68.8 0.0 copy-start.3
  68.8 0.0 collective-permute-done.4.rest_3_
  68.8 0.0 copy-start.4
  68.8 0.0 collective-permute-done.6.rest_7_
  68.8 1.1 copy-done.3
  69.9 0.4 copy-done.4
  70.2 0.0 copy-start.5
  70.2 1.1 copy-done.5
  71.4 0.0 collective-permute-done.5.rest_6_
  71.4 14.6 %all-to-all-done.1.x_ref = bf16[8,272,640]{2,1,0:T(8,128)(2,1)S(1)} async-done(((bf16[8,272,640]{2,1,0:T(8,128)(2,1)}), bf16[8,272,640]{2,1,0:T(8,128)(2,1)S(1)}, u32[]{:S(2)}, u32[]{:S(2)}) %all-to-all-start.1) | async-done | bytes 2785312 | tf_op jit(solution)/shard_map/all_to_all | solution.py:212
  86.0 6.5 %shard_map.75 = bf16[8,256,512]{2,1,0:T(8,128)(2,1)} custom-call(bf16[8,272,640]{2,1,0:T(8,128)(2,1)S(1)} %all-to-all-done.1.x_ref, bf16[5120,128]{1,0:T(8,128)(2,1)} %bitcast.16, bf16[5120,128]{1,0:T(8,128)(2,1)} %bitcast.19, bf16[5120,128]{1,0:T(8,128)(2,1)} %copy-done.3, bf16[5120,128]{1,0:T(8,128)(2,1)} %copy-done.4, bf16[5120,128]{1,0:T(8,128)(2,1)} %copy-done.2, ...), custom_call_target="tpu_custom_call" | custom-call | flops 2684354560 | bytes 13107200 | tf_op jit(solution)/shard_map/pallas_call | solution.py:146
  92.5 0.0 copy-start.1
  92.5 6.5 %all-to-all-start.2 = ((bf16[8,256,512]{2,1,0:T(8,128)(2,1)}), bf16[8,256,512]{2,1,0:T(8,128)(2,1)S(1)}, u32[]{:S(2)}, u32[]{:S(2)}) async-start(bf16[8,256,512]{2,1,0:T(8,128)(2,1)} %shard_map.75), calls=%async_computation.2 | async-start | bytes 4194304 | tf_op jit(solution)/shard_map/all_to_all | solution.py:212
  99.0 0.0 copy-done.1
  99.0 0.0 copy-start
  99.0 2.0 %collective-permute-start.7 = (bf16[1024,640]{1,0:T(8,128)(2,1)S(1)}, bf16[1024,640]{1,0:T(8,128)(2,1)S(1)}, u32[]{:S(2)}, u32[]{:S(2)}) collective-permute-start(bf16[1024,640]{1,0:T(8,128)(2,1)S(1)} %bitcast.22), channel_id=1, source_target_pairs={{0,128},{128,0},{1,129},{129,1},{2,130},{130,2},{3,131},{131,3},{4... | collective-permute-start | bytes 3932168 | tf_op jit(solution)/shard_map/ppermute | solution.py:221
  101.1 0.0 collective-permute-done.8.d2
  101.1 2.4 %collective-permute-start.9 = (bf16[1024,640]{1,0:T(8,128)(2,1)}, bf16[1024,640]{1,0:T(8,128)(2,1)}, u32[]{:S(2)}, u32[]{:S(2)}) collective-permute-start(bf16[1024,640]{1,0:T(8,128)(2,1)} %collective-permute-done.8.d2), channel_id=1, source_target_pairs={{0,128},{128,0},{1,129},{129,1},{2,130},{130,2},{3,131},{131,3},{4... | collective-permute-start | bytes 3932168 | tf_op jit(solution)/shard_map/ppermute | solution.py:221
  103.5 0.6 collective-permute-done.7.d1
  104.1 0.0 copy-start.6
  104.1 1.1 copy-done.6
  105.2 1.3 collective-permute-done.9.d3
  106.5 16.0 %all-to-all-done.2.h_ref = bf16[8,256,512]{2,1,0:T(8,128)(2,1)S(1)} async-done(((bf16[8,256,512]{2,1,0:T(8,128)(2,1)}), bf16[8,256,512]{2,1,0:T(8,128)(2,1)S(1)}, u32[]{:S(2)}, u32[]{:S(2)}) %all-to-all-start.2) | async-done | bytes 2097184 | tf_op jit(solution)/shard_map/all_to_all | solution.py:212
  122.5 3.8 %shard_map.76 = bf16[256,640]{1,0:T(8,128)(2,1)S(1)} custom-call(bf16[8,256,512]{2,1,0:T(8,128)(2,1)S(1)} %all-to-all-done.2.h_ref, bf16[1024,640]{1,0:T(8,128)(2,1)} %bitcast.21, bf16[1024,640]{1,0:T(8,128)(2,1)} %copy-done.6, bf16[1024,640]{1,0:T(8,128)(2,1)} %collective-permute-done.8.d2, bf16[1024,640]{1,0:T(8,128)(2,1)} %collective-permute-done.9.d3), custom_call_target="tpu_custom_call" | custom-call | flops 1342177280 | bytes 7340032 | tf_op jit(solution)/shard_map/pallas_call | solution.py:192
  126.3 32.4 %all_to_all.20 = bf16[16,16,640]{2,1,0:T(8,128)(2,1)S(1)} all-to-all(bf16[16,16,640]{2,1,0:T(8,128)(2,1)S(1)} %bitcast.10), channel_id=1, replica_groups=mesh['xh'=2,'co'=2,'z'=16,'y'=4,'xl'=2] {'z'}, dimensions={0} | all-to-all | bytes 655360 | tf_op jit(solution)/shard_map/all_to_all | solution.py:217
  158.7 0.0 copy-done
  158.7 1.0 shard_map.77
  (7 shorter events, 0.0 us)
Async XLA Ops:
  0.0 40.0 %collective-permute-start.2 = (bf16[5120,128]{1,0:T(8,128)(2,1)}, bf16[5120,128]{1,0:T(8,128)(2,1)S(1)}, u32[]{:S(2)}, u32[]{:S(2)}) collective-permute-start(bf16[5120,128]{1,0:T(8,128)(2,1)} %bitcast.14), channel_id=1, source_target_pairs={{0,257},{1,256},{256,1},{257,0},{2,259},{3,258},{258,3},{259,2},{4... | collective-permute-start | bytes 3932168 | tf_op jit(solution)/shard_map/ppermute | solution.py:225
  4.4 35.6 %all-to-all-start = ((bf16[16,16,640]{2,1,0:T(8,128)(2,1)}), bf16[16,16,640]{2,1,0:T(8,128)(2,1)S(1)}, u32[]{:S(2)}, u32[]{:S(2)}) async-start(bf16[16,16,640]{2,1,0:T(8,128)(2,1)} %bitcast.13), calls=%async_computation | async-start | bytes 655360 | tf_op jit(solution)/shard_map/all_to_all | solution.py:217
  19.6 42.4 %collective-permute-start = (bf16[5120,128]{1,0:T(8,128)(2,1)}, bf16[5120,128]{1,0:T(8,128)(2,1)}, u32[]{:S(2)}, u32[]{:S(2)}) collective-permute-start(bf16[5120,128]{1,0:T(8,128)(2,1)} %bitcast.17), channel_id=1, source_target_pairs={{0,257},{1,256},{256,1},{257,0},{2,259},{3,258},{258,3},{259,2},{4... | collective-permute-start | bytes 3932168 | tf_op jit(solution)/shard_map/ppermute | solution.py:225
  24.3 37.7 %collective-permute-start.1 = (bf16[1024,640]{1,0:T(8,128)(2,1)}, bf16[1024,640]{1,0:T(8,128)(2,1)}, u32[]{:S(2)}, u32[]{:S(2)}) collective-permute-start(bf16[1024,640]{1,0:T(8,128)(2,1)} %bitcast.20), channel_id=1, source_target_pairs={{0,1},{1,0},{2,3},{3,2},{4,5},{5,4},{6,7},{7,6},{8,9},{9,8},{10,11... | collective-permute-start | bytes 3932168 | tf_op jit(solution)/shard_map/ppermute | solution.py:229
  40.0 2.0 %copy-start.2 = (bf16[5120,128]{1,0:T(8,128)(2,1)}, bf16[5120,128]{1,0:T(8,128)(2,1)S(1)}, u32[]{:S(2)}) copy-start(bf16[5120,128]{1,0:T(8,128)(2,1)S(1)} %collective-permute-done.2.rest_4_) | copy-start | bytes 3932164
  42.0 43.9 %all-to-all-start.1 = ((bf16[8,272,640]{2,1,0:T(8,128)(2,1)}), bf16[8,272,640]{2,1,0:T(8,128)(2,1)S(1)}, u32[]{:S(2)}, u32[]{:S(2)}) async-start(bf16[8,272,640]{2,1,0:T(8,128)(2,1)} %shard_map.74), calls=%async_computation.1 | async-start | bytes 5570560 | tf_op jit(solution)/shard_map/all_to_all | solution.py:212
  47.8 20.9 %collective-permute-start.3 = (bf16[5120,128]{1,0:T(8,128)(2,1)}, bf16[5120,128]{1,0:T(8,128)(2,1)S(1)}, u32[]{:S(2)}, u32[]{:S(2)}) collective-permute-start(bf16[5120,128]{1,0:T(8,128)(2,1)} %bitcast.15), channel_id=1, source_target_pairs={{0,128},{128,0},{1,129},{129,1},{2,130},{130,2},{3,131},{131,3},{4... | collective-permute-start | bytes 3932168 | tf_op jit(solution)/shard_map/ppermute | solution.py:221
  49.7 19.0 %collective-permute-start.4 = (bf16[5120,128]{1,0:T(8,128)(2,1)}, bf16[5120,128]{1,0:T(8,128)(2,1)S(1)}, u32[]{:S(2)}, u32[]{:S(2)}) collective-permute-start(bf16[5120,128]{1,0:T(8,128)(2,1)} %bitcast.18), channel_id=1, source_target_pairs={{0,128},{128,0},{1,129},{129,1},{2,130},{130,2},{3,131},{131,3},{4... | collective-permute-start | bytes 3932168 | tf_op jit(solution)/shard_map/ppermute | solution.py:221
  62.0 6.8 %collective-permute-start.6 = (bf16[5120,128]{1,0:T(8,128)(2,1)}, bf16[5120,128]{1,0:T(8,128)(2,1)S(1)}, u32[]{:S(2)}, u32[]{:S(2)}) collective-permute-start(bf16[5120,128]{1,0:T(8,128)(2,1)} %collective-permute-done.rest_5_), channel_id=1, source_target_pairs={{0,128},{128,0},{1,129},{129,1},{2,130},{130,2},{3,131},{131,3},{4... | collective-permute-start | bytes 3932168 | tf_op jit(solution)/shard_map/ppermute | solution.py:221
  63.9 7.4 %collective-permute-start.5 = (bf16[5120,128]{1,0:T(8,128)(2,1)}, bf16[5120,128]{1,0:T(8,128)(2,1)}, u32[]{:S(2)}, u32[]{:S(2)}) collective-permute-start(bf16[5120,128]{1,0:T(8,128)(2,1)} %copy-done.2), channel_id=1, source_target_pairs={{0,128},{128,0},{1,129},{129,1},{2,130},{130,2},{3,131},{131,3},{4... | collective-permute-start | bytes 3932168 | tf_op jit(solution)/shard_map/ppermute | solution.py:221
  66.4 34.7 %collective-permute-start.8 = (bf16[1024,640]{1,0:T(8,128)(2,1)}, bf16[1024,640]{1,0:T(8,128)(2,1)}, u32[]{:S(2)}, u32[]{:S(2)}) collective-permute-start(bf16[1024,640]{1,0:T(8,128)(2,1)} %collective-permute-done.1), channel_id=1, source_target_pairs={{0,257},{1,256},{256,1},{257,0},{2,259},{3,258},{258,3},{259,2},{4... | collective-permute-start | bytes 3932168 | tf_op jit(solution)/shard_map/ppermute | solution.py:225
  68.8 1.1 copy-start.3
  68.8 1.4 copy-start.4
  70.2 1.1 copy-start.5
  92.5 6.5 %copy-start.1 = (bf16[1,1024,640]{2,1,0:T(8,128)(2,1)S(1)}, bf16[1,1024,640]{2,1,0:T(8,128)(2,1)}, u32[]{:S(2)}) copy-start(bf16[1,1024,640]{2,1,0:T(8,128)(2,1)} %param.13) | copy-start | bytes 3932164
  92.5 29.9 %all-to-all-start.2 = ((bf16[8,256,512]{2,1,0:T(8,128)(2,1)}), bf16[8,256,512]{2,1,0:T(8,128)(2,1)S(1)}, u32[]{:S(2)}, u32[]{:S(2)}) async-start(bf16[8,256,512]{2,1,0:T(8,128)(2,1)} %shard_map.75), calls=%async_computation.2 | async-start | bytes 4194304 | tf_op jit(solution)/shard_map/all_to_all | solution.py:212
  99.0 59.7 %copy-start = (s32[128,1]{0,1:T(1,128)S(1)}, s32[128,1]{0,1:T(1,128)}, u32[]{:S(2)}) copy-start(s32[128,1]{0,1:T(1,128)} %param.10) | copy-start | bytes 1540
  99.0 5.1 %collective-permute-start.7 = (bf16[1024,640]{1,0:T(8,128)(2,1)S(1)}, bf16[1024,640]{1,0:T(8,128)(2,1)S(1)}, u32[]{:S(2)}, u32[]{:S(2)}) collective-permute-start(bf16[1024,640]{1,0:T(8,128)(2,1)S(1)} %bitcast.22), channel_id=1, source_target_pairs={{0,128},{128,0},{1,129},{129,1},{2,130},{130,2},{3,131},{131,3},{4... | collective-permute-start | bytes 3932168 | tf_op jit(solution)/shard_map/ppermute | solution.py:221
  101.1 5.4 %collective-permute-start.9 = (bf16[1024,640]{1,0:T(8,128)(2,1)}, bf16[1024,640]{1,0:T(8,128)(2,1)}, u32[]{:S(2)}, u32[]{:S(2)}) collective-permute-start(bf16[1024,640]{1,0:T(8,128)(2,1)} %collective-permute-done.8.d2), channel_id=1, source_target_pairs={{0,128},{128,0},{1,129},{129,1},{2,130},{130,2},{3,131},{131,3},{4... | collective-permute-start | bytes 3932168 | tf_op jit(solution)/shard_map/ppermute | solution.py:221
  104.1 1.1 copy-start.6

commit v11 on v6

--- a/solution.py
+++ b/solution.py
@@ -135,6 +135,7 @@
 IN_VMEM = pl.BlockSpec(memory_space=pltpu.VMEM)
 IN_HBM = pl.BlockSpec(memory_space=pl.ANY)
 PARAMS = pltpu.CompilerParams(vmem_limit_bytes=VMEM)
+SMALL = pltpu.CompilerParams(vmem_limit_bytes=8 * 1024 * 1024)
 
 
 def left_in_hbm(arrays):
@@ -146,7 +147,7 @@
         hidden_kernel,
         in_specs=[IN_VMEM] + [IN_HBM] * len(weights),
         out_specs=IN_HBM,
-        out_shape=jax.ShapeDtypeStruct((TENSOR, SLOTS, 512), jnp.bfloat16),
+        out_shape=pltpu.HBM((TENSOR, SLOTS, 512), jnp.bfloat16),
         scratch_shapes=[
             pltpu.VMEM((8, D, 128), jnp.bfloat16),
             pltpu.VMEM((SLOTS, 1024), jnp.float32),
@@ -246,7 +247,9 @@
     summed = down_sums(gathered(hidden), down, down_near, down_far, down_last)
     returned = over_experts(summed)
     return pl.pallas_call(
-        combine_kernel, out_shape=jax.ShapeDtypeStruct((TOK, FEAT), jnp.bfloat16)
+        combine_kernel,
+        out_shape=jax.ShapeDtypeStruct((TOK, FEAT), jnp.bfloat16),
+        compiler_params=SMALL,
     )(token, returned)
 
 

time: 155 us -> 154 us (level)
  transfers between devices with their start and end apart: 13 -> 13, of which waited for: 6 -> 6; matrix products, arithmetic and copies ran while one was open for 2% -> 2% of each run, Pallas kernels for 5% -> 6%
where the time goes in v11:
time: 154 us; the launch traced here: 153 us
  starting transfers between devices  51.9 us (34%)
  waiting for transfers between devices  41 us (27%)
  blocking collectives  38.5 us (25%)
  Pallas kernels  13.4 us (9%)
  local copies, waits for them, and re-layouts  6.81 us (4%)
  other arithmetic  1.59 us (1%)
    all_to_all x1, blocking collectives, over_experts(): return lax.all_to_all(parts, 'z', 0, 0, tiled=True).reshape(SLOTS, FEAT)  38.5 us
    all_to_all x1, waiting for transfers between devices, over_experts(): return lax.all_to_all(parts, 'z', 0, 0, tiled=True).reshape(SLOTS, FEAT)  16.8 us
    all_to_all x1, starting transfers between devices, over_experts(): return lax.all_to_all(parts, 'z', 0, 0, tiled=True).reshape(SLOTS, FEAT)  15.2 us
    all_to_all x2, waiting for transfers between devices, gathered(): return lax.all_to_all(copies, TENSOR_AXES, 0, 0, tiled=True)  13.6 us
    ppermute x6, starting transfers between devices, other_core(): return lax.ppermute(array, 'co', [(0, 1), (1, 0)])  12.6 us
    all_to_all x2, starting transfers between devices, gathered(): return lax.all_to_all(copies, TENSOR_AXES, 0, 0, tiled=True)  11.6 us
    ppermute x3, starting transfers between devices, across_border(): return lax.ppermute(array, ('xh', 'xl'), [(i, 3 - i) for i in range(4)])  8.71 us
    ppermute x3, waiting for transfers between devices, across_border(): return lax.ppermute(array, ('xh', 'xl'), [(i, 3 - i) for i in range(4)])  8.25 us
  transfers between devices with their start and end apart: 13, of which 6 were waited for; matrix products, arithmetic and copies ran while one was open for 2% of the time, Pallas kernels for 6%

profile of v11, /device:TPU:10, one launch (start us, length us, event | category | flops | bytes accessed | tf_op | source)
XLA Modules:
  0.0 153.3 jit_solution(5386552334503670873)
XLA Ops:
  0.0 3.4 %collective-permute-start.1 = (bf16[5120,128]{1,0:T(8,128)(2,1)}, bf16[5120,128]{1,0:T(8,128)(2,1)S(1)}, u32[]{:S(2)}, u32[]{:S(2)}) collective-permute-start(bf16[5120,128]{1,0:T(8,128)(2,1)} %bitcast.12), channel_id=1, source_target_pairs={{0,257},{1,256},{256,1},{257,0},{2,259},{3,258},{258,3},{259,2},{4... | collective-permute-start | bytes 3932168 | tf_op jit(solution)/shard_map/ppermute | solution.py:201
  3.4 3.7 %collective-permute-start.2 = (bf16[1024,640]{1,0:T(8,128)(2,1)}, bf16[1024,640]{1,0:T(8,128)(2,1)S(1)}, u32[]{:S(2)}, u32[]{:S(2)}) collective-permute-start(bf16[1024,640]{1,0:T(8,128)(2,1)} %bitcast.20), channel_id=1, source_target_pairs={{0,1},{1,0},{2,3},{3,2},{4,5},{5,4},{6,7},{7,6},{8,9},{9,8},{10,11... | collective-permute-start | bytes 3932168 | tf_op jit(solution)/shard_map/ppermute | solution.py:205
  7.1 2.0 %shard_map.73 = bf16[256,640]{1,0:T(8,128)(2,1)} custom-call(s32[1,128]{1,0:T(1,128)} %bitcast.10, bf16[128,640]{1,0:T(8,128)(2,1)} %tokens_ref.1), custom_call_target="tpu_custom_call" | custom-call | tf_op jit(solution)/shard_map/pallas_call | solution.py:227
  9.1 15.2 %all-to-all-start = ((bf16[16,16,640]{2,1,0:T(8,128)(2,1)}), bf16[16,16,640]{2,1,0:T(8,128)(2,1)S(1)}, u32[]{:S(2)}, u32[]{:S(2)}) async-start(bf16[16,16,640]{2,1,0:T(8,128)(2,1)} %bitcast.19), calls=%async_computation | async-start | bytes 655360 | tf_op jit(solution)/shard_map/all_to_all | solution.py:193
  24.3 1.9 %collective-permute-start = (bf16[5120,128]{1,0:T(8,128)(2,1)}, bf16[5120,128]{1,0:T(8,128)(2,1)}, u32[]{:S(2)}, u32[]{:S(2)}) collective-permute-start(bf16[5120,128]{1,0:T(8,128)(2,1)} %bitcast.15), channel_id=1, source_target_pairs={{0,257},{1,256},{256,1},{257,0},{2,259},{3,258},{258,3},{259,2},{4... | collective-permute-start | bytes 3932168 | tf_op jit(solution)/shard_map/ppermute | solution.py:201
  26.3 0.8 subtract_convert_fusion
  27.1 0.8 select_reduce_fusion
  27.9 16.8 %all-to-all-done = bf16[16,16,640]{2,1,0:T(8,128)(2,1)S(1)} async-done(((bf16[16,16,640]{2,1,0:T(8,128)(2,1)}), bf16[16,16,640]{2,1,0:T(8,128)(2,1)S(1)}, u32[]{:S(2)}, u32[]{:S(2)}) %all-to-all-start) | async-done | bytes 327712 | tf_op jit(solution)/shard_map/all_to_all | solution.py:193
  44.7 0.0 collective-permute-done.1.rest_4_
  44.7 0.0 copy-start.1
  44.7 0.0 collective-permute-done.2
  44.8 0.0 copy-start.7
  44.8 1.1 copy-done.1
  45.8 0.3 concatenate.7
  46.2 1.7 %broadcast_in_dim.21 = bf16[8,264,640]{2,1,0:T(8,128)(2,1)} broadcast(bf16[264,640]{1,0:T(8,128)(2,1)S(1)} %concatenate.7), dimensions={1,2} | broadcast | bytes 3041280 | tf_op jit(solution)/shard_map/broadcast_in_dim | solution.py:242
  47.9 0.0 copy-done.7
  47.9 5.8 %all-to-all-start.1 = ((bf16[8,264,640]{2,1,0:T(8,128)(2,1)}), bf16[8,264,640]{2,1,0:T(8,128)(2,1)S(1)}, u32[]{:S(2)}, u32[]{:S(2)}) async-start(bf16[8,264,640]{2,1,0:T(8,128)(2,1)} %broadcast_in_dim.21), calls=%async_computation.1 | async-start | bytes 5406720 | tf_op jit(solution)/shard_map/all_to_all | solution.py:188
  53.7 1.9 %collective-permute-start.3 = (bf16[5120,128]{1,0:T(8,128)(2,1)}, bf16[5120,128]{1,0:T(8,128)(2,1)S(1)}, u32[]{:S(2)}, u32[]{:S(2)}) collective-permute-start(bf16[5120,128]{1,0:T(8,128)(2,1)} %bitcast.13), channel_id=1, source_target_pairs={{0,128},{128,0},{1,129},{129,1},{2,130},{130,2},{3,131},{131,3},{4... | collective-permute-start | bytes 3932168 | tf_op jit(solution)/shard_map/ppermute | solution.py:197
  55.6 2.4 %collective-permute-start.4 = (bf16[5120,128]{1,0:T(8,128)(2,1)}, bf16[5120,128]{1,0:T(8,128)(2,1)S(1)}, u32[]{:S(2)}, u32[]{:S(2)}) collective-permute-start(bf16[5120,128]{1,0:T(8,128)(2,1)} %bitcast.16), channel_id=1, source_target_pairs={{0,128},{128,0},{1,129},{129,1},{2,130},{130,2},{3,131},{131,3},{4... | collective-permute-start | bytes 3932168 | tf_op jit(solution)/shard_map/ppermute | solution.py:197
  58.1 2.7 %collective-permute-done.rest_5_ = bf16[5120,128]{1,0:T(8,128)(2,1)} collective-permute-done((bf16[5120,128]{1,0:T(8,128)(2,1)}, bf16[5120,128]{1,0:T(8,128)(2,1)}, u32[]{:S(2)}, u32[]{:S(2)}) %collective-permute-start) | collective-permute-done | bytes 1310752 | tf_op jit(solution)/shard_map/ppermute | solution.py:201
  60.8 1.9 %collective-permute-start.6 = (bf16[5120,128]{1,0:T(8,128)(2,1)}, bf16[5120,128]{1,0:T(8,128)(2,1)S(1)}, u32[]{:S(2)}, u32[]{:S(2)}) collective-permute-start(bf16[5120,128]{1,0:T(8,128)(2,1)} %collective-permute-done.rest_5_), channel_id=1, source_target_pairs={{0,128},{128,0},{1,129},{129,1},{2,130},{130,2},{3,131},{131,3},{4... | collective-permute-start | bytes 3932168 | tf_op jit(solution)/shard_map/ppermute | solution.py:197
  62.7 2.4 %collective-permute-start.5 = (bf16[5120,128]{1,0:T(8,128)(2,1)}, bf16[5120,128]{1,0:T(8,128)(2,1)}, u32[]{:S(2)}, u32[]{:S(2)}) collective-permute-start(bf16[5120,128]{1,0:T(8,128)(2,1)} %copy-done.1), channel_id=1, source_target_pairs={{0,128},{128,0},{1,129},{129,1},{2,130},{130,2},{3,131},{131,3},{4... | collective-permute-start | bytes 3932168 | tf_op jit(solution)/shard_map/ppermute | solution.py:197
  65.1 3.4 %collective-permute-start.8 = (bf16[1024,640]{1,0:T(8,128)(2,1)}, bf16[1024,640]{1,0:T(8,128)(2,1)}, u32[]{:S(2)}, u32[]{:S(2)}) collective-permute-start(bf16[1024,640]{1,0:T(8,128)(2,1)} %copy-done.7), channel_id=1, source_target_pairs={{0,257},{1,256},{256,1},{257,0},{2,259},{3,258},{258,3},{259,2},{4... | collective-permute-start | bytes 3932168 | tf_op jit(solution)/shard_map/ppermute | solution.py:201
  68.5 0.0 collective-permute-done.3.rest_2_
  68.6 0.0 copy-start.2
  68.6 0.0 collective-permute-done.4.rest_3_
  68.6 0.0 copy-start.3
  68.6 0.0 collective-permute-done.6.rest_7_
  68.6 1.0 copy-done.2
  69.6 0.4 copy-done.3
  70.0 0.0 copy-start.4
  70.0 1.1 copy-done.4
  71.2 0.0 collective-permute-done.5.rest_6_
  71.2 6.9 %all-to-all-done.1.x_ref = bf16[8,264,640]{2,1,0:T(8,128)(2,1)S(1)} async-done(((bf16[8,264,640]{2,1,0:T(8,128)(2,1)}), bf16[8,264,640]{2,1,0:T(8,128)(2,1)S(1)}, u32[]{:S(2)}, u32[]{:S(2)}) %all-to-all-start.1) | async-done | bytes 2703392 | tf_op jit(solution)/shard_map/all_to_all | solution.py:188
  78.1 6.5 %shard_map.74 = bf16[8,256,512]{2,1,0:T(8,128)(2,1)} custom-call(bf16[8,264,640]{2,1,0:T(8,128)(2,1)S(1)} %all-to-all-done.1.x_ref, bf16[5120,128]{1,0:T(8,128)(2,1)} %bitcast.14, bf16[5120,128]{1,0:T(8,128)(2,1)} %bitcast.17, bf16[5120,128]{1,0:T(8,128)(2,1)} %copy-done.2, bf16[5120,128]{1,0:T(8,128)(2,1)} %copy-done.3, bf16[5120,128]{1,0:T(8,128)(2,1)} %copy-done.1, ...), custom_call_target="tpu_custom_call" | custom-call | flops 2684354560 | bytes 13107200 | tf_op jit(solution)/shard_map/pallas_call | solution.py:146
  84.6 0.0 copy-start.5
  84.7 5.8 %all-to-all-start.2 = ((bf16[8,256,512]{2,1,0:T(8,128)(2,1)}), bf16[8,256,512]{2,1,0:T(8,128)(2,1)S(1)}, u32[]{:S(2)}, u32[]{:S(2)}) async-start(bf16[8,256,512]{2,1,0:T(8,128)(2,1)} %shard_map.74), calls=%async_computation.2 | async-start | bytes 4194304 | tf_op jit(solution)/shard_map/all_to_all | solution.py:188
  90.5 0.0 copy-done.5
  90.5 0.0 copy-start
  90.5 2.0 %collective-permute-start.7 = (bf16[1024,640]{1,0:T(8,128)(2,1)S(1)}, bf16[1024,640]{1,0:T(8,128)(2,1)S(1)}, u32[]{:S(2)}, u32[]{:S(2)}) collective-permute-start(bf16[1024,640]{1,0:T(8,128)(2,1)S(1)} %bitcast.22), channel_id=1, source_target_pairs={{0,128},{128,0},{1,129},{129,1},{2,130},{130,2},{3,131},{131,3},{4... | collective-permute-start | bytes 3932168 | tf_op jit(solution)/shard_map/ppermute | solution.py:197
  92.5 5.5 %collective-permute-done.8.d2 = bf16[1024,640]{1,0:T(8,128)(2,1)} collective-permute-done((bf16[1024,640]{1,0:T(8,128)(2,1)}, bf16[1024,640]{1,0:T(8,128)(2,1)}, u32[]{:S(2)}, u32[]{:S(2)}) %collective-permute-start.8) | collective-permute-done | bytes 1310752 | tf_op jit(solution)/shard_map/ppermute | solution.py:201
  98.0 1.9 %collective-permute-start.9 = (bf16[1024,640]{1,0:T(8,128)(2,1)}, bf16[1024,640]{1,0:T(8,128)(2,1)}, u32[]{:S(2)}, u32[]{:S(2)}) collective-permute-start(bf16[1024,640]{1,0:T(8,128)(2,1)} %collective-permute-done.8.d2), channel_id=1, source_target_pairs={{0,128},{128,0},{1,129},{129,1},{2,130},{130,2},{3,131},{131,3},{4... | collective-permute-start | bytes 3932168 | tf_op jit(solution)/shard_map/ppermute | solution.py:197
  100.0 0.0 collective-permute-done.7.d1
  100.0 0.0 copy-start.6
  100.0 1.1 copy-done.6
  101.1 2.3 %collective-permute-done.9.d3 = bf16[1024,640]{1,0:T(8,128)(2,1)} collective-permute-done((bf16[1024,640]{1,0:T(8,128)(2,1)}, bf16[1024,640]{1,0:T(8,128)(2,1)}, u32[]{:S(2)}, u32[]{:S(2)}) %collective-permute-start.9) | collective-permute-done | bytes 1310752 | tf_op jit(solution)/shard_map/ppermute | solution.py:197
  103.3 6.7 %all-to-all-done.2.h_ref = bf16[8,256,512]{2,1,0:T(8,128)(2,1)S(1)} async-done(((bf16[8,256,512]{2,1,0:T(8,128)(2,1)}), bf16[8,256,512]{2,1,0:T(8,128)(2,1)S(1)}, u32[]{:S(2)}, u32[]{:S(2)}) %all-to-all-start.2) | async-done | bytes 2097184 | tf_op jit(solution)/shard_map/all_to_all | solution.py:188
  110.0 3.8 %shard_map.75 = bf16[256,640]{1,0:T(8,128)(2,1)S(1)} custom-call(bf16[8,256,512]{2,1,0:T(8,128)(2,1)S(1)} %all-to-all-done.2.h_ref, bf16[1024,640]{1,0:T(8,128)(2,1)} %bitcast.21, bf16[1024,640]{1,0:T(8,128)(2,1)} %copy-done.6, bf16[1024,640]{1,0:T(8,128)(2,1)} %collective-permute-done.8.d2, bf16[1024,640]{1,0:T(8,128)(2,1)} %collective-permute-done.9.d3), custom_call_target="tpu_custom_call" | custom-call | flops 1342177280 | bytes 7340032 | tf_op jit(solution)/shard_map/pallas_call | solution.py:168
  113.8 38.5 %all_to_all.20 = bf16[16,16,640]{2,1,0:T(8,128)(2,1)S(1)} all-to-all(bf16[16,16,640]{2,1,0:T(8,128)(2,1)S(1)} %bitcast.9), channel_id=1, replica_groups=mesh['xh'=2,'co'=2,'z'=16,'y'=4,'xl'=2] {'z'}, dimensions={0} | all-to-all | bytes 655360 | tf_op jit(solution)/shard_map/all_to_all | solution.py:193
  152.3 0.0 copy-done
  152.3 1.0 shard_map.76
  (6 shorter events, 0.0 us)
Async XLA Ops:
  0.0 44.7 %collective-permute-start.1 = (bf16[5120,128]{1,0:T(8,128)(2,1)}, bf16[5120,128]{1,0:T(8,128)(2,1)S(1)}, u32[]{:S(2)}, u32[]{:S(2)}) collective-permute-start(bf16[5120,128]{1,0:T(8,128)(2,1)} %bitcast.12), channel_id=1, source_target_pairs={{0,257},{1,256},{256,1},{257,0},{2,259},{3,258},{258,3},{259,2},{4... | collective-permute-start | bytes 3932168 | tf_op jit(solution)/shard_map/ppermute | solution.py:201
  3.4 41.4 %collective-permute-start.2 = (bf16[1024,640]{1,0:T(8,128)(2,1)}, bf16[1024,640]{1,0:T(8,128)(2,1)S(1)}, u32[]{:S(2)}, u32[]{:S(2)}) collective-permute-start(bf16[1024,640]{1,0:T(8,128)(2,1)} %bitcast.20), channel_id=1, source_target_pairs={{0,1},{1,0},{2,3},{3,2},{4,5},{5,4},{6,7},{7,6},{8,9},{9,8},{10,11... | collective-permute-start | bytes 3932168 | tf_op jit(solution)/shard_map/ppermute | solution.py:205
  9.1 35.6 %all-to-all-start = ((bf16[16,16,640]{2,1,0:T(8,128)(2,1)}), bf16[16,16,640]{2,1,0:T(8,128)(2,1)S(1)}, u32[]{:S(2)}, u32[]{:S(2)}) async-start(bf16[16,16,640]{2,1,0:T(8,128)(2,1)} %bitcast.19), calls=%async_computation | async-start | bytes 655360 | tf_op jit(solution)/shard_map/all_to_all | solution.py:193
  24.3 36.5 %collective-permute-start = (bf16[5120,128]{1,0:T(8,128)(2,1)}, bf16[5120,128]{1,0:T(8,128)(2,1)}, u32[]{:S(2)}, u32[]{:S(2)}) collective-permute-start(bf16[5120,128]{1,0:T(8,128)(2,1)} %bitcast.15), channel_id=1, source_target_pairs={{0,257},{1,256},{256,1},{257,0},{2,259},{3,258},{258,3},{259,2},{4... | collective-permute-start | bytes 3932168 | tf_op jit(solution)/shard_map/ppermute | solution.py:201
  44.7 1.1 copy-start.1
  44.8 3.2 %copy-start.7 = (bf16[1024,640]{1,0:T(8,128)(2,1)}, bf16[1024,640]{1,0:T(8,128)(2,1)S(1)}, u32[]{:S(2)}) copy-start(bf16[1024,640]{1,0:T(8,128)(2,1)S(1)} %collective-permute-done.2) | copy-start | bytes 3932164
  47.9 30.2 %all-to-all-start.1 = ((bf16[8,264,640]{2,1,0:T(8,128)(2,1)}), bf16[8,264,640]{2,1,0:T(8,128)(2,1)S(1)}, u32[]{:S(2)}, u32[]{:S(2)}) async-start(bf16[8,264,640]{2,1,0:T(8,128)(2,1)} %broadcast_in_dim.21), calls=%async_computation.1 | async-start | bytes 5406720 | tf_op jit(solution)/shard_map/all_to_all | solution.py:188
  53.7 14.8 %collective-permute-start.3 = (bf16[5120,128]{1,0:T(8,128)(2,1)}, bf16[5120,128]{1,0:T(8,128)(2,1)S(1)}, u32[]{:S(2)}, u32[]{:S(2)}) collective-permute-start(bf16[5120,128]{1,0:T(8,128)(2,1)} %bitcast.13), channel_id=1, source_target_pairs={{0,128},{128,0},{1,129},{129,1},{2,130},{130,2},{3,131},{131,3},{4... | collective-permute-start | bytes 3932168 | tf_op jit(solution)/shard_map/ppermute | solution.py:197
  55.6 12.9 %collective-permute-start.4 = (bf16[5120,128]{1,0:T(8,128)(2,1)}, bf16[5120,128]{1,0:T(8,128)(2,1)S(1)}, u32[]{:S(2)}, u32[]{:S(2)}) collective-permute-start(bf16[5120,128]{1,0:T(8,128)(2,1)} %bitcast.16), channel_id=1, source_target_pairs={{0,128},{128,0},{1,129},{129,1},{2,130},{130,2},{3,131},{131,3},{4... | collective-permute-start | bytes 3932168 | tf_op jit(solution)/shard_map/ppermute | solution.py:197
  60.8 7.8 %collective-permute-start.6 = (bf16[5120,128]{1,0:T(8,128)(2,1)}, bf16[5120,128]{1,0:T(8,128)(2,1)S(1)}, u32[]{:S(2)}, u32[]{:S(2)}) collective-permute-start(bf16[5120,128]{1,0:T(8,128)(2,1)} %collective-permute-done.rest_5_), channel_id=1, source_target_pairs={{0,128},{128,0},{1,129},{129,1},{2,130},{130,2},{3,131},{131,3},{4... | collective-permute-start | bytes 3932168 | tf_op jit(solution)/shard_map/ppermute | solution.py:197
  62.7 8.4 %collective-permute-start.5 = (bf16[5120,128]{1,0:T(8,128)(2,1)}, bf16[5120,128]{1,0:T(8,128)(2,1)}, u32[]{:S(2)}, u32[]{:S(2)}) collective-permute-start(bf16[5120,128]{1,0:T(8,128)(2,1)} %copy-done.1), channel_id=1, source_target_pairs={{0,128},{128,0},{1,129},{129,1},{2,130},{130,2},{3,131},{131,3},{4... | collective-permute-start | bytes 3932168 | tf_op jit(solution)/shard_map/ppermute | solution.py:197
  65.1 32.9 %collective-permute-start.8 = (bf16[1024,640]{1,0:T(8,128)(2,1)}, bf16[1024,640]{1,0:T(8,128)(2,1)}, u32[]{:S(2)}, u32[]{:S(2)}) collective-permute-start(bf16[1024,640]{1,0:T(8,128)(2,1)} %copy-done.7), channel_id=1, source_target_pairs={{0,257},{1,256},{256,1},{257,0},{2,259},{3,258},{258,3},{259,2},{4... | collective-permute-start | bytes 3932168 | tf_op jit(solution)/shard_map/ppermute | solution.py:201
  68.6 1.1 copy-start.2
  68.6 1.5 copy-start.3
  70.0 1.1 copy-start.4
  84.6 5.8 %copy-start.5 = (bf16[1,1024,640]{2,1,0:T(8,128)(2,1)S(1)}, bf16[1,1024,640]{2,1,0:T(8,128)(2,1)}, u32[]{:S(2)}) copy-start(bf16[1,1024,640]{2,1,0:T(8,128)(2,1)} %param.13) | copy-start | bytes 3932164
  84.7 25.3 %all-to-all-start.2 = ((bf16[8,256,512]{2,1,0:T(8,128)(2,1)}), bf16[8,256,512]{2,1,0:T(8,128)(2,1)S(1)}, u32[]{:S(2)}, u32[]{:S(2)}) async-start(bf16[8,256,512]{2,1,0:T(8,128)(2,1)} %shard_map.74), calls=%async_computation.2 | async-start | bytes 4194304 | tf_op jit(solution)/shard_map/all_to_all | solution.py:188
  90.5 61.8 %copy-start = (s32[128,1]{0,1:T(1,128)S(1)}, s32[128,1]{0,1:T(1,128)}, u32[]{:S(2)}) copy-start(s32[128,1]{0,1:T(1,128)} %param.10) | copy-start | bytes 1540
  90.5 9.5 %collective-permute-start.7 = (bf16[1024,640]{1,0:T(8,128)(2,1)S(1)}, bf16[1024,640]{1,0:T(8,128)(2,1)S(1)}, u32[]{:S(2)}, u32[]{:S(2)}) collective-permute-start(bf16[1024,640]{1,0:T(8,128)(2,1)S(1)} %bitcast.22), channel_id=1, source_target_pairs={{0,128},{128,0},{1,129},{129,1},{2,130},{130,2},{3,131},{131,3},{4... | collective-permute-start | bytes 3932168 | tf_op jit(solution)/shard_map/ppermute | solution.py:197
  98.0 5.3 %collective-permute-start.9 = (bf16[1024,640]{1,0:T(8,128)(2,1)}, bf16[1024,640]{1,0:T(8,128)(2,1)}, u32[]{:S(2)}, u32[]{:S(2)}) collective-permute-start(bf16[1024,640]{1,0:T(8,128)(2,1)} %collective-permute-done.8.d2), channel_id=1, source_target_pairs={{0,128},{128,0},{1,129},{129,1},{2,130},{130,2},{3,131},{131,3},{4... | collective-permute-start | bytes 3932168 | tf_op jit(solution)/shard_map/ppermute | solution.py:197
  100.0 1.1 copy-start.6
